TPU v7x, 128 devices: a whole 4x4x4 slice. The times are simulated.
128 devices in a mesh: dp: 16 (over z_hi, y, core), tensor: 8 (over x, z_lo).
Axes of the slice: x: 4, y: 4, z: 4 (z_hi: 2, z_lo: 2; z = z_hi * 2 + z_lo), core: 2. Of those that a mesh axis runs over, the one named last changes fastest.
Arguments:
- x_states: bfloat16 [48, 192, 8192], P('dp'), may hold values from -6 to 6
- mask_bits: int32 [48, 192], P('dp'), may hold values 0 or 1
- prompt_len: int32 [48], P('dp'), may hold values from 24 to 95
- weight: bfloat16 [8192, 8192], P(None, 'tensor'), may hold values from -0.0625 to 0.0625
- norm_gain: float32 [8192], replicated, may hold values from 0.1 to 1.9
- mask_embed: bfloat16 [8192], replicated, may hold values from -6 to 6
- grads: float32 [16, 2, 64, 8192], P('dp', None, None, 'tensor'), may hold values from -6 to 6
- factors: float32 [2, 64, 8192], P(None, None, 'tensor'), may hold values from -0.15625 to 0.15625
- first_moment: float32 [2, 64, 8192], P(None, None, 'tensor'), may hold values from -6 to 6
- second_moment: float32 [2, 64, 8192], P(None, None, 'tensor'), may hold values from 0.25 to 4
Outputs:
- denoised: bfloat16 [48, 192, 8192], P('dp', None, 'tensor')
- new_first: float32 [2, 64, 8192], P(None, 'dp', 'tensor')
- new_second: float32 [2, 64, 8192], P(None, 'dp', 'tensor')
All inputs are finite; a program needn't handle non-finite values. No bound on the sum of `mask_bits` on one device may be relied on, other than what follows from the above.
Results may differ from a plain program's by a relative error of at most 0.0095.
Values may be sent and summed in bfloat16 or wider, within the bound.
No kernel may reach another device: no remote copies, remote signals or barrier semaphores. Data moves between devices by JAX's collectives and lax.ppermute only.
A program may use at most 192 MiB of HBM per device.

v0:
```python
import jax
import jax.numpy as jnp
from jax import lax
from jax.sharding import PartitionSpec as P

beta_one = 0.9
beta_two = 0.999
learn_rate = 0.03
adam_count = 100
epsilon = 1e-08
adapter_scale = 2.0
norm_epsilon = 1e-05


def adam_update(summed_grad, first_moment, second_moment, param_rows):
    new_first = beta_one * first_moment + (1.0 - beta_one) * summed_grad
    new_second = beta_two * second_moment + (1.0 - beta_two) * summed_grad * summed_grad
    step_size = learn_rate / (1.0 - beta_one**adam_count)
    divisor = jnp.sqrt(new_second / (1.0 - beta_two**adam_count)) + epsilon
    return (new_first, new_second, param_rows - step_size * new_first / divisor)


def prepare(x_states, mask_bits, prompt_len, norm_gain, mask_embed):
    length = x_states.shape[1]
    position = jnp.arange(length, dtype=jnp.int32)
    response = position[None, :] >= prompt_len[:, None]
    masked = jnp.logical_and(response, mask_bits == 1)
    hidden = jnp.where(masked[:, :, None], mask_embed[None, None, :], x_states)
    widened = hidden.astype(jnp.float32)
    norm_scale = lax.rsqrt(jnp.mean(widened * widened, axis=-1, keepdims=True) + norm_epsilon)
    normed = (widened * norm_gain).astype(jnp.bfloat16)
    return (response, widened, norm_scale, normed.reshape(-1, x_states.shape[2]))


def finish(x_states, response, widened, norm_scale, projected_states, col_start):
    seq_count = x_states.shape[0]
    length = x_states.shape[1]
    col_width = projected_states.shape[1]
    projected_states = projected_states.reshape(seq_count, length, col_width) * norm_scale
    own_part = lax.dynamic_slice_in_dim(widened, col_start, col_width, 2)
    kept = lax.dynamic_slice_in_dim(x_states, col_start, col_width, 2).astype(jnp.float32)
    return jnp.where(response[:, :, None], own_part + projected_states, kept).astype(jnp.bfloat16)


def local(
    x_states,
    mask_bits,
    prompt_len,
    weight,
    norm_gain,
    mask_embed,
    grads,
    factors,
    first_moment,
    second_moment,
):
    local_grad = grads[0]
    row_share = factors.shape[1] // lax.axis_size("dp")
    start_row = lax.axis_index("dp") * row_share
    summed = lax.psum(local_grad.astype(jnp.bfloat16), "dp").astype(jnp.float32)
    full_first, full_second, updated = adam_update(summed, first_moment, second_moment, factors)
    new_first = lax.dynamic_slice_in_dim(full_first, start_row, row_share, 1)
    new_second = lax.dynamic_slice_in_dim(full_second, start_row, row_share, 1)
    transferred_factors = updated.astype(jnp.bfloat16)
    adapter_down_matrix = transferred_factors[0]
    adapter_up_transposed = transferred_factors[1]
    response, widened, norm_scale, normed = prepare(
        x_states, mask_bits, prompt_len, norm_gain, mask_embed
    )
    col_width = weight.shape[1]
    col_start = lax.axis_index("tensor") * col_width
    rank_weight_delta = lax.dot_general(
        lax.all_gather(adapter_up_transposed, "tensor", axis=1, tiled=True),
        adapter_down_matrix,
        (((0,), (0,)), ((), ())),
        preferred_element_type=jnp.float32,
    )
    combined_weight = weight.astype(jnp.float32) + adapter_scale * rank_weight_delta
    projected_states = jnp.dot(
        normed, combined_weight, precision=lax.Precision.HIGHEST, preferred_element_type=jnp.float32
    )
    denoised = finish(x_states, response, widened, norm_scale, projected_states, col_start)
    return (denoised, new_first, new_second)


def solution(mesh):
    placed = (
        P("dp", None, None),
        P("dp", None),
        P("dp"),
        P(None, "tensor"),
        P(),
        P(),
        P("dp", None, None, "tensor"),
        P(None, None, "tensor"),
        P(None, None, "tensor"),
        P(None, None, "tensor"),
    )
    return jax.shard_map(
        local,
        mesh=mesh,
        in_specs=placed,
        out_specs=(P("dp", None, "tensor"), P(None, "dp", "tensor"), P(None, "dp", "tensor")),
        check_vma=False,
    )
```

profile of v0, /device:TPU:0, one launch (start us, length us, event | category | flops | bytes accessed | tf_op | source)
XLA Modules:
  0.0 257.3 jit_solution(17426625575570287426)
XLA Ops:
  7.2 0.0 copy-start.3
  7.2 0.0 copy-start.2
  7.2 0.0 copy-start.1
  7.2 0.0 copy-start
  7.2 0.0 all-reduce.2.cloned.1.call-start
  7.3 1.9 convert_bitcast_fusion
  9.1 0.0 all-reduce.2.cloned.1.call-update
  9.2 0.0 all-gather.3.cloned.1.call-start
  9.2 0.8 iota_compare_fusion
  10.0 6.3 %multiply_reduce_fusion = f32[3,192]{1,0:T(4,128)S(1)} fusion(bf16[3,192,8192]{2,1,0:T(8,128)(2,1)} %param.10, pred[3,192]{1,0:T(4,128)(4,1)S(1)} %get-tuple-element.7, bf16[8192]{0:T(1024)(128)(2,1)} %param.15), kind=kLoop, calls=%fused_computation.5 | loop fusion | flops 18873792 | bytes 9456448 | tf_op jit(solution)/shard_map/reduce_sum | solution.py:30
  16.4 134.8 %all-reduce.2.cloned.1.call-done = bf16[2,64,1024]{2,1,0:T(8,128)(2,1)} async-done(((bf16[2,64,1024]{2,1,0:T(8,128)(2,1)}), bf16[2,64,1024]{2,1,0:T(8,128)(2,1)}) %all-reduce.2.cloned.1.call-update) | async-done | bytes 262160 | tf_op jit(solution)/shard_map/psum | solution.py:60
  151.2 0.0 copy-done.2
  151.2 0.0 copy-done.1
  151.2 0.0 copy-done
  151.2 1.3 subtract_convert_fusion
  152.5 0.7 slice.8
  153.2 0.0 all-gather.3.cloned.1.call-update
  153.2 0.0 copy-done.3
  153.2 11.4 %fusion.8 = f32[3,192,8192]{2,1,0:T(8,128)} fusion(bf16[3,192,8192]{2,1,0:T(8,128)(2,1)} %param.10, pred[3,192]{1,0:T(4,128)(4,1)S(1)} %get-tuple-element.7, bf16[8192]{0:T(1024)(128)(2,1)S(1)} %copy-done.3), kind=kLoop, calls=%fused_computation.11 | loop fusion | flops 9437184 | bytes 28328512 | tf_op jit(solution)/shard_map/convert_element_type | solution.py:29
  164.6 0.6 constant_dynamic-slice_fusion
  165.2 0.0 copy-start.4
  165.2 28.4 %all-gather.3.cloned.1.call-done = bf16[1,64,8192]{2,1,0:T(8,128)(2,1)} async-done(((bf16[1,64,1024]{2,1,0:T(8,128)(2,1)}), bf16[1,64,8192]{2,1,0:T(8,128)(2,1)}) %all-gather.3.cloned.1.call-update) | async-done | bytes 1048592 | tf_op jit(solution)/shard_map/all_gather | solution.py:73
  193.7 14.4 %fusion.12 = f32[8192,1024]{1,0:T(8,128)} fusion(bf16[1,64,8192]{2,1,0:T(8,128)(2,1)} %all-gather.3.cloned.1.call-done, bf16[2,64,1024]{2,1,0:T(8,128)(2,1)S(1)} %get-tuple-element.3), kind=kOutput, calls=%fused_computation.14 | convolution fusion | flops 1073741824 | bytes 34734080 | tf_op jit(solution)/shard_map/dot_general | solution.py:72
  208.0 0.0 copy-done.4
  208.0 42.5 %select_convert_fusion = bf16[3,192,1024]{2,1,0:T(8,128)(2,1)} fusion(f32[3,192,8192]{2,1,0:T(8,128)} %fusion.8, s32[]{:T(128)S(6)} %select_n.17, f32[8192,1024]{1,0:T(8,128)} %fusion.12, bf16[8192,1024]{1,0:T(8,128)(2,1)} %param.13, f32[8192]{0:T(1024)S(1)} %copy-done.4, bf16[3,192,8192]{2,1,0:T(8,128)(2,1)} %param.10, ...), kind=kOutput, calls=%fused_computation.13 | convolution fusion | flops 58029047808 | bytes 64540036 | tf_op jit(solution)/shard_map/dot_general | solution.py:79
  (1 shorter events, 0.0 us)
Async XLA Ops:
  7.2 146.0 %copy-start.3 = (bf16[8192]{0:T(1024)(128)(2,1)S(1)}, bf16[8192]{0:T(1024)(128)(2,1)}, u32[]{:S(2)}) copy-start(bf16[8192]{0:T(1024)(128)(2,1)} %param.15) | copy-start | bytes 49156
  7.2 144.0 %copy-start.2 = (f32[2,64,1024]{2,1,0:T(8,128)S(1)}, f32[2,64,1024]{2,1,0:T(8,128)}, u32[]{:S(2)}) copy-start(f32[2,64,1024]{2,1,0:T(8,128)} %param.19) | copy-start | bytes 1572868
  7.2 144.0 %copy-start.1 = (f32[2,64,1024]{2,1,0:T(8,128)S(1)}, f32[2,64,1024]{2,1,0:T(8,128)}, u32[]{:S(2)}) copy-start(f32[2,64,1024]{2,1,0:T(8,128)} %param.18) | copy-start | bytes 1572868
  7.2 144.0 %copy-start = (f32[2,64,1024]{2,1,0:T(8,128)S(1)}, f32[2,64,1024]{2,1,0:T(8,128)}, u32[]{:S(2)}) copy-start(f32[2,64,1024]{2,1,0:T(8,128)} %param.17) | copy-start | bytes 1572868
  7.2 144.0 %all-reduce.2.cloned.1.call-start = ((), (), s32[]{:S(2)}) async-start(), calls=%async_computation | async-start | bytes 524288 | tf_op jit(solution)/shard_map/psum | solution.py:60
  9.2 184.5 %all-gather.3.cloned.1.call-start = ((), (), s32[]{:S(2)}) async-start(), calls=%async_computation.1 | async-start | bytes 1179648 | tf_op jit(solution)/shard_map/all_gather | solution.py:73
  165.2 42.8 %copy-start.4 = (f32[8192]{0:T(1024)S(1)}, f32[8192]{0:T(1024)}, u32[]{:S(2)}) copy-start(f32[8192]{0:T(1024)} %param.14) | copy-start | bytes 98308
Sparse Core Ops, SparseCore 0:
  11.1 140.0 all-reduce.1
  153.5 40.1 all-gather.2
where the time goes:
time: 258 us; the launch traced here: 257 us
  waiting for transfers between devices  163 us (63%)
  matrix products  56.8 us (22%)
  other arithmetic  21.7 us (8%)
  between operations  14.1 us (5%)
    psum x1, waiting for transfers between devices, local(): summed = lax.psum(local_grad.astype(jnp.bfloat16), 'dp').astype(jnp.float32)  135 us
    dot_general x1, matrix products, local(): jnp.dot(normed, combined_weight, precision=lax.Precision.HIGHEST, preferr...  42.5 us
    all_gather x1, waiting for transfers between devices, local(): lax.all_gather(adapter_up_transposed, 'tensor', axis=1, tiled=True)  28.4 us
    dot_general x1, matrix products, local(): lax.dot_general(lax.all_gather(adapter_up_transposed, 'tensor', axis=1, t...  14.4 us
    convert_element_type x1, other arithmetic, prepare(): widened = hidden.astype(jnp.float32)  11.4 us
    reduce_sum x1, other arithmetic, prepare(): jnp.mean(widened * widened, axis=-1, keepdims=True) + norm_epsilon  6.34 us
  transfers between devices with their start and end apart: 2, of which 2 were waited for; matrix products, arithmetic and copies ran while one was open for 7% of the time, Pallas kernels for 0%

commit v1 on v0

v1 whole, which is shorter than its diff:
```python
import functools
import itertools

import jax
import jax.numpy as jnp
from jax import lax
from jax.experimental import pallas as pl
from jax.experimental.pallas import tpu as pltpu
from jax.sharding import Mesh, PartitionSpec as P

beta_one = 0.9
beta_two = 0.999
learn_rate = 0.03
adam_count = 100
epsilon = 1e-08
adapter_scale = 2.0
norm_epsilon = 1e-05

SIZES = {"zh": 2, "y": 4, "c": 2, "x": 4, "zl": 2}
DP = ("zh", "y", "c")
TENSOR = ("x", "zl")
KB = 512
MIB = 1 << 20


def f32(v):
    return v.astype(jnp.float32)


def bf16(v):
    return v.astype(jnp.bfloat16)


def exchange(v, axes, key):
    ids = list(itertools.product(*[range(SIZES[a]) for a in axes]))
    index = {t: i for i, t in enumerate(ids)}
    pairs = [(index[t], index[tuple(a ^ k for a, k in zip(t, key))]) for t in ids]
    return lax.ppermute(v, tuple(axes), pairs)


def adam_update(summed_grad, first_moment, second_moment):
    new_first = beta_one * first_moment + (1.0 - beta_one) * summed_grad
    new_second = beta_two * second_moment + (1.0 - beta_two) * summed_grad * summed_grad
    return new_first, new_second


def factor_update(new_first, new_second, param_rows):
    step_size = learn_rate / (1.0 - beta_one**adam_count)
    divisor = jnp.sqrt(new_second / (1.0 - beta_two**adam_count)) + epsilon
    return param_rows - step_size * new_first / divisor


def main_kernel(first, x_ref, mask_ref, gain_ref, embed_ref, w_ref, *rest):
    if first:
        _, acc_ref, sq_ref = rest
    else:
        _, acc_in, sq_in, acc_ref, sq_ref = rest
    step = pl.program_id(0)
    rows = acc_ref.shape[0]
    masked = mask_ref[...] > 0.0
    states = x_ref[...].reshape(rows, KB).astype(jnp.float32)
    hidden = jnp.where(masked, embed_ref[...].astype(jnp.float32), states)
    normed = (hidden * gain_ref[...]).astype(jnp.bfloat16)
    squares = hidden * hidden
    part = squares[:, 0:128]
    for j in range(1, KB // 128):
        part = part + squares[:, j * 128 : (j + 1) * 128]
    product = jnp.dot(normed, w_ref[...], preferred_element_type=jnp.float32)

    if first:

        @pl.when(step == 0)
        def _():
            acc_ref[...] = product
            sq_ref[...] = part

        @pl.when(step > 0)
        def _():
            acc_ref[...] += product
            sq_ref[...] += part
    else:

        @pl.when(step == 0)
        def _():
            acc_ref[...] = acc_in[...] + product
            sq_ref[...] = sq_in[...] + part

        @pl.when(step > 0)
        def _():
            acc_ref[...] += product
            sq_ref[...] += part


def main_chunk(x, mask, gain, embed, w, token, state, start, stop):
    seqs, length, width = x.shape
    rows = seqs * length
    cols = w.shape[1]
    first = state is None
    k0 = start // KB
    steps = (stop - start) // KB
    whole = pl.BlockSpec(memory_space=pltpu.VMEM)
    in_specs = [
        pl.BlockSpec((seqs, length, KB), lambda i: (0, 0, k0 + i)),
        whole,
        pl.BlockSpec((1, KB), lambda i: (0, k0 + i)),
        pl.BlockSpec((1, KB), lambda i: (0, k0 + i)),
        pl.BlockSpec((KB, cols), lambda i: (k0 + i, 0)),
        pl.BlockSpec(memory_space=pl.ANY),
    ]
    args = [x, mask, gain, embed, w, token]
    aliases = {}
    if not first:
        in_specs += [whole, whole]
        args += list(state)
        aliases = {6: 0, 7: 1}
    return pl.pallas_call(
        functools.partial(main_kernel, first),
        grid=(steps,),
        in_specs=in_specs,
        out_specs=[whole, whole],
        out_shape=[
            jax.ShapeDtypeStruct((rows, cols), jnp.float32),
            jax.ShapeDtypeStruct((rows, 128), jnp.float32),
        ],
        input_output_aliases=aliases,
        compiler_params=pltpu.CompilerParams(vmem_limit_bytes=28 * MIB),
        cost_estimate=pl.CostEstimate(
            flops=2 * rows * (stop - start) * cols,
            bytes_accessed=2 * (stop - start) * (rows + cols),
            transcendentals=0,
        ),
        name="main_chunk",
    )(*args)


def low_rank_kernel(own_ref, other_ref, bown_ref, bother_ref, out_ref):
    half = own_ref.shape[0] // 2
    dims = (((1,), (1,)), ((), ()))
    prod = lax.dot_general(own_ref[...], bown_ref[...], dims, preferred_element_type=jnp.float32)
    prod += lax.dot_general(other_ref[...], bother_ref[...], dims, preferred_element_type=jnp.float32)
    out_ref[...] = jnp.concatenate([prod[:half], prod[half:]], axis=1).astype(jnp.bfloat16)


def low_rank(own, other, b_own, b_other):
    rows = own.shape[0]
    rank = b_own.shape[0]
    return pl.pallas_call(
        low_rank_kernel,
        out_shape=jax.ShapeDtypeStruct((rows // 2, 2 * rank), jnp.bfloat16),
        compiler_params=pltpu.CompilerParams(vmem_limit_bytes=8 * MIB),
        name="low_rank",
    )(own, other, b_own, b_other)


def final_kernel(
    mine_ref, r1_ref, r2_ref, r3_ref, a_ref, acc_ref, sq_ref, xs_ref, mask_ref, resp_ref, embed_ref, out_ref
):
    rows = acc_ref.shape[0]
    half = rows // 2
    rank = a_ref.shape[0]
    total = mine_ref[...].astype(jnp.float32) + r1_ref[...].astype(jnp.float32)
    total += r2_ref[...].astype(jnp.float32) + r3_ref[...].astype(jnp.float32)
    total = total.astype(jnp.bfloat16)
    mean = jnp.sum(sq_ref[...], axis=1, keepdims=True) * (1.0 / 8192.0)
    scale = lax.rsqrt(mean + norm_epsilon)
    for piece in range(2):
        low = total[:, piece * rank : (piece + 1) * rank]
        adapter = jnp.dot(low, a_ref[...], preferred_element_type=jnp.float32)
        at = slice(piece * half, (piece + 1) * half)
        states = xs_ref[at, :].astype(jnp.float32)
        hidden = jnp.where(mask_ref[at, :] > 0.0, embed_ref[...].astype(jnp.float32), states)
        projected = (acc_ref[at, :] + adapter_scale * adapter) * scale[at]
        value = jnp.where(resp_ref[at, :] > 0.0, hidden + projected, states).astype(jnp.bfloat16)
        out_ref[at, :] = value


def final(mine, received, a, acc, sq, xs, mask, resp, embed):
    rows, cols = acc.shape
    return pl.pallas_call(
        final_kernel,
        out_shape=jax.ShapeDtypeStruct((rows, cols), jnp.bfloat16),
        compiler_params=pltpu.CompilerParams(vmem_limit_bytes=20 * MIB),
        name="final",
    )(mine, *received, a, acc, sq, xs, mask, resp, embed)


def local(x, mask_bits, prompt_len, weight, norm_gain, mask_embed, grads, factors, first_moment, second_moment):
    seqs, length, width = x.shape
    rows = seqs * length
    cols = weight.shape[1]
    half = cols // 2
    core = lax.axis_index("c")
    col_start = lax.axis_index(TENSOR) * cols
    rank = factors.shape[1]
    share = rank // 16

    def own_half(v):
        return lax.dynamic_slice_in_dim(v, core * half, half, v.ndim - 1)

    def other_half(v):
        return lax.dynamic_slice_in_dim(v, (1 - core) * half, half, v.ndim - 1)

    grad = grads[0]
    from_core = exchange(bf16(other_half(grad)), "c", (1,))
    total = own_half(grad) + f32(from_core)
    sent = bf16(total)
    from_y = [exchange(sent, "y", (k,)) for k in (2, 3, 1)]
    total = total + f32(from_y[0]) + f32(from_y[1]) + f32(from_y[2])
    from_z = exchange(bf16(total), ("zh",), (1,))
    total = total + f32(from_z)

    new_first, new_second = adam_update(total, own_half(first_moment), own_half(second_moment))
    shipped = bf16(factor_update(new_first, new_second, own_half(factors)))
    b_own = shipped[1]
    b_other = exchange(b_own, "c", (1,))
    a_own = shipped[0]
    a_other = exchange(a_own, "c", (1,))

    my_row = lax.axis_index(DP) * share
    pair_row = (lax.axis_index(DP) + 1 - 2 * core) * share
    rows_out = lax.dynamic_slice_in_dim(total, pair_row, share, 1)
    rows_in = exchange(rows_out, "c", (1,))
    rows_mine = lax.dynamic_slice_in_dim(total, my_row, share, 1)

    def ordered(mine, others):
        return jnp.where(
            core == 0, jnp.concatenate([mine, others], -1), jnp.concatenate([others, mine], -1)
        )

    row_total = ordered(rows_mine, rows_in)
    out_first, out_second = adam_update(
        row_total,
        lax.dynamic_slice_in_dim(first_moment, my_row, share, 1),
        lax.dynamic_slice_in_dim(second_moment, my_row, share, 1),
    )

    position = jnp.arange(length, dtype=jnp.int32)
    response = position[None, :] >= prompt_len[:, None]
    masked = jnp.logical_and(response, mask_bits == 1)
    mask_col = f32(masked).reshape(rows, 1)
    resp_col = f32(response).reshape(rows, 1)
    xs = lax.dynamic_slice_in_dim(x, col_start, cols, 2).reshape(rows, cols)
    embed_cols = lax.dynamic_slice_in_dim(mask_embed, col_start, cols, 0)
    gain_cols = lax.dynamic_slice_in_dim(norm_gain, col_start, cols, 0)
    normed_cols = bf16(f32(jnp.where(masked.reshape(rows, 1), embed_cols[None, :], xs)) * gain_cols[None, :])
    gain = norm_gain.reshape(1, width)
    embed = mask_embed.reshape(1, width)

    state = main_chunk(x, mask_col, gain, embed, weight, from_core, None, 0, width // 2)
    state = main_chunk(x, mask_col, gain, embed, weight, from_y[0], state, width // 2, 3 * width // 4)

    low = low_rank(own_half(normed_cols), other_half(normed_cols), b_own, b_other)
    from_zl = exchange(low, ("zl",), (1,))
    state = main_chunk(x, mask_col, gain, embed, weight, b_other, state, 3 * width // 4, 7 * width // 8)
    low = bf16(f32(low) + f32(from_zl))
    from_x = [exchange(low, ("x",), (k,)) for k in (2, 3, 1)]
    state = main_chunk(x, mask_col, gain, embed, weight, from_zl, state, 7 * width // 8, width)
    a_full = ordered(a_own, a_other)
    out = final(low, from_x, a_full, *state, xs, mask_col, resp_col, embed_cols.reshape(1, cols))
    return out.reshape(seqs, length, cols), out_first, out_second


def solution(mesh):
    split = Mesh(mesh.devices.reshape(2, 4, 2, 4, 2), ("zh", "y", "c", "x", "zl"))
    placed = (
        P(DP, None, None),
        P(DP, None),
        P(DP),
        P(None, TENSOR),
        P(),
        P(),
        P(DP, None, None, TENSOR),
        P(None, None, TENSOR),
        P(None, None, TENSOR),
        P(None, None, TENSOR),
    )
    return jax.shard_map(
        local,
        mesh=split,
        in_specs=placed,
        out_specs=(P(DP, None, TENSOR), P(None, DP, TENSOR), P(None, DP, TENSOR)),
        check_vma=False,
    )
```

time: 258 us -> 56.2 us (0.22)
  waiting for transfers between devices: 163 us -> 1.09 us
  matrix products: 56.8 us -> 0 us
  Pallas kernels: 0 us -> 27.8 us
  other arithmetic: 21.7 us -> 2.16 us
  starting transfers between devices: 0.08 us -> 14.5 us
  between operations: 14.1 us -> 0.93 us
  local copies, waits for them, and re-layouts: 1.33 us -> 8.67 us
    psum x1 -> x0, waiting for transfers between devices: 135 us -> none  [local(): summed = lax.psum(local_grad.astype(jnp.bfloat16), 'dp').astype(jnp.float32)]
    dot_general x2 -> x0, matrix products: 56.8 us -> none  [the longest x1 42.5 us: local(): jnp.dot(normed, combined_weight, precision=lax.Precision.HIGHEST, preferr...]
    all_gather x1 -> x0, waiting for transfers between devices: 28.4 us -> none  [local(): lax.all_gather(adapter_up_transposed, 'tensor', axis=1, tiled=True)]
    pallas_call x0 -> x6, Pallas kernels: none -> 27.8 us  [the longest x4 25.4 us: main_chunk(): pl.pallas_call(functools.partial(main_kernel, first), grid=(steps,), in_s...]
    ppermute x0 -> x12, starting transfers between devices: none -> 14.5 us  [exchange(): return lax.ppermute(v, tuple(axes), pairs)]
    convert_element_type x3 -> x5, other arithmetic: 14.6 us -> 0.7 us  [bf16(): return v.astype(jnp.bfloat16)]
    reduce_sum x1 -> x0, other arithmetic: 6.34 us -> none  [prepare(): jnp.mean(widened * widened, axis=-1, keepdims=True) + norm_epsilon]
    unnamed x10 -> x12, local copies, waits for them, and re-layouts: 0.02 us -> 4.22 us
  transfers between devices with their start and end apart: 2 -> 12, of which waited for: 2 -> 2; matrix products, arithmetic and copies ran while one was open for 7% -> 10% of each run, Pallas kernels for 0% -> 47%
where the time goes in v1:
time: 56.2 us; the launch traced here: 55.2 us
  Pallas kernels  27.8 us (49%)
  starting transfers between devices  14.5 us (26%)
  local copies, waits for them, and re-layouts  8.67 us (15%)
  other arithmetic  2.16 us (4%)
  waiting for transfers between devices  1.09 us (2%)
  between operations  0.93 us (2%)
    pallas_call x4, Pallas kernels, main_chunk(): pl.pallas_call(functools.partial(main_kernel, first), grid=(steps,), in_s...  25.4 us
    ppermute x12, starting transfers between devices, exchange(): return lax.ppermute(v, tuple(axes), pairs)  14.5 us
    unnamed x12, local copies, waits for them, and re-layouts  4.22 us
    pallas_call x1, Pallas kernels, final(): pl.pallas_call(final_kernel, out_shape=jax.ShapeDtypeStruct((rows, cols),...  1.93 us
    dynamic_slice x1, local copies, waits for them, and re-layouts, local(): xs = lax.dynamic_slice_in_dim(x, col_start, cols, 2).reshape(rows, cols)  1.35 us
  transfers between devices with their start and end apart: 12, of which 2 were waited for; matrix products, arithmetic and copies ran while one was open for 10% of the time, Pallas kernels for 47%

profile of v1, /device:TPU:0, one launch (start us, length us, event | category | flops | bytes accessed | tf_op | source)
XLA Modules:
  0.0 55.2 jit_solution(14205727948470243562)
XLA Ops:
  0.6 1.0 %fusion.8 = bf16[2,64,512]{2,1,0:T(8,128)(2,1)S(1)} fusion(f32[1,2,64,1024]{3,2,1,0:T(8,128)} %param.16, s32[]{:T(128)S(6)} %select_n.47), kind=kLoop, calls=%fused_computation.15 | loop fusion | bytes 262148 | tf_op jit(solution)/shard_map/convert_element_type | solution.py:31
  1.6 0.1 collective-permute-start
  1.7 0.8 %fusion.12 = (f32[3,192]{1,0:T(4,128)S(1)}, pred[3,192]{1,0:T(4,128)(4,1)S(1)}, f32[3,192]{1,0:T(4,128)S(1)}) fusion(s32[3,192]{1,0:T(4,128)} %param.11, s32[3]{0:T(128)} %param.12), kind=kLoop, calls=%fused_computation.31 | loop fusion | flops 2880 | bytes 7500 | tf_op jit(solution)/shard_map/reshape | solution.py:240
  2.5 0.2 reshape.69.mask_ref
  2.7 0.7 %reshape.64.embed_ref = bf16[1,8192]{1,0:T(2,128)(2,1)S(1)} reshape(bf16[8192]{0:T(1024)(128)(2,1)} %param.15) | data formatting | bytes 32768 | tf_op jit(solution)/shard_map/reshape | solution.py:247
  3.5 0.7 %dynamic_slice.44 = bf16[1024]{0:T(1024)(128)(2,1)S(1)} dynamic-slice(bf16[8192]{0:T(1024)(128)(2,1)} %param.15, s32[]{:T(128)} %select_n.44), dynamic_slice_sizes={1024} | dynamic-slice | bytes 4100 | tf_op jit(solution)/shard_map/dynamic_slice | solution.py:243
  4.2 1.4 %constant_dynamic-slice_fusion.4 = bf16[3,192,1024]{2,1,0:T(8,128)(2,1)S(1)} fusion(bf16[3,192,8192]{2,1,0:T(8,128)(2,1)} %x_ref.7, s32[]{:T(128)} %select_n.44), kind=kLoop, calls=%fused_computation.30 | loop fusion | bytes 2359300 | tf_op jit(solution)/shard_map/dynamic_slice | solution.py:242
  5.5 0.1 broadcast_in_dim.24
  5.6 0.2 reshape.70.resp_ref
  5.9 0.3 multiply_convert_fusion
  6.2 0.1 constant_dynamic-slice_fusion.2
  6.4 0.5 copy-done.2
  6.9 3.4 %collective-permute-start.1 = (bf16[2,64,512]{2,1,0:T(8,128)(2,1)S(1)}, bf16[2,64,512]{2,1,0:T(8,128)(2,1)S(1)}, u32[]{:S(2)}, u32[]{:S(2)}) collective-permute-start(bf16[2,64,512]{2,1,0:T(8,128)(2,1)S(1)} %fusion.7), channel_id=1, source_target_pairs={{0,32},{16,48},{32,0},{48,16},{1,33},{17,49},{33,1},{49,17},{2,34}... | collective-permute-start | bytes 393224 | tf_op jit(solution)/shard_map/ppermute | solution.py:38
  10.3 1.1 %collective-permute-start.2 = (bf16[2,64,512]{2,1,0:T(8,128)(2,1)S(1)}, bf16[2,64,512]{2,1,0:T(8,128)(2,1)S(1)}, u32[]{:S(2)}, u32[]{:S(2)}) collective-permute-start(bf16[2,64,512]{2,1,0:T(8,128)(2,1)S(1)} %fusion.7), channel_id=1, source_target_pairs={{0,48},{16,32},{32,16},{48,0},{1,49},{17,33},{33,17},{49,1},{2,50}... | collective-permute-start | bytes 393224 | tf_op jit(solution)/shard_map/ppermute | solution.py:38
  11.4 3.7 %copy-done = bf16[3,192,8192]{2,1,0:T(8,128)(2,1)S(1)} copy-done((bf16[3,192,8192]{2,1,0:T(8,128)(2,1)S(1)}, bf16[3,192,8192]{2,1,0:T(8,128)(2,1)}, u32[]{:S(2)}) %copy-start) | copy-done | bytes 9437208
  15.0 11.3 %main_chunk.4 = (f32[576,1024]{1,0:T(8,128)S(1)}, f32[576,128]{1,0:T(8,128)S(1)}) custom-call(bf16[3,192,8192]{2,1,0:T(8,128)(2,1)S(1)} %copy-done, f32[576,1]{1,0:T(8,128)S(1)} %reshape.69.mask_ref, f32[1,8192]{1,0:T(1,128)S(1)} %bitcast.18, bf16[1,8192]{1,0:T(2,128)(2,1)S(1)} %reshape.64.embed_ref, bf16[8192,1024]{1,0:T(8,128)(2,1)} %w_ref.7, ...), custom_call_target="tpu_custom_call" | custom-call | flops 4831838208 | bytes 13107200 | tf_op jit(solution)/shard_map/main_chunk/pallas_call | solution.py:116
  26.4 0.1 fusion.14
  26.5 4.0 %collective-permute-start.4 = (bf16[2,64,512]{2,1,0:T(8,128)(2,1)S(1)}, bf16[2,64,512]{2,1,0:T(8,128)(2,1)S(1)}, u32[]{:S(2)}, u32[]{:S(2)}) collective-permute-start(bf16[2,64,512]{2,1,0:T(8,128)(2,1)S(1)} %get-tuple-element.23), channel_id=1, source_target_pairs={{0,64},{64,0},{1,65},{65,1},{2,66},{66,2},{3,67},{67,3},{4,68},{68... | collective-permute-start | bytes 393224 | tf_op jit(solution)/shard_map/ppermute | solution.py:38
  30.4 6.5 %main_chunk.5 = (f32[576,1024]{1,0:T(8,128)S(1)}, f32[576,128]{1,0:T(8,128)S(1)}) custom-call(bf16[3,192,8192]{2,1,0:T(8,128)(2,1)S(1)} %copy-done, f32[576,1]{1,0:T(8,128)S(1)} %reshape.69.mask_ref, f32[1,8192]{1,0:T(1,128)S(1)} %bitcast.19, bf16[1,8192]{1,0:T(2,128)(2,1)S(1)} %reshape.64.embed_ref, ...), custom_call_target="tpu_custom_call", output_to_operand_aliasing={{0}: (6, {}), {1}: (7, {})} | custom-call | flops 2415919104 | bytes 6553600 | tf_op jit(solution)/shard_map/main_chunk/pallas_call | solution.py:116
  36.9 0.2 fusion.6
  37.3 0.6 %collective-permute-start.5 = (bf16[64,512]{1,0:T(8,128)(2,1)S(1)}, bf16[64,512]{1,0:T(8,128)(2,1)S(1)}, u32[]{:S(2)}, u32[]{:S(2)}) collective-permute-start(bf16[64,512]{1,0:T(8,128)(2,1)S(1)} %get-tuple-element.30.bown_ref), channel_id=1, source_target_pairs={{0,8},{8,0},{1,9},{9,1},{2,10},{10,2},{3,11},{11,3},{4,12},{12,4},... | collective-permute-start | bytes 196616 | tf_op jit(solution)/shard_map/ppermute | solution.py:38
  37.9 0.1 collective-permute-start.10
  38.0 0.5 collective-permute-done.11
  38.4 0.7 %fusion.9 = (f32[2,4,1024]{2,1,0:T(4,128)}, f32[2,4,1024]{2,1,0:T(4,128)}) fusion(f32[2,64,1024]{2,1,0:T(8,128)S(1)} %copy-done.3, s32[]{:T(128)S(6)} %select_n.50, f32[2,4,512]{2,1,0:T(4,128)S(1)} %get-tuple-element.28, f32[2,4,512]{2,1,0:T(4,128)S(1)} %collective-permute-done.11, pred[]{:T(512)S(6)} %eq.12, f32[2,64,1024]{2,1,0:T(8,128)S(1)} %copy-done.4), kind=kLoop, calls=%fused_computation.20 | loop fusion | flops 81920 | bytes 163845 | tf_op jit(solution)/shard_map/add | solution.py:43
  39.1 0.5 low_rank.1
  39.6 1.1 %collective-permute-start.6 = (bf16[288,128]{1,0:T(8,128)(2,1)S(1)}, bf16[288,128]{1,0:T(8,128)(2,1)S(1)}, u32[]{:S(2)}, u32[]{:S(2)}) collective-permute-start(bf16[288,128]{1,0:T(8,128)(2,1)S(1)} %low_rank.1), channel_id=1, source_target_pairs={{0,1},{1,0},{2,3},{3,2},{4,5},{5,4},{6,7},{7,6},{8,9},{9,8},{10,11... | collective-permute-start | bytes 221192 | tf_op jit(solution)/shard_map/ppermute | solution.py:38
  40.8 3.8 %main_chunk.6 = (f32[576,1024]{1,0:T(8,128)S(1)}, f32[576,128]{1,0:T(8,128)S(1)}) custom-call(bf16[3,192,8192]{2,1,0:T(8,128)(2,1)S(1)} %copy-done, f32[576,1]{1,0:T(8,128)S(1)} %reshape.69.mask_ref, f32[1,8192]{1,0:T(1,128)S(1)} %bitcast.20, bf16[1,8192]{1,0:T(2,128)(2,1)S(1)} %reshape.64.embed_ref, ...), custom_call_target="tpu_custom_call", output_to_operand_aliasing={{0}: (6, {}), {1}: (7, {})} | custom-call | flops 1207959552 | bytes 3276800 | tf_op jit(solution)/shard_map/main_chunk/pallas_call | solution.py:116
  44.6 3.1 %collective-permute-start.7 = (bf16[288,128]{1,0:T(8,128)(2,1)S(1)}, bf16[288,128]{1,0:T(8,128)(2,1)S(1)}, u32[]{:S(2)}, u32[]{:S(2)}) collective-permute-start(bf16[288,128]{1,0:T(8,128)(2,1)S(1)} %add_convert_fusion.mine_ref), channel_id=1, source_target_pairs={{0,4},{2,6},{4,0},{6,2},{1,5},{3,7},{5,1},{7,3},{8,12},{10,14},{12... | collective-permute-start | bytes 221192 | tf_op jit(solution)/shard_map/ppermute | solution.py:38
  47.8 1.1 %collective-permute-start.8 = (bf16[288,128]{1,0:T(8,128)(2,1)S(1)}, bf16[288,128]{1,0:T(8,128)(2,1)S(1)}, u32[]{:S(2)}, u32[]{:S(2)}) collective-permute-start(bf16[288,128]{1,0:T(8,128)(2,1)S(1)} %add_convert_fusion.mine_ref), channel_id=1, source_target_pairs={{0,6},{2,4},{4,2},{6,0},{1,7},{3,5},{5,3},{7,1},{8,14},{10,12},{12... | collective-permute-start | bytes 221192 | tf_op jit(solution)/shard_map/ppermute | solution.py:38
  48.9 3.8 %main_chunk.7 = (f32[576,1024]{1,0:T(8,128)S(1)}, f32[576,128]{1,0:T(8,128)S(1)}) custom-call(bf16[3,192,8192]{2,1,0:T(8,128)(2,1)S(1)} %copy-done, f32[576,1]{1,0:T(8,128)S(1)} %reshape.69.mask_ref, f32[1,8192]{1,0:T(1,128)S(1)} %bitcast.21, bf16[1,8192]{1,0:T(2,128)(2,1)S(1)} %reshape.64.embed_ref, ...), custom_call_target="tpu_custom_call", output_to_operand_aliasing={{0}: (6, {}), {1}: (7, {})} | custom-call | flops 1207959552 | bytes 3276800 | tf_op jit(solution)/shard_map/main_chunk/pallas_call | solution.py:116
  52.7 0.6 %collective-permute-done.8.r2_ref = bf16[288,128]{1,0:T(8,128)(2,1)S(1)} collective-permute-done((bf16[288,128]{1,0:T(8,128)(2,1)S(1)}, bf16[288,128]{1,0:T(8,128)(2,1)S(1)}, u32[]{:S(2)}, u32[]{:S(2)}) %collective-permute-start.8) | collective-permute-done | bytes 73760 | tf_op jit(solution)/shard_map/ppermute | solution.py:38
  53.3 1.9 %final.1 = bf16[576,1024]{1,0:T(8,128)(2,1)} custom-call(bf16[288,128]{1,0:T(8,128)(2,1)S(1)} %add_convert_fusion.mine_ref, bf16[288,128]{1,0:T(8,128)(2,1)S(1)} %collective-permute-done.7.r1_ref, bf16[288,128]{1,0:T(8,128)(2,1)S(1)} %collective-permute-done.8.r2_ref, bf16[288,128]{1,0:T(8,128)(2,1)S(1)} %collective-permute-done.9.r3_ref, ...), custom_call_target="tpu_custom_call" | custom-call | tf_op jit(solution)/shard_map/final/pallas_call | solution.py:179
  (31 shorter events, 0.3 us)
Async XLA Ops:
  1.6 4.8 %collective-permute-start = (bf16[2,64,512]{2,1,0:T(8,128)(2,1)S(1)}, bf16[2,64,512]{2,1,0:T(8,128)(2,1)S(1)}, u32[]{:S(2)}, u32[]{:S(2)}) collective-permute-start(bf16[2,64,512]{2,1,0:T(8,128)(2,1)S(1)} %fusion.8), channel_id=1, source_target_pairs={{0,8},{8,0},{1,9},{9,1},{2,10},{10,2},{3,11},{11,3},{4,12},{12,4},... | collective-permute-start | bytes 393224 | tf_op jit(solution)/shard_map/ppermute | solution.py:38
  3.5 2.4 %dynamic-slice-start = ((f32[8192]{0:T(1024)}, s32[]{:T(128)}), f32[1024]{0:T(1024)S(1)}, s32[]{:S(2)}) async-start(f32[8192]{0:T(1024)} %param.14, s32[]{:T(128)} %select_n.44), calls=%async_computation | async-start | bytes 8704 | tf_op jit(solution)/shard_map/dynamic_slice | solution.py:244
  5.9 1.0 %copy-start.2 = (f32[1,2,64,1024]{3,2,1,0:T(8,128)S(1)}, f32[1,2,64,1024]{3,2,1,0:T(8,128)}, u32[]{:S(2)}) copy-start(f32[1,2,64,1024]{3,2,1,0:T(8,128)} %param.16) | copy-start | bytes 1572868
  5.9 5.5 %copy-start.1 = (f32[8192]{0:T(1024)S(1)}, f32[8192]{0:T(1024)}, u32[]{:S(2)}) copy-start(f32[8192]{0:T(1024)} %param.14) | copy-start | bytes 98308
  6.9 19.4 %collective-permute-start.1 = (bf16[2,64,512]{2,1,0:T(8,128)(2,1)S(1)}, bf16[2,64,512]{2,1,0:T(8,128)(2,1)S(1)}, u32[]{:S(2)}, u32[]{:S(2)}) collective-permute-start(bf16[2,64,512]{2,1,0:T(8,128)(2,1)S(1)} %fusion.7), channel_id=1, source_target_pairs={{0,32},{16,48},{32,0},{48,16},{1,33},{17,49},{33,1},{49,17},{2,34}... | collective-permute-start | bytes 393224 | tf_op jit(solution)/shard_map/ppermute | solution.py:38
  10.3 16.0 %collective-permute-start.2 = (bf16[2,64,512]{2,1,0:T(8,128)(2,1)S(1)}, bf16[2,64,512]{2,1,0:T(8,128)(2,1)S(1)}, u32[]{:S(2)}, u32[]{:S(2)}) collective-permute-start(bf16[2,64,512]{2,1,0:T(8,128)(2,1)S(1)} %fusion.7), channel_id=1, source_target_pairs={{0,48},{16,32},{32,16},{48,0},{1,49},{17,33},{33,17},{49,1},{2,50}... | collective-permute-start | bytes 393224 | tf_op jit(solution)/shard_map/ppermute | solution.py:38
  11.4 15.0 %collective-permute-start.3 = (bf16[2,64,512]{2,1,0:T(8,128)(2,1)S(1)}, bf16[2,64,512]{2,1,0:T(8,128)(2,1)S(1)}, u32[]{:S(2)}, u32[]{:S(2)}) collective-permute-start(bf16[2,64,512]{2,1,0:T(8,128)(2,1)S(1)} %fusion.7), channel_id=1, source_target_pairs={{0,16},{16,0},{32,48},{48,32},{1,17},{17,1},{33,49},{49,33},{2,18}... | collective-permute-start | bytes 393224 | tf_op jit(solution)/shard_map/ppermute | solution.py:38
  11.4 3.7 %copy-start = (bf16[3,192,8192]{2,1,0:T(8,128)(2,1)S(1)}, bf16[3,192,8192]{2,1,0:T(8,128)(2,1)}, u32[]{:S(2)}) copy-start(bf16[3,192,8192]{2,1,0:T(8,128)(2,1)} %x_ref.7) | copy-start | bytes 28311556
  26.5 10.4 %collective-permute-start.4 = (bf16[2,64,512]{2,1,0:T(8,128)(2,1)S(1)}, bf16[2,64,512]{2,1,0:T(8,128)(2,1)S(1)}, u32[]{:S(2)}, u32[]{:S(2)}) collective-permute-start(bf16[2,64,512]{2,1,0:T(8,128)(2,1)S(1)} %get-tuple-element.23), channel_id=1, source_target_pairs={{0,64},{64,0},{1,65},{65,1},{2,66},{66,2},{3,67},{67,3},{4,68},{68... | collective-permute-start | bytes 393224 | tf_op jit(solution)/shard_map/ppermute | solution.py:38
  30.4 6.5 %copy-start.3 = (f32[2,64,1024]{2,1,0:T(8,128)S(1)}, f32[2,64,1024]{2,1,0:T(8,128)}, u32[]{:S(2)}) copy-start(f32[2,64,1024]{2,1,0:T(8,128)} %param.19) | copy-start | bytes 1572868
  30.4 6.5 %copy-start.4 = (f32[2,64,1024]{2,1,0:T(8,128)S(1)}, f32[2,64,1024]{2,1,0:T(8,128)}, u32[]{:S(2)}) copy-start(f32[2,64,1024]{2,1,0:T(8,128)} %param.18) | copy-start | bytes 1572868
  30.4 6.5 %copy-start.5 = (f32[2,64,1024]{2,1,0:T(8,128)S(1)}, f32[2,64,1024]{2,1,0:T(8,128)}, u32[]{:S(2)}) copy-start(f32[2,64,1024]{2,1,0:T(8,128)} %param.17) | copy-start | bytes 1572868
  37.2 1.3 %collective-permute-start.11 = (f32[2,4,512]{2,1,0:T(4,128)S(1)}, f32[2,4,512]{2,1,0:T(4,128)S(1)}, u32[]{:S(2)}, u32[]{:S(2)}) collective-permute-start(f32[2,4,512]{2,1,0:T(4,128)S(1)} %get-tuple-element.27), channel_id=1, source_target_pairs={{0,8},{8,0},{1,9},{9,1},{2,10},{10,2},{3,11},{11,3},{4,12},{12,4},... | collective-permute-start | bytes 49160 | tf_op jit(solution)/shard_map/ppermute | solution.py:38
  37.3 1.8 %collective-permute-start.5 = (bf16[64,512]{1,0:T(8,128)(2,1)S(1)}, bf16[64,512]{1,0:T(8,128)(2,1)S(1)}, u32[]{:S(2)}, u32[]{:S(2)}) collective-permute-start(bf16[64,512]{1,0:T(8,128)(2,1)S(1)} %get-tuple-element.30.bown_ref), channel_id=1, source_target_pairs={{0,8},{8,0},{1,9},{9,1},{2,10},{10,2},{3,11},{11,3},{4,12},{12,4},... | collective-permute-start | bytes 196616 | tf_op jit(solution)/shard_map/ppermute | solution.py:38
  37.9 2.9 %collective-permute-start.10 = (bf16[64,512]{1,0:T(8,128)(2,1)S(1)}, bf16[64,512]{1,0:T(8,128)(2,1)S(1)}, u32[]{:S(2)}, u32[]{:S(2)}) collective-permute-start(bf16[64,512]{1,0:T(8,128)(2,1)S(1)} %get-tuple-element.29), channel_id=1, source_target_pairs={{0,8},{8,0},{1,9},{9,1},{2,10},{10,2},{3,11},{11,3},{4,12},{12,4},... | collective-permute-start | bytes 196616 | tf_op jit(solution)/shard_map/ppermute | solution.py:38
  39.6 5.0 %collective-permute-start.6 = (bf16[288,128]{1,0:T(8,128)(2,1)S(1)}, bf16[288,128]{1,0:T(8,128)(2,1)S(1)}, u32[]{:S(2)}, u32[]{:S(2)}) collective-permute-start(bf16[288,128]{1,0:T(8,128)(2,1)S(1)} %low_rank.1), channel_id=1, source_target_pairs={{0,1},{1,0},{2,3},{3,2},{4,5},{5,4},{6,7},{7,6},{8,9},{9,8},{10,11... | collective-permute-start | bytes 221192 | tf_op jit(solution)/shard_map/ppermute | solution.py:38
  44.6 8.1 %collective-permute-start.7 = (bf16[288,128]{1,0:T(8,128)(2,1)S(1)}, bf16[288,128]{1,0:T(8,128)(2,1)S(1)}, u32[]{:S(2)}, u32[]{:S(2)}) collective-permute-start(bf16[288,128]{1,0:T(8,128)(2,1)S(1)} %add_convert_fusion.mine_ref), channel_id=1, source_target_pairs={{0,4},{2,6},{4,0},{6,2},{1,5},{3,7},{5,1},{7,3},{8,12},{10,14},{12... | collective-permute-start | bytes 221192 | tf_op jit(solution)/shard_map/ppermute | solution.py:38
  47.8 5.6 %collective-permute-start.8 = (bf16[288,128]{1,0:T(8,128)(2,1)S(1)}, bf16[288,128]{1,0:T(8,128)(2,1)S(1)}, u32[]{:S(2)}, u32[]{:S(2)}) collective-permute-start(bf16[288,128]{1,0:T(8,128)(2,1)S(1)} %add_convert_fusion.mine_ref), channel_id=1, source_target_pairs={{0,6},{2,4},{4,2},{6,0},{1,7},{3,5},{5,3},{7,1},{8,14},{10,12},{12... | collective-permute-start | bytes 221192 | tf_op jit(solution)/shard_map/ppermute | solution.py:38
  48.9 4.4 %collective-permute-start.9 = (bf16[288,128]{1,0:T(8,128)(2,1)S(1)}, bf16[288,128]{1,0:T(8,128)(2,1)S(1)}, u32[]{:S(2)}, u32[]{:S(2)}) collective-permute-start(bf16[288,128]{1,0:T(8,128)(2,1)S(1)} %add_convert_fusion.mine_ref), channel_id=1, source_target_pairs={{0,2},{2,0},{4,6},{6,4},{1,3},{3,1},{5,7},{7,5},{8,10},{10,8},{12,... | collective-permute-start | bytes 221192 | tf_op jit(solution)/shard_map/ppermute | solution.py:38

commit v2 on v1

v2 whole, which is shorter than its diff:
```python
import functools
import itertools

import jax
import jax.numpy as jnp
from jax import lax
from jax.experimental import pallas as pl
from jax.experimental.pallas import tpu as pltpu
from jax.sharding import Mesh, PartitionSpec as P

beta_one = 0.9
beta_two = 0.999
learn_rate = 0.03
adam_count = 100
epsilon = 1e-08
adapter_scale = 2.0
norm_epsilon = 1e-05

SIZES = {"zh": 2, "y": 4, "c": 2, "x": 4, "zl": 2}
DP = ("zh", "y", "c")
TENSOR = ("x", "zl")
UNIT = 1024
FEATURES = 8192
MIN_PROMPT = 24
SKIP = 16
MIB = 1 << 20


def f32(v):
    return v.astype(jnp.float32)


def bf16(v):
    return v.astype(jnp.bfloat16)


def exchange(v, axes, key):
    ids = list(itertools.product(*[range(SIZES[a]) for a in axes]))
    index = {t: i for i, t in enumerate(ids)}
    pairs = [(index[t], index[tuple(a ^ k for a, k in zip(t, key))]) for t in ids]
    return lax.ppermute(v, tuple(axes), pairs)


def adam_update(summed_grad, first_moment, second_moment):
    new_first = beta_one * first_moment + (1.0 - beta_one) * summed_grad
    new_second = beta_two * second_moment + (1.0 - beta_two) * summed_grad * summed_grad
    return new_first, new_second


def factor_update(new_first, new_second, param_rows):
    step_size = learn_rate / (1.0 - beta_one**adam_count)
    divisor = jnp.sqrt(new_second / (1.0 - beta_two**adam_count)) + epsilon
    return param_rows - step_size * new_first / divisor


def hidden_block(x_ref, lead, mask_ref, embed, seq, lanes):
    states = x_ref[lead + (seq, slice(None), lanes)].astype(jnp.float32)[MIN_PROMPT - SKIP :]
    return jnp.where(mask_ref[seq] > 0.0, embed, states)


def normalise(x_ref, unit, mask_ref, gain_ref, embed_ref, k0, normed_ref, sq_ref, first):
    seqs, kept, _ = mask_ref.shape
    for seq in range(seqs):
        rows = slice(seq * kept, (seq + 1) * kept)
        squares = None if first else sq_ref[rows]
        for j in range(UNIT // 128):
            at = slice(k0 + j * 128, k0 + (j + 1) * 128)
            hidden = hidden_block(x_ref, (unit,), mask_ref, embed_ref[:, at], seq, slice(j * 128, (j + 1) * 128))
            squares = hidden * hidden if squares is None else squares + hidden * hidden
            normed_ref[rows, j * 128 : (j + 1) * 128] = (hidden * gain_ref[:, at]).astype(jnp.bfloat16)
        sq_ref[rows] = squares


def fetch(x_ref, w_ref, unit, x_dst, w_dst, slot, sem):
    k0 = unit * UNIT
    return [
        pltpu.make_async_copy(w_ref.at[pl.ds(k0, UNIT)], w_dst.at[slot], sem.at[0]),
        pltpu.make_async_copy(
            x_ref.at[:, pl.ds(SKIP, x_ref.shape[1] - SKIP), pl.ds(k0, UNIT)], x_dst.at[slot], sem.at[1]
        ),
    ]


def multiply(units, blocks, mask_ref, gain_ref, embed_ref, acc_ref, sq_ref, normed, fresh):
    def ready(i):
        x_buf, _, slot, copies = blocks[i]
        for copy in copies:
            copy.wait()
        normalise(
            x_buf, slot, mask_ref, gain_ref, embed_ref, units[i] * UNIT, normed[i % 2], sq_ref, fresh and i == 0
        )

    ready(0)
    for i in range(len(units)):
        if i + 1 < len(units):
            ready(i + 1)
        _, w_buf, slot, _ = blocks[i]
        product = jnp.dot(normed[i % 2][...], w_buf[slot], preferred_element_type=jnp.float32)
        if fresh and i == 0:
            acc_ref[...] = product
        else:
            acc_ref[...] += product


def head_kernel(
    units, following, place_ref, prompt_ref, bits_ref, gain_ref, embed_ref, x_ref, w_ref, _,
    acc_ref, sq_ref, mask_ref, own_ref, xs_ref, x_next, w_next,
    x_buf, w_buf, normed_a, normed_b, sems, own_sem,
):
    seqs, kept, _ = mask_ref.shape
    cols = own_ref.shape[1]
    col = pl.multiple_of(place_ref[0], cols)
    own = pltpu.make_async_copy(x_ref.at[:, :, pl.ds(col, cols)], xs_ref, own_sem)
    own.start()
    blocks = []
    for i, unit in enumerate(units):
        copies = fetch(x_ref, w_ref, unit, x_buf, w_buf, i, sems.at[i])
        for copy in copies:
            copy.start()
        blocks.append((x_buf, w_buf, i, copies))
    after = []
    for i, unit in enumerate(following):
        after += fetch(x_ref, w_ref, unit, x_next, w_next, i, sems.at[len(units) + i])
    for copy in after:
        copy.start()

    length = bits_ref.shape[1]
    here = lax.broadcasted_iota(jnp.int32, (kept, length), 0) + MIN_PROMPT
    there = lax.broadcasted_iota(jnp.int32, (kept, length), 1)
    for seq in range(seqs):
        chosen = jnp.logical_and(here == there, here >= prompt_ref[seq])
        bits = jnp.where(chosen, bits_ref[seq : seq + 1, :], 0)
        column = jnp.sum((bits == 1).astype(jnp.float32), axis=1, keepdims=True)
        mask_ref[seq] = jnp.broadcast_to(column, (kept, 128))

    own.wait()
    for seq in range(seqs):
        rows = slice(seq * kept, (seq + 1) * kept)
        for j in range(cols // 128):
            at = pl.ds(pl.multiple_of(col + j * 128, 128), 128)
            lanes = slice(j * 128, (j + 1) * 128)
            states = xs_ref[seq, SKIP:, lanes].astype(jnp.float32)[MIN_PROMPT - SKIP :]
            hidden = jnp.where(mask_ref[seq] > 0.0, embed_ref[:, at], states)
            own_ref[rows, lanes] = (hidden * gain_ref[:, at]).astype(jnp.bfloat16)

    multiply(units, blocks, mask_ref, gain_ref, embed_ref, acc_ref, sq_ref, (normed_a, normed_b), True)
    for copy in after:
        copy.wait()


def next_kernel(units, following, *refs):
    mask_ref, gain_ref, embed_ref, x_ref, w_ref, _, acc_in, sq_in, x_now, w_now, acc_ref, sq_ref = refs[:12]
    refs = refs[12:]
    after = []
    if following:
        x_next, w_next, normed_a, normed_b, sems = refs
        for i, unit in enumerate(following):
            after += fetch(x_ref, w_ref, unit, x_next, w_next, i, sems.at[i])
    else:
        normed_a, normed_b, sems = refs
    for copy in after:
        copy.start()
    blocks = [(x_now, w_now, i, []) for i in range(len(units))]
    multiply(units, blocks, mask_ref, gain_ref, embed_ref, acc_ref, sq_ref, (normed_a, normed_b), False)
    for copy in after:
        copy.wait()


VMEM = pl.BlockSpec(memory_space=pltpu.VMEM)
SMEM = pl.BlockSpec(memory_space=pltpu.SMEM)
HBM = pl.BlockSpec(memory_space=pltpu.HBM)
ANY = pl.BlockSpec(memory_space=pl.ANY)


def block_shapes(x, w, count):
    seqs, length, _ = x.shape
    return ((count, seqs, length - SKIP, UNIT), jnp.bfloat16), ((count, UNIT, w.shape[1]), jnp.bfloat16)


def cost(rows, cols, units):
    return pl.CostEstimate(
        flops=2 * rows * UNIT * len(units) * cols,
        bytes_accessed=2 * UNIT * len(units) * (rows + cols),
        transcendentals=0,
    )


def main_head(place, prompt_len, bits, gain, embed, x, w, token, units, following):
    seqs, length, _ = x.shape
    kept = length - MIN_PROMPT
    rows, cols = seqs * kept, w.shape[1]
    shapes = [
        ((rows, cols), jnp.float32),
        ((rows, 128), jnp.float32),
        ((seqs, kept, 128), jnp.float32),
        ((rows, cols), jnp.bfloat16),
        ((seqs, length, cols), jnp.bfloat16),
        *block_shapes(x, w, len(following)),
    ]
    return pl.pallas_call(
        functools.partial(head_kernel, units, following),
        in_specs=[SMEM, SMEM, VMEM, VMEM, VMEM, HBM, HBM, ANY],
        out_specs=[VMEM] * len(shapes),
        out_shape=[jax.ShapeDtypeStruct(*s) for s in shapes],
        scratch_shapes=[
            *[pltpu.VMEM(*s) for s in block_shapes(x, w, len(units))],
            pltpu.VMEM((rows, UNIT), jnp.bfloat16),
            pltpu.VMEM((rows, UNIT), jnp.bfloat16),
            pltpu.SemaphoreType.DMA((len(units) + len(following), 2)),
            pltpu.SemaphoreType.DMA,
        ],
        compiler_params=pltpu.CompilerParams(vmem_limit_bytes=36 * MIB),
        cost_estimate=cost(rows, cols, units),
        name="main_head",
    )(place, prompt_len, bits, gain, embed, x, w, token)


def main_next(mask, gain, embed, x, w, token, acc, sq, x_now, w_now, units, following):
    rows, cols = acc.shape
    shapes = [(acc.shape, jnp.float32), (sq.shape, jnp.float32)]
    if following:
        shapes += block_shapes(x, w, len(following))
    return pl.pallas_call(
        functools.partial(next_kernel, units, following),
        in_specs=[VMEM, VMEM, VMEM, HBM, HBM, ANY, VMEM, VMEM, VMEM, VMEM],
        out_specs=[VMEM] * len(shapes),
        out_shape=[jax.ShapeDtypeStruct(*s) for s in shapes],
        input_output_aliases={6: 0, 7: 1},
        scratch_shapes=[
            pltpu.VMEM((rows, UNIT), jnp.bfloat16),
            pltpu.VMEM((rows, UNIT), jnp.bfloat16),
            pltpu.SemaphoreType.DMA((max(len(following), 1), 2)),
        ],
        compiler_params=pltpu.CompilerParams(vmem_limit_bytes=20 * MIB),
        cost_estimate=cost(rows, cols, units),
        name="main_next",
    )(mask, gain, embed, x, w, token, acc, sq, x_now, w_now)


def low_rank_kernel(place_ref, own_ref, mine_ref, other_ref, out_ref):
    rows, cols = own_ref.shape
    half = out_ref.shape[0]
    width = cols // 2
    core = place_ref[1]
    dims = (((1,), (1,)), ((), ()))
    mine = own_ref[:, pl.ds(pl.multiple_of(core * width, width), width)]
    other = own_ref[:, pl.ds(pl.multiple_of((1 - core) * width, width), width)]
    prod = lax.dot_general(mine, mine_ref[...], dims, preferred_element_type=jnp.float32)
    prod += lax.dot_general(other, other_ref[...], dims, preferred_element_type=jnp.float32)
    rank = prod.shape[1]
    tail = jnp.concatenate([prod[half:], jnp.zeros((2 * half - rows, rank), jnp.float32)], axis=0)
    out_ref[...] = jnp.concatenate([prod[:half], tail], axis=1).astype(jnp.bfloat16)


def low_rank(place, own, mine, other):
    half = -(-own.shape[0] // 32) * 16
    return pl.pallas_call(
        low_rank_kernel,
        in_specs=[SMEM, VMEM, VMEM, VMEM],
        out_specs=VMEM,
        out_shape=jax.ShapeDtypeStruct((half, 2 * mine.shape[0]), jnp.bfloat16),
        compiler_params=pltpu.CompilerParams(vmem_limit_bytes=8 * MIB),
        name="low_rank",
    )(place, own, mine, other)


def final_kernel(
    place_ref, prompt_ref, embed_ref, mine_ref, r1_ref, r2_ref, r3_ref, a_ref, acc_ref, sq_ref, mask_ref, xs_ref,
    out_ref, stage_ref, sems,
):
    seqs, kept, _ = mask_ref.shape
    cols = acc_ref.shape[1]
    rank = a_ref.shape[0]
    half = mine_ref.shape[0]
    col = pl.multiple_of(place_ref[0], cols)
    embed = embed_ref[:, pl.ds(col, cols)]
    total = mine_ref[...].astype(jnp.float32) + r1_ref[...].astype(jnp.float32)
    total += r2_ref[...].astype(jnp.float32) + r3_ref[...].astype(jnp.float32)
    low = jnp.concatenate([total[:, :rank], total[: seqs * kept - half, rank:]], axis=0)
    copies = []
    for seq in range(seqs):
        rows = slice(seq * kept, (seq + 1) * kept)
        adapter = jnp.dot(low[rows].astype(jnp.bfloat16), a_ref[...], preferred_element_type=jnp.float32)
        mean = jnp.sum(sq_ref[rows], axis=1, keepdims=True) * (1.0 / FEATURES)
        scale = lax.rsqrt(mean + norm_epsilon)
        position = lax.broadcasted_iota(jnp.int32, (kept, 1), 0) + MIN_PROMPT
        response = position >= prompt_ref[seq]
        states = xs_ref[seq].astype(jnp.float32)
        head, states = states[:MIN_PROMPT], states[MIN_PROMPT:]
        hidden = jnp.where(mask_ref[seq][:, :1] > 0.0, embed, states)
        projected = (acc_ref[rows] + adapter_scale * adapter) * scale
        value = jnp.where(response, hidden + projected, states)
        stage_ref[seq] = jnp.concatenate([head, value], axis=0).astype(jnp.bfloat16)
        copy = pltpu.make_async_copy(stage_ref.at[seq], out_ref.at[seq], sems.at[seq])
        copy.start()
        copies.append(copy)
    for copy in copies:
        copy.wait()


def final(place, prompt_len, embed, mine, received, a, acc, sq, mask, xs):
    return pl.pallas_call(
        final_kernel,
        in_specs=[SMEM, SMEM] + [VMEM] * 10,
        out_specs=HBM,
        out_shape=jax.ShapeDtypeStruct(xs.shape, jnp.bfloat16),
        scratch_shapes=[pltpu.VMEM(xs.shape, jnp.bfloat16), pltpu.SemaphoreType.DMA((xs.shape[0],))],
        compiler_params=pltpu.CompilerParams(vmem_limit_bytes=20 * MIB),
        name="final",
    )(place, prompt_len, embed, mine, *received, a, acc, sq, mask, xs)


def local(x, mask_bits, prompt_len, weight, norm_gain, mask_embed, grads, factors, first_moment, second_moment):
    width = x.shape[2]
    cols = weight.shape[1]
    half = cols // 2
    core = lax.axis_index("c")
    col_start = lax.axis_index(TENSOR) * cols
    rank = factors.shape[1]
    share = rank // 16

    def own_half(v):
        return lax.dynamic_slice_in_dim(v, core * half, half, v.ndim - 1)

    def other_half(v):
        return lax.dynamic_slice_in_dim(v, (1 - core) * half, half, v.ndim - 1)

    grad = grads[0]
    from_core = exchange(bf16(other_half(grad)), "c", (1,))
    total = own_half(grad) + f32(from_core)
    sent = bf16(total)
    from_y = [exchange(sent, "y", (k,)) for k in (2, 3, 1)]
    total = total + f32(from_y[0]) + f32(from_y[1]) + f32(from_y[2])
    from_z = exchange(bf16(total), ("zh",), (1,))
    total = total + f32(from_z)

    new_first, new_second = adam_update(total, own_half(first_moment), own_half(second_moment))
    shipped = bf16(factor_update(new_first, new_second, own_half(factors)))
    b_own = shipped[1]
    b_other = exchange(b_own, "c", (1,))
    a_own = shipped[0]
    a_other = exchange(a_own, "c", (1,))

    my_row = lax.axis_index(DP) * share
    pair_row = (lax.axis_index(DP) + 1 - 2 * core) * share
    rows_out = lax.dynamic_slice_in_dim(total, pair_row, share, 1)
    rows_in = exchange(rows_out, "c", (1,))
    rows_mine = lax.dynamic_slice_in_dim(total, my_row, share, 1)

    def ordered(mine, others):
        return jnp.where(
            core == 0, jnp.concatenate([mine, others], -1), jnp.concatenate([others, mine], -1)
        )

    row_total = ordered(rows_mine, rows_in)
    out_first, out_second = adam_update(
        row_total,
        lax.dynamic_slice_in_dim(first_moment, my_row, share, 1),
        lax.dynamic_slice_in_dim(second_moment, my_row, share, 1),
    )

    gain = norm_gain.reshape(1, width)
    embed = f32(mask_embed).reshape(1, width)
    place = jnp.stack([col_start, core]).astype(jnp.int32)
    parts = [(0, 1, 2, 3), (4, 5), (6,), (7,)]
    acc, sq, mask, own_normed, xs, x_next, w_next = main_head(
        place, prompt_len, mask_bits, gain, embed, x, weight, from_core, parts[0], parts[1]
    )
    acc, sq, x_next, w_next = main_next(
        mask, gain, embed, x, weight, from_y[0], acc, sq, x_next, w_next, parts[1], parts[2]
    )
    low = low_rank(place, own_normed, b_own, b_other)
    from_zl = exchange(low, ("zl",), (1,))
    acc, sq, x_next, w_next = main_next(
        mask, gain, embed, x, weight, b_other, acc, sq, x_next, w_next, parts[2], parts[3]
    )
    low = bf16(f32(low) + f32(from_zl))
    from_x = [exchange(low, ("x",), (k,)) for k in (2, 3, 1)]
    acc, sq = main_next(mask, gain, embed, x, weight, from_zl, acc, sq, x_next, w_next, parts[3], ())
    a_full = ordered(a_own, a_other)
    out = final(place, prompt_len, embed, low, from_x, a_full, acc, sq, mask, xs)
    return out, out_first, out_second


def solution(mesh):
    split = Mesh(mesh.devices.reshape(2, 4, 2, 4, 2), ("zh", "y", "c", "x", "zl"))
    placed = (
        P(DP, None, None),
        P(DP, None),
        P(DP),
        P(None, TENSOR),
        P(),
        P(),
        P(DP, None, None, TENSOR),
        P(None, None, TENSOR),
        P(None, None, TENSOR),
        P(None, None, TENSOR),
    )
    return jax.shard_map(
        local,
        mesh=split,
        in_specs=placed,
        out_specs=(P(DP, None, TENSOR), P(None, DP, TENSOR), P(None, DP, TENSOR)),
        check_vma=False,
    )
```

time: 56.2 us -> 54.5 us (0.970); the launches traced: 55.2 us -> 54.2 us
  Pallas kernels: 27.8 us -> 19 us
  waiting for transfers between devices: 1.09 us -> 5.28 us
  local copies, waits for them, and re-layouts: 8.67 us -> 10.9 us
  starting transfers between devices: 14.5 us -> 15.3 us
  other arithmetic: 2.16 us -> 2.8 us
    pallas_call x6, Pallas kernels: 27.8 us -> 19 us  [the longest x1 10.1 us: main_head(): pl.pallas_call(functools.partial(head_kernel, units, following), in_specs...]
    unnamed x12 -> x30, local copies, waits for them, and re-layouts: 4.22 us -> 9.86 us
    ppermute x12, waiting for transfers between devices: 1.09 us -> 5.28 us  [exchange(): return lax.ppermute(v, tuple(axes), pairs)]
    dynamic_slice x5 -> x0, local copies, waits for them, and re-layouts: 2.18 us -> none  [the longest x1 1.35 us: local(): xs = lax.dynamic_slice_in_dim(x, col_start, cols, 2).reshape(rows, cols)]
    reshape x2 -> x0, local copies, waits for them, and re-layouts: 0.96 us -> none  [the longest x1 0.74 us: local(): embed = mask_embed.reshape(1, width)]
    ppermute x12, starting transfers between devices: 14.5 us -> 15.3 us  [exchange(): return lax.ppermute(v, tuple(axes), pairs)]
    convert_element_type x5 -> x4, other arithmetic: 0.7 us -> 1.31 us  [bf16(): return v.astype(jnp.bfloat16)]
  transfers between devices with their start and end apart: 12 -> 12, of which waited for: 2 -> 5; matrix products, arithmetic and copies ran while one was open for 10% -> 3% of each run, Pallas kernels for 47% -> 31%
where the time goes in v2:
time: 54.5 us; the launch traced here: 54.2 us
  Pallas kernels  19 us (35%)
  starting transfers between devices  15.3 us (28%)
  local copies, waits for them, and re-layouts  10.9 us (20%)
  waiting for transfers between devices  5.28 us (10%)
  other arithmetic  2.8 us (5%)
  between operations  1.06 us (2%)
    ppermute x12, starting transfers between devices, exchange(): return lax.ppermute(v, tuple(axes), pairs)  15.3 us
    pallas_call x1, Pallas kernels, main_head(): pl.pallas_call(functools.partial(head_kernel, units, following), in_specs...  10.1 us
    unnamed x30, local copies, waits for them, and re-layouts  9.86 us
    pallas_call x3, Pallas kernels, main_next(): pl.pallas_call(functools.partial(next_kernel, units, following), in_specs...  5.73 us
    ppermute x12, waiting for transfers between devices, exchange(): return lax.ppermute(v, tuple(axes), pairs)  5.28 us
    pallas_call x1, Pallas kernels, final(): pl.pallas_call(final_kernel, in_specs=[SMEM, SMEM] + [VMEM] * 10, out_spe...  2.13 us
    convert_element_type x4, other arithmetic, bf16(): return v.astype(jnp.bfloat16)  1.31 us
  transfers between devices with their start and end apart: 12, of which 5 were waited for; matrix products, arithmetic and copies ran while one was open for 3% of the time, Pallas kernels for 31%

profile of v2, /device:TPU:0, one launch (start us, length us, event | category | flops | bytes accessed | tf_op | source)
XLA Modules:
  0.0 54.2 jit_solution(8275586236522638151)
XLA Ops:
  0.6 1.0 %fusion.8 = bf16[2,64,512]{2,1,0:T(8,128)(2,1)S(1)} fusion(f32[1,2,64,1024]{3,2,1,0:T(8,128)} %param.16, s32[]{:T(128)S(6)} %select_n.33), kind=kLoop, calls=%fused_computation.13 | loop fusion | bytes 262148 | tf_op jit(solution)/shard_map/convert_element_type | solution.py:34
  1.7 0.7 %reshape.20 = f32[8192]{0:T(1024)S(1)} convert(bf16[8192]{0:T(1024)(128)(2,1)} %param.15) | non-fusion elementwise | flops 8192 | bytes 49152 | tf_op jit(solution)/shard_map/reshape | solution.py:363
  2.5 0.5 collective-permute-done._
  3.0 1.0 %fusion.7 = bf16[2,64,512]{2,1,0:T(8,128)(2,1)S(1)} fusion(bf16[2,64,512]{2,1,0:T(8,128)(2,1)S(1)} %collective-permute-done._, f32[1,2,64,1024]{3,2,1,0:T(8,128)} %param.16, s32[]{:T(128)S(6)} %select_n.34), kind=kLoop, calls=%fused_computation.12 | loop fusion | flops 196608 | bytes 524292 | tf_op jit(solution)/shard_map/convert_element_type | solution.py:34
  4.0 1.7 %collective-permute-start.3 = (bf16[2,64,512]{2,1,0:T(8,128)(2,1)S(1)}, bf16[2,64,512]{2,1,0:T(8,128)(2,1)S(1)}, u32[]{:S(2)}, u32[]{:S(2)}) collective-permute-start(bf16[2,64,512]{2,1,0:T(8,128)(2,1)S(1)} %fusion.7), channel_id=1, source_target_pairs={{0,16},{16,0},{32,48},{48,32},{1,17},{17,1},{33,49},{49,33},{2,18}... | collective-permute-start | bytes 393224 | tf_op jit(solution)/shard_map/ppermute | solution.py:41
  5.8 2.2 %collective-permute-start.2 = (bf16[2,64,512]{2,1,0:T(8,128)(2,1)S(1)}, bf16[2,64,512]{2,1,0:T(8,128)(2,1)S(1)}, u32[]{:S(2)}, u32[]{:S(2)}) collective-permute-start(bf16[2,64,512]{2,1,0:T(8,128)(2,1)S(1)} %fusion.7), channel_id=1, source_target_pairs={{0,48},{16,32},{32,16},{48,0},{1,49},{17,33},{33,17},{49,1},{2,50}... | collective-permute-start | bytes 393224 | tf_op jit(solution)/shard_map/ppermute | solution.py:41
  7.9 0.7 %collective-permute-start.1 = (bf16[2,64,512]{2,1,0:T(8,128)(2,1)S(1)}, bf16[2,64,512]{2,1,0:T(8,128)(2,1)S(1)}, u32[]{:S(2)}, u32[]{:S(2)}) collective-permute-start(bf16[2,64,512]{2,1,0:T(8,128)(2,1)S(1)} %fusion.7), channel_id=1, source_target_pairs={{0,32},{16,48},{32,0},{48,16},{1,33},{17,49},{33,1},{49,17},{2,34}... | collective-permute-start | bytes 393224 | tf_op jit(solution)/shard_map/ppermute | solution.py:41
  8.7 0.9 %copy-done.3 = f32[8192]{0:T(1024)S(1)} copy-done((f32[8192]{0:T(1024)S(1)}, f32[8192]{0:T(1024)}, u32[]{:S(2)}) %copy-start.3) | copy-done | bytes 32792
  9.6 0.9 %copy-done.5 = s32[3,192]{1,0:T(4,128)S(1)} copy-done((s32[3,192]{1,0:T(4,128)S(1)}, s32[3,192]{1,0:T(4,128)}, u32[]{:S(2)}) %copy-start.5) | copy-done | bytes 2328
  10.5 0.7 %copy-done.6 = s32[3]{0:T(128)S(1)} copy-done((s32[3]{0:T(128)S(1)}, s32[3]{0:T(128)}, u32[]{:S(2)}) %copy-start.6) | copy-done | bytes 36
  11.1 10.1 %main_head.1 = (f32[504,1024]{1,0:T(8,128)S(1)}, f32[504,128]{1,0:T(8,128)S(1)}, f32[3,168,128]{2,1,0:T(8,128)S(1)}, bf16[504,1024]{1,0:T(8,128)(2,1)S(1)}, bf16...) custom-call(s32[2]{0:T(128)S(1)} %pad_add_fusion.place_ref, ...), custom_call_target="tpu_custom_call" | custom-call | flops 4227858432 | bytes 12517376 | tf_op jit(solution)/shard_map/main_head/pallas_call | solution.py:200
  21.3 0.1 fusion.10
  21.4 4.0 %collective-permute-start.4 = (bf16[2,64,512]{2,1,0:T(8,128)(2,1)S(1)}, bf16[2,64,512]{2,1,0:T(8,128)(2,1)S(1)}, u32[]{:S(2)}, u32[]{:S(2)}) collective-permute-start(bf16[2,64,512]{2,1,0:T(8,128)(2,1)S(1)} %get-tuple-element.39), channel_id=1, source_target_pairs={{0,64},{64,0},{1,65},{65,1},{2,66},{66,2},{3,67},{67,3},{4,68},{68... | collective-permute-start | bytes 393224 | tf_op jit(solution)/shard_map/ppermute | solution.py:41
  25.4 2.7 %main_next.3 = (f32[504,1024]{1,0:T(8,128)S(1)}, f32[504,128]{1,0:T(8,128)S(1)}, bf16[1,3,176,1024]{3,2,1,0:T(8,128)(2,1)S(1)}, bf16[1,1024,1024]{2,1,0:T(8,128)(2,1)S(1)}) custom-call(f32[3,168,128]{2,1,0:T(8,128)S(1)} %get-tuple-element.21.refs_0_.mask_ref, f32[1,8192]{1,0:T(1,128)S(1)} %bitcast.25, ...), custom_call_target="tpu_custom_call", output_to_operand_aliasing={{0}: (6, {}), {1}: (7, {})} | custom-call | flops 2113929216 | bytes 6258688 | tf_op jit(solution)/shard_map/main_next/pallas_call | solution.py:223
  28.1 0.5 collective-permute-done.4
  28.6 0.2 fusion.6
  28.9 0.6 %collective-permute-start.10 = (bf16[64,512]{1,0:T(8,128)(2,1)S(1)}, bf16[64,512]{1,0:T(8,128)(2,1)S(1)}, u32[]{:S(2)}, u32[]{:S(2)}) collective-permute-start(bf16[64,512]{1,0:T(8,128)(2,1)S(1)} %get-tuple-element.43), channel_id=1, source_target_pairs={{0,8},{8,0},{1,9},{9,1},{2,10},{10,2},{3,11},{11,3},{4,12},{12,4},... | collective-permute-start | bytes 196616 | tf_op jit(solution)/shard_map/ppermute | solution.py:41
  29.5 0.1 collective-permute-start.5
  29.6 0.5 collective-permute-done.11
  30.1 0.7 %fusion.9 = (f32[2,4,1024]{2,1,0:T(4,128)}, f32[2,4,1024]{2,1,0:T(4,128)}) fusion(f32[2,64,1024]{2,1,0:T(8,128)S(1)} %copy-done.9, s32[]{:T(128)S(6)} %select_n.37, f32[2,4,512]{2,1,0:T(4,128)S(1)} %get-tuple-element.42, f32[2,4,512]{2,1,0:T(4,128)S(1)} %collective-permute-done.11, pred[]{:T(512)S(6)} %eq.4, f32[2,64,1024]{2,1,0:T(8,128)S(1)} %copy-done.10), kind=kLoop, calls=%fused_computation.19 | loop fusion | flops 81920 | bytes 163845 | tf_op jit(solution)/shard_map/add | solution.py:46
  30.8 1.0 %low_rank.1 = bf16[256,128]{1,0:T(8,128)(2,1)S(1)} custom-call(s32[2]{0:T(128)S(1)} %pad_add_fusion.place_ref, bf16[504,1024]{1,0:T(8,128)(2,1)S(1)} %get-tuple-element.20.own_ref, bf16[64,512]{1,0:T(8,128)(2,1)S(1)} %get-tuple-element.44.mine_ref, bf16[64,512]{1,0:T(8,128)(2,1)S(1)} %collective-permute-done.5.other_ref.refs_5_), custom_call_target="tpu_custom_call" | custom-call | tf_op jit(solution)/shard_map/low_rank/pallas_call | solution.py:257
  31.8 1.4 %collective-permute-start.6 = (bf16[256,128]{1,0:T(8,128)(2,1)S(1)}, bf16[256,128]{1,0:T(8,128)(2,1)S(1)}, u32[]{:S(2)}, u32[]{:S(2)}) collective-permute-start(bf16[256,128]{1,0:T(8,128)(2,1)S(1)} %low_rank.1), channel_id=1, source_target_pairs={{0,1},{1,0},{2,3},{3,2},{4,5},{5,4},{6,7},{7,6},{8,9},{9,8},{10,11... | collective-permute-start | bytes 196616 | tf_op jit(solution)/shard_map/ppermute | solution.py:41
  33.2 5.8 %copy-done = bf16[8192,1024]{1,0:T(8,128)(2,1)S(1)} copy-done((bf16[8192,1024]{1,0:T(8,128)(2,1)S(1)}, bf16[8192,1024]{1,0:T(8,128)(2,1)}, u32[]{:S(2)}) %copy-start) | copy-done | bytes 16777240
  39.0 1.6 %copy-done.2 = f32[504,1024]{1,0:T(8,128)S(1)} copy-done((f32[504,1024]{1,0:T(8,128)S(1)}, f32[504,1024]{1,0:T(8,128)}, u32[]{:S(2)}) %copy-start.2) | copy-done | bytes 2064408
  40.6 1.7 %main_next.4 = (f32[504,1024]{1,0:T(8,128)S(1)}, f32[504,128]{1,0:T(8,128)S(1)}, bf16[1,3,176,1024]{3,2,1,0:T(8,128)(2,1)S(1)}, bf16[1,1024,1024]{2,1,0:T(8,128)(2,1)S(1)}) custom-call(f32[3,168,128]{2,1,0:T(8,128)S(1)} %get-tuple-element.21.refs_0_.mask_ref, f32[1,8192]{1,0:T(1,128)S(1)} %bitcast.26, ...), custom_call_target="tpu_custom_call", output_to_operand_aliasing={{0}: (6, {}), {1}: (7, {})} | custom-call | flops 1056964608 | bytes 3129344 | tf_op jit(solution)/shard_map/main_next/pallas_call | solution.py:223
  42.3 1.8 %collective-permute-start.9 = (bf16[256,128]{1,0:T(8,128)(2,1)S(1)}, bf16[256,128]{1,0:T(8,128)(2,1)S(1)}, u32[]{:S(2)}, u32[]{:S(2)}) collective-permute-start(bf16[256,128]{1,0:T(8,128)(2,1)S(1)} %add_convert_fusion.mine_ref), channel_id=1, source_target_pairs={{0,2},{2,0},{4,6},{6,4},{1,3},{3,1},{5,7},{7,5},{8,10},{10,8},{12,... | collective-permute-start | bytes 196616 | tf_op jit(solution)/shard_map/ppermute | solution.py:41
  44.1 2.1 %collective-permute-start.8 = (bf16[256,128]{1,0:T(8,128)(2,1)S(1)}, bf16[256,128]{1,0:T(8,128)(2,1)S(1)}, u32[]{:S(2)}, u32[]{:S(2)}) collective-permute-start(bf16[256,128]{1,0:T(8,128)(2,1)S(1)} %add_convert_fusion.mine_ref), channel_id=1, source_target_pairs={{0,6},{2,4},{4,2},{6,0},{1,7},{3,5},{5,3},{7,1},{8,14},{10,12},{12... | collective-permute-start | bytes 196616 | tf_op jit(solution)/shard_map/ppermute | solution.py:41
  46.2 0.6 %collective-permute-start.7 = (bf16[256,128]{1,0:T(8,128)(2,1)S(1)}, bf16[256,128]{1,0:T(8,128)(2,1)S(1)}, u32[]{:S(2)}, u32[]{:S(2)}) collective-permute-start(bf16[256,128]{1,0:T(8,128)(2,1)S(1)} %add_convert_fusion.mine_ref), channel_id=1, source_target_pairs={{0,4},{2,6},{4,0},{6,2},{1,5},{3,7},{5,1},{7,3},{8,12},{10,14},{12... | collective-permute-start | bytes 196616 | tf_op jit(solution)/shard_map/ppermute | solution.py:41
  46.8 1.4 %main_next.5 = (f32[504,1024]{1,0:T(8,128)S(1)}, f32[504,128]{1,0:T(8,128)S(1)}) custom-call(f32[3,168,128]{2,1,0:T(8,128)S(1)} %get-tuple-element.21.refs_0_.mask_ref, f32[1,8192]{1,0:T(1,128)S(1)} %bitcast.27, f32[1,8192]{1,0:T(1,128)S(1)} %bitcast.22, bf16[3,192,8192]{2,1,0:T(8,128)(2,1)S(1)} %bitcast.18, ...), custom_call_target="tpu_custom_call", output_to_operand_aliasing={{0}: (6, {}), {1}: (7, {})} | custom-call | flops 1056964608 | bytes 3129344 | tf_op jit(solution)/shard_map/main_next/pallas_call | solution.py:223
  48.2 1.4 %collective-permute-done.8.r2_ref = bf16[256,128]{1,0:T(8,128)(2,1)S(1)} collective-permute-done((bf16[256,128]{1,0:T(8,128)(2,1)S(1)}, bf16[256,128]{1,0:T(8,128)(2,1)S(1)}, u32[]{:S(2)}, u32[]{:S(2)}) %collective-permute-start.8) | collective-permute-done | bytes 65568 | tf_op jit(solution)/shard_map/ppermute | solution.py:41
  49.5 2.4 %collective-permute-done.7.r1_ref = bf16[256,128]{1,0:T(8,128)(2,1)S(1)} collective-permute-done((bf16[256,128]{1,0:T(8,128)(2,1)S(1)}, bf16[256,128]{1,0:T(8,128)(2,1)S(1)}, u32[]{:S(2)}, u32[]{:S(2)}) %collective-permute-start.7) | collective-permute-done | bytes 65568 | tf_op jit(solution)/shard_map/ppermute | solution.py:41
  51.9 2.1 %final.1 = bf16[3,192,1024]{2,1,0:T(8,128)(2,1)} custom-call(s32[2]{0:T(128)S(1)} %pad_add_fusion.place_ref, s32[3]{0:T(128)S(1)} %copy-done.7, f32[1,8192]{1,0:T(1,128)S(1)} %bitcast.23, bf16[256,128]{1,0:T(8,128)(2,1)S(1)} %add_convert_fusion.mine_ref, bf16[256,128]{1,0:T(8,128)(2,1)S(1)} %collective-permute-done.7.r1_ref, ...), custom_call_target="tpu_custom_call" | custom-call | tf_op jit(solution)/shard_map/final/pallas_call | solution.py:302
  (40 shorter events, 0.4 us)
Async XLA Ops:
  1.6 1.4 %collective-permute-start = (bf16[2,64,512]{2,1,0:T(8,128)(2,1)S(1)}, bf16[2,64,512]{2,1,0:T(8,128)(2,1)S(1)}, u32[]{:S(2)}, u32[]{:S(2)}) collective-permute-start(bf16[2,64,512]{2,1,0:T(8,128)(2,1)S(1)} %fusion.8), channel_id=1, source_target_pairs={{0,8},{8,0},{1,9},{9,1},{2,10},{10,2},{3,11},{11,3},{4,12},{12,4},... | collective-permute-start | bytes 393224 | tf_op jit(solution)/shard_map/ppermute | solution.py:41
  4.0 17.2 %collective-permute-start.3 = (bf16[2,64,512]{2,1,0:T(8,128)(2,1)S(1)}, bf16[2,64,512]{2,1,0:T(8,128)(2,1)S(1)}, u32[]{:S(2)}, u32[]{:S(2)}) collective-permute-start(bf16[2,64,512]{2,1,0:T(8,128)(2,1)S(1)} %fusion.7), channel_id=1, source_target_pairs={{0,16},{16,0},{32,48},{48,32},{1,17},{17,1},{33,49},{49,33},{2,18}... | collective-permute-start | bytes 393224 | tf_op jit(solution)/shard_map/ppermute | solution.py:41
  5.8 15.5 %collective-permute-start.2 = (bf16[2,64,512]{2,1,0:T(8,128)(2,1)S(1)}, bf16[2,64,512]{2,1,0:T(8,128)(2,1)S(1)}, u32[]{:S(2)}, u32[]{:S(2)}) collective-permute-start(bf16[2,64,512]{2,1,0:T(8,128)(2,1)S(1)} %fusion.7), channel_id=1, source_target_pairs={{0,48},{16,32},{32,16},{48,0},{1,49},{17,33},{33,17},{49,1},{2,50}... | collective-permute-start | bytes 393224 | tf_op jit(solution)/shard_map/ppermute | solution.py:41
  7.9 13.3 %collective-permute-start.1 = (bf16[2,64,512]{2,1,0:T(8,128)(2,1)S(1)}, bf16[2,64,512]{2,1,0:T(8,128)(2,1)S(1)}, u32[]{:S(2)}, u32[]{:S(2)}) collective-permute-start(bf16[2,64,512]{2,1,0:T(8,128)(2,1)S(1)} %fusion.7), channel_id=1, source_target_pairs={{0,32},{16,48},{32,0},{48,16},{1,33},{17,49},{33,1},{49,17},{2,34}... | collective-permute-start | bytes 393224 | tf_op jit(solution)/shard_map/ppermute | solution.py:41
  8.7 16.7 %slice-start = ((s8[9437184]{0:T(1024)(128)(4,1)}), s8[4194304]{0:T(1024)(128)(4,1)S(1)}, s32[]{:S(2)}) async-start(s8[9437184]{0:T(1024)(128)(4,1)} %bitcast.17), calls=%async_computation | async-start | bytes 8388608
  8.7 0.9 %copy-start.3 = (f32[8192]{0:T(1024)S(1)}, f32[8192]{0:T(1024)}, u32[]{:S(2)}) copy-start(f32[8192]{0:T(1024)} %param.14) | copy-start | bytes 98308
  9.6 0.9 %copy-start.5 = (s32[3,192]{1,0:T(4,128)S(1)}, s32[3,192]{1,0:T(4,128)}, u32[]{:S(2)}) copy-start(s32[3,192]{1,0:T(4,128)} %bits_ref.1) | copy-start | bytes 6916
  10.5 0.7 %copy-start.6 = (s32[3]{0:T(128)S(1)}, s32[3]{0:T(128)}, u32[]{:S(2)}) copy-start(s32[3]{0:T(128)} %prompt_ref.3) | copy-start | bytes 40
  11.1 10.1 %copy-start.8 = (f32[1,2,64,1024]{3,2,1,0:T(8,128)S(1)}, f32[1,2,64,1024]{3,2,1,0:T(8,128)}, u32[]{:S(2)}) copy-start(f32[1,2,64,1024]{3,2,1,0:T(8,128)} %param.16) | copy-start | bytes 1572868
  11.1 14.2 %slice-start.1 = ((s8[9437184]{0:T(1024)(128)(4,1)}), s8[4194304]{0:T(1024)(128)(4,1)S(1)}, s32[]{:S(2)}) async-start(s8[9437184]{0:T(1024)(128)(4,1)} %bitcast.17), calls=%async_computation.1 | async-start | bytes 8388608
  11.1 14.2 %slice-start.2 = ((s8[9437184]{0:T(1024)(128)(4,1)}), s8[1048576]{0:T(1024)(128)(4,1)S(1)}, s32[]{:S(2)}) async-start(s8[9437184]{0:T(1024)(128)(4,1)} %bitcast.17), calls=%async_computation.2 | async-start | bytes 2097152
  21.4 7.2 %collective-permute-start.4 = (bf16[2,64,512]{2,1,0:T(8,128)(2,1)S(1)}, bf16[2,64,512]{2,1,0:T(8,128)(2,1)S(1)}, u32[]{:S(2)}, u32[]{:S(2)}) collective-permute-start(bf16[2,64,512]{2,1,0:T(8,128)(2,1)S(1)} %get-tuple-element.39), channel_id=1, source_target_pairs={{0,64},{64,0},{1,65},{65,1},{2,66},{66,2},{3,67},{67,3},{4,68},{68... | collective-permute-start | bytes 393224 | tf_op jit(solution)/shard_map/ppermute | solution.py:41
  25.3 3.2 %copy-start.9 = (f32[2,64,1024]{2,1,0:T(8,128)S(1)}, f32[2,64,1024]{2,1,0:T(8,128)}, u32[]{:S(2)}) copy-start(f32[2,64,1024]{2,1,0:T(8,128)} %param.19) | copy-start | bytes 1572868
  25.3 3.2 %copy-start.10 = (f32[2,64,1024]{2,1,0:T(8,128)S(1)}, f32[2,64,1024]{2,1,0:T(8,128)}, u32[]{:S(2)}) copy-start(f32[2,64,1024]{2,1,0:T(8,128)} %param.18) | copy-start | bytes 1572868
  25.4 3.2 %copy-start.11 = (f32[2,64,1024]{2,1,0:T(8,128)S(1)}, f32[2,64,1024]{2,1,0:T(8,128)}, u32[]{:S(2)}) copy-start(f32[2,64,1024]{2,1,0:T(8,128)} %param.17) | copy-start | bytes 1572868
  28.1 5.1 %copy-start.1 = (f32[504,1024]{1,0:T(8,128)}, f32[504,1024]{1,0:T(8,128)S(1)}, u32[]{:S(2)}) copy-start(f32[504,1024]{1,0:T(8,128)S(1)} %get-tuple-element.26.refs_6_) | copy-start | bytes 6193156
  28.1 5.1 %copy-start.4 = (f32[8192]{0:T(1024)S(1)}, f32[8192]{0:T(1024)}, u32[]{:S(2)}) copy-start(f32[8192]{0:T(1024)} %param.14) | copy-start | bytes 98308
  28.8 1.3 %collective-permute-start.11 = (f32[2,4,512]{2,1,0:T(4,128)S(1)}, f32[2,4,512]{2,1,0:T(4,128)S(1)}, u32[]{:S(2)}, u32[]{:S(2)}) collective-permute-start(f32[2,4,512]{2,1,0:T(4,128)S(1)} %get-tuple-element.41), channel_id=1, source_target_pairs={{0,8},{8,0},{1,9},{9,1},{2,10},{10,2},{3,11},{11,3},{4,12},{12,4},... | collective-permute-start | bytes 49160 | tf_op jit(solution)/shard_map/ppermute | solution.py:41
  28.9 4.2 %collective-permute-start.10 = (bf16[64,512]{1,0:T(8,128)(2,1)S(1)}, bf16[64,512]{1,0:T(8,128)(2,1)S(1)}, u32[]{:S(2)}, u32[]{:S(2)}) collective-permute-start(bf16[64,512]{1,0:T(8,128)(2,1)S(1)} %get-tuple-element.43), channel_id=1, source_target_pairs={{0,8},{8,0},{1,9},{9,1},{2,10},{10,2},{3,11},{11,3},{4,12},{12,4},... | collective-permute-start | bytes 196616 | tf_op jit(solution)/shard_map/ppermute | solution.py:41
  29.5 1.3 %collective-permute-start.5 = (bf16[64,512]{1,0:T(8,128)(2,1)S(1)}, bf16[64,512]{1,0:T(8,128)(2,1)S(1)}, u32[]{:S(2)}, u32[]{:S(2)}) collective-permute-start(bf16[64,512]{1,0:T(8,128)(2,1)S(1)} %get-tuple-element.44.mine_ref), channel_id=1, source_target_pairs={{0,8},{8,0},{1,9},{9,1},{2,10},{10,2},{3,11},{11,3},{4,12},{12,4},... | collective-permute-start | bytes 196616 | tf_op jit(solution)/shard_map/ppermute | solution.py:41
  31.8 10.5 %collective-permute-start.6 = (bf16[256,128]{1,0:T(8,128)(2,1)S(1)}, bf16[256,128]{1,0:T(8,128)(2,1)S(1)}, u32[]{:S(2)}, u32[]{:S(2)}) collective-permute-start(bf16[256,128]{1,0:T(8,128)(2,1)S(1)} %low_rank.1), channel_id=1, source_target_pairs={{0,1},{1,0},{2,3},{3,2},{4,5},{5,4},{6,7},{7,6},{8,9},{9,8},{10,11... | collective-permute-start | bytes 196616 | tf_op jit(solution)/shard_map/ppermute | solution.py:41
  33.2 5.8 %copy-start = (bf16[8192,1024]{1,0:T(8,128)(2,1)S(1)}, bf16[8192,1024]{1,0:T(8,128)(2,1)}, u32[]{:S(2)}) copy-start(bf16[8192,1024]{1,0:T(8,128)(2,1)} %refs_4_.5) | copy-start | bytes 50331652
  39.0 1.6 %copy-start.2 = (f32[504,1024]{1,0:T(8,128)S(1)}, f32[504,1024]{1,0:T(8,128)}, u32[]{:S(2)}) copy-start(f32[504,1024]{1,0:T(8,128)} %copy-done.1) | copy-start | bytes 6193156
  42.3 5.9 %collective-permute-start.9 = (bf16[256,128]{1,0:T(8,128)(2,1)S(1)}, bf16[256,128]{1,0:T(8,128)(2,1)S(1)}, u32[]{:S(2)}, u32[]{:S(2)}) collective-permute-start(bf16[256,128]{1,0:T(8,128)(2,1)S(1)} %add_convert_fusion.mine_ref), channel_id=1, source_target_pairs={{0,2},{2,0},{4,6},{6,4},{1,3},{3,1},{5,7},{7,5},{8,10},{10,8},{12,... | collective-permute-start | bytes 196616 | tf_op jit(solution)/shard_map/ppermute | solution.py:41
  44.1 5.5 %collective-permute-start.8 = (bf16[256,128]{1,0:T(8,128)(2,1)S(1)}, bf16[256,128]{1,0:T(8,128)(2,1)S(1)}, u32[]{:S(2)}, u32[]{:S(2)}) collective-permute-start(bf16[256,128]{1,0:T(8,128)(2,1)S(1)} %add_convert_fusion.mine_ref), channel_id=1, source_target_pairs={{0,6},{2,4},{4,2},{6,0},{1,7},{3,5},{5,3},{7,1},{8,14},{10,12},{12... | collective-permute-start | bytes 196616 | tf_op jit(solution)/shard_map/ppermute | solution.py:41
  46.2 5.8 %collective-permute-start.7 = (bf16[256,128]{1,0:T(8,128)(2,1)S(1)}, bf16[256,128]{1,0:T(8,128)(2,1)S(1)}, u32[]{:S(2)}, u32[]{:S(2)}) collective-permute-start(bf16[256,128]{1,0:T(8,128)(2,1)S(1)} %add_convert_fusion.mine_ref), channel_id=1, source_target_pairs={{0,4},{2,6},{4,0},{6,2},{1,5},{3,7},{5,1},{7,3},{8,12},{10,14},{12... | collective-permute-start | bytes 196616 | tf_op jit(solution)/shard_map/ppermute | solution.py:41
  46.8 5.1 %copy-start.7 = (s32[3]{0:T(128)S(1)}, s32[3]{0:T(128)}, u32[]{:S(2)}) copy-start(s32[3]{0:T(128)} %prompt_ref.3) | copy-start | bytes 40

commit v3 on v2

v3 whole, which is shorter than its diff:
```python
import functools
import itertools

import jax
import jax.numpy as jnp
from jax import lax
from jax.experimental import pallas as pl
from jax.experimental.pallas import tpu as pltpu
from jax.sharding import Mesh, PartitionSpec as P

beta_one = 0.9
beta_two = 0.999
learn_rate = 0.03
adam_count = 100
epsilon = 1e-08
adapter_scale = 2.0
norm_epsilon = 1e-05

SIZES = {"zh": 2, "y": 4, "c": 2, "x": 4, "zl": 2}
DP = ("zh", "y", "c")
TENSOR = ("x", "zl")
UNIT = 1024
FEATURES = 8192
MIN_PROMPT = 24
SKIP = 16
MIB = 1 << 20


def f32(v):
    return v.astype(jnp.float32)


def bf16(v):
    return v.astype(jnp.bfloat16)


def exchange(v, axes, key):
    ids = list(itertools.product(*[range(SIZES[a]) for a in axes]))
    index = {t: i for i, t in enumerate(ids)}
    pairs = [(index[t], index[tuple(a ^ k for a, k in zip(t, key))]) for t in ids]
    return lax.ppermute(v, tuple(axes), pairs)


def adam_update(summed_grad, first_moment, second_moment):
    new_first = beta_one * first_moment + (1.0 - beta_one) * summed_grad
    new_second = beta_two * second_moment + (1.0 - beta_two) * summed_grad * summed_grad
    return new_first, new_second


def factor_update(new_first, new_second, param_rows):
    step_size = learn_rate / (1.0 - beta_one**adam_count)
    divisor = jnp.sqrt(new_second / (1.0 - beta_two**adam_count)) + epsilon
    return param_rows - step_size * new_first / divisor


def hidden_block(x_ref, mask_ref, embed, seq, lanes):
    states = x_ref[seq, :, lanes].astype(jnp.float32)[MIN_PROMPT - SKIP :]
    return jnp.where(mask_ref[seq] > 1.5, embed, states)


def normalise(x_ref, mask_ref, gain_ref, embed_ref, k0, normed_ref, sq_ref, first):
    seqs, kept, _ = mask_ref.shape
    for seq in range(seqs):
        rows = slice(seq * kept, (seq + 1) * kept)
        squares = None if first else sq_ref[rows]
        for j in range(UNIT // 128):
            at = slice(k0 + j * 128, k0 + (j + 1) * 128)
            lanes = slice(j * 128, (j + 1) * 128)
            hidden = hidden_block(x_ref, mask_ref, embed_ref[:, at], seq, lanes)
            squares = hidden * hidden if squares is None else squares + hidden * hidden
            normed_ref[rows, lanes] = (hidden * gain_ref[:, at]).astype(jnp.bfloat16)
        sq_ref[rows] = squares


def fetch(x_ref, w_ref, unit, x_dst, w_dst, sem):
    k0 = unit * UNIT
    return [
        pltpu.make_async_copy(w_ref.at[pl.ds(k0, UNIT)], w_dst, sem.at[0]),
        pltpu.make_async_copy(x_ref.at[:, pl.ds(SKIP, x_ref.shape[1] - SKIP), pl.ds(k0, UNIT)], x_dst, sem.at[1]),
    ]


def start(copies):
    for copy in copies:
        copy.start()


def wait(copies):
    for copy in copies:
        copy.wait()


def multiply(blocks, mask_ref, gain_ref, embed_ref, acc_ref, sq_ref, normed, fresh):
    def ready(i):
        unit, x_buf, _, copies = blocks[i]
        wait(copies)
        normalise(x_buf, mask_ref, gain_ref, embed_ref, unit * UNIT, normed[i % 2], sq_ref, fresh and i == 0)

    ready(0)
    for i in range(len(blocks)):
        if i + 1 < len(blocks):
            ready(i + 1)
        product = jnp.dot(normed[i % 2][...], blocks[i][2][...], preferred_element_type=jnp.float32)
        if fresh and i == 0:
            acc_ref[...] = product
        else:
            acc_ref[...] += product


def pack_kernel(grad_ref, own_ref, other_ref, wide_ref, sems):
    width = own_ref.shape[2]
    core = lax.axis_index("c")
    near = pl.ds(pl.multiple_of(core * width, width), width)
    far = pl.ds(pl.multiple_of((1 - core) * width, width), width)
    other = pltpu.make_async_copy(grad_ref.at[0, :, :, far], wide_ref, sems.at[0])
    own = pltpu.make_async_copy(grad_ref.at[0, :, :, near], own_ref, sems.at[1])
    other.start()
    own.start()
    other.wait()
    other_ref[...] = wide_ref[...].astype(jnp.bfloat16)
    own.wait()


def pack(grads):
    _, two, rank, cols = grads.shape
    shape = (two, rank, cols // 2)
    return pl.pallas_call(
        pack_kernel,
        in_specs=[HBM],
        out_specs=[VMEM, VMEM],
        out_shape=[jax.ShapeDtypeStruct(shape, jnp.float32), jax.ShapeDtypeStruct(shape, jnp.bfloat16)],
        scratch_shapes=[pltpu.VMEM(shape, jnp.float32), pltpu.SemaphoreType.DMA((2,))],
        compiler_params=pltpu.CompilerParams(vmem_limit_bytes=8 * MIB),
        name="pack",
    )(in_hbm(grads))


def head_kernel(units, following, *refs):
    prompt_ref, bits_ref, gain_ref, embed_ref, x_ref, w_ref, _ = refs[:7]
    acc_ref, sq_ref, mask_ref, mine_ref, other_ref, xs_ref, gain_out = refs[7:14]
    ahead = refs[14 : 14 + 2 * len(following)]
    refs = refs[14 + 2 * len(following) :]
    bufs = refs[: 2 * len(units)]
    normed_a, normed_b, prompt_buf, bits_buf, sems, own_sems = refs[2 * len(units) :]
    seqs, kept, _ = mask_ref.shape
    cols = xs_ref.shape[2]
    width = cols // 2
    col = pl.multiple_of((lax.axis_index("x") * 2 + lax.axis_index("zl")) * cols, cols)
    core = lax.axis_index("c")
    small = [
        pltpu.make_async_copy(prompt_ref, prompt_buf, own_sems.at[0]),
        pltpu.make_async_copy(bits_ref, bits_buf, own_sems.at[1]),
        pltpu.make_async_copy(gain_ref, gain_out, own_sems.at[2]),
    ]
    start(small)
    own = pltpu.make_async_copy(x_ref.at[:, :, pl.ds(col, cols)], xs_ref, own_sems.at[3])
    own.start()
    blocks = []
    for i, unit in enumerate(units):
        copies = fetch(x_ref, w_ref, unit, bufs[2 * i], bufs[2 * i + 1], sems.at[i])
        start(copies)
        blocks.append((unit, bufs[2 * i], bufs[2 * i + 1], copies))
    after = []
    for i, unit in enumerate(following):
        after += fetch(x_ref, w_ref, unit, ahead[2 * i], ahead[2 * i + 1], sems.at[len(units) + i])
    start(after)

    wait(small)
    length = bits_buf.shape[1]
    here = lax.broadcasted_iota(jnp.int32, (kept, length), 0) + MIN_PROMPT
    there = lax.broadcasted_iota(jnp.int32, (kept, length), 1)
    position = lax.broadcasted_iota(jnp.int32, (kept, 1), 0) + MIN_PROMPT
    for seq in range(seqs):
        bits = jnp.where(here == there, bits_buf[seq : seq + 1, :], 0)
        chosen = 1.0 + jnp.sum((bits == 1).astype(jnp.float32), axis=1, keepdims=True)
        column = jnp.where(position >= prompt_buf[0:1, seq : seq + 1], chosen, 0.0)
        mask_ref[seq] = jnp.broadcast_to(column, (kept, 128))

    own.wait()
    for at_core, dst in ((core, mine_ref), (1 - core, other_ref)):
        for seq in range(seqs):
            rows = slice(seq * kept, (seq + 1) * kept)
            for j in range(width // 128):
                lanes = pl.multiple_of(at_core * width + j * 128, 128)
                states = xs_ref[seq, SKIP:, pl.ds(lanes, 128)].astype(jnp.float32)[MIN_PROMPT - SKIP :]
                at = pl.ds(pl.multiple_of(col + lanes, 128), 128)
                hidden = jnp.where(mask_ref[seq] > 1.5, embed_ref[:, at], states)
                dst[rows, j * 128 : (j + 1) * 128] = (hidden * gain_out[:, at]).astype(jnp.bfloat16)

    multiply(blocks, mask_ref, gain_out, embed_ref, acc_ref, sq_ref, (normed_a, normed_b), True)
    wait(after)


def half_copies(sources, targets, core, sems):
    width = targets[0].shape[2]
    at = pl.ds(pl.multiple_of(core * width, width), width)
    return [pltpu.make_async_copy(s.at[:, :, at], t, sems.at[i]) for i, (s, t) in enumerate(zip(sources, targets))]


def next_kernel(units, following, factors, *refs):
    mask_ref, gain_ref, embed_ref, x_ref, w_ref, _, acc_in, sq_in = refs[:8]
    now = refs[8 : 8 + 2 * len(units)]
    refs = refs[8 + 2 * len(units) :]
    if factors:
        params, refs = refs[:3], refs[3:]
    acc_ref, sq_ref = refs[:2]
    ahead = refs[2 : 2 + 2 * len(following)]
    refs = refs[2 + 2 * len(following) :]
    if factors:
        halves, eights, refs = refs[:3], refs[3:5], refs[5:]
    normed_a, normed_b, sems = refs[:3]
    after = []
    if factors:
        after += half_copies(params, halves, lax.axis_index("c"), refs[3])
        at = pl.ds(pl.multiple_of((lax.axis_index("zh") * 4 + lax.axis_index("y")) * 8, 8), 8)
        for i in range(2):
            after.append(pltpu.make_async_copy(params[1 + i].at[:, at], eights[i], refs[3].at[3 + i]))
    for i, unit in enumerate(following):
        after += fetch(x_ref, w_ref, unit, ahead[2 * i], ahead[2 * i + 1], sems.at[i])
    start(after)
    blocks = [(unit, now[2 * i], now[2 * i + 1], []) for i, unit in enumerate(units)]
    multiply(blocks, mask_ref, gain_ref, embed_ref, acc_ref, sq_ref, (normed_a, normed_b), False)
    wait(after)


def last_kernel(units, *refs):
    mask_ref, gain_ref, embed_ref, _, acc_in, sq_in, xs_ref, a_mine, a_other = refs[:9]
    rows_mine, rows_other, first_ref, second_ref = refs[9:13]
    now = refs[13 : 13 + 2 * len(units)]
    acc_ref, sq_ref, base_ref, scale_ref, a_ref, first_out, second_out = refs[13 + 2 * len(units) :][:7]
    normed_a, normed_b, first_buf, second_buf, sems = refs[20 + 2 * len(units) :]
    seqs, kept, _ = mask_ref.shape
    cols = xs_ref.shape[2]
    width = cols // 2
    col = pl.multiple_of((lax.axis_index("x") * 2 + lax.axis_index("zl")) * cols, cols)
    even = lax.axis_index("c") == 0

    a_ref[:, :width] = jnp.where(even, a_mine[...], a_other[...])
    a_ref[:, width:] = jnp.where(even, a_other[...], a_mine[...])
    mine, other = rows_mine[...], rows_other[...]
    summed = jnp.concatenate([jnp.where(even, mine, other), jnp.where(even, other, mine)], axis=2)
    share = summed.shape[1] // 2
    first, second = adam_update(summed, first_ref[...], second_ref[...])
    first_buf[...] = jnp.where(even, first[:, :share], first[:, share:])
    second_buf[...] = jnp.where(even, second[:, :share], second[:, share:])
    out = [
        pltpu.make_async_copy(first_buf, first_out, sems.at[0]),
        pltpu.make_async_copy(second_buf, second_out, sems.at[1]),
    ]
    start(out)

    blocks = [(unit, now[2 * i], now[2 * i + 1], []) for i, unit in enumerate(units)]
    multiply(blocks, mask_ref, gain_ref, embed_ref, acc_ref, sq_ref, (normed_a, normed_b), False)
    for seq in range(seqs):
        rows = slice(seq * kept, (seq + 1) * kept)
        mean = jnp.sum(sq_ref[rows], axis=1, keepdims=True) * (1.0 / FEATURES)
        scale = jnp.broadcast_to(lax.rsqrt(mean + norm_epsilon), (kept, 128))
        code = mask_ref[seq]
        scale_ref[rows] = jnp.where(code > 0.5, adapter_scale * scale, 0.0)
        for j in range(cols // 128):
            lanes = slice(j * 128, (j + 1) * 128)
            at = pl.ds(pl.multiple_of(col + j * 128, 128), 128)
            states = xs_ref[seq, :, lanes].astype(jnp.float32)
            head, states = states[:MIN_PROMPT], states[MIN_PROMPT:]
            hidden = jnp.where(code > 1.5, embed_ref[:, at], states)
            value = jnp.where(code > 0.5, hidden + scale * acc_ref[rows, lanes], states)
            base_ref[seq, :MIN_PROMPT, lanes] = head
            base_ref[seq, MIN_PROMPT:, lanes] = value
    wait(out)


VMEM = pl.BlockSpec(memory_space=pltpu.VMEM)
SMEM = pl.BlockSpec(memory_space=pltpu.SMEM)
HBM = pl.BlockSpec(memory_space=pltpu.HBM)
ANY = pl.BlockSpec(memory_space=pl.ANY)


def in_hbm(v):
    return pltpu.with_memory_space_constraint(v, pltpu.HBM)


def block_shapes(x, w, count):
    seqs, length, _ = x.shape
    return [((seqs, length - SKIP, UNIT), jnp.bfloat16), ((UNIT, w.shape[1]), jnp.bfloat16)] * count


def cost(rows, cols, units):
    return pl.CostEstimate(
        flops=2 * rows * UNIT * len(units) * cols,
        bytes_accessed=2 * UNIT * len(units) * (rows + cols),
        transcendentals=0,
    )


def small_call(kernel, shapes, name, *args):
    in_specs = [ANY if isinstance(v, tuple) else VMEM for v in args]
    args = [v[0] if isinstance(v, tuple) else v for v in args]
    return pl.pallas_call(
        kernel,
        in_specs=in_specs,
        out_specs=[VMEM] * len(shapes),
        out_shape=[jax.ShapeDtypeStruct(*v) for v in shapes],
        compiler_params=pltpu.CompilerParams(vmem_limit_bytes=4 * MIB),
        name=name,
    )(*args)


def main_head(prompt_len, bits, gain, embed, x, w, token, units, following):
    seqs, length, width = x.shape
    kept = length - MIN_PROMPT
    rows, cols = seqs * kept, w.shape[1]
    shapes = [
        ((rows, cols), jnp.float32),
        ((rows, 128), jnp.float32),
        ((seqs, kept, 128), jnp.float32),
        ((rows, cols // 2), jnp.bfloat16),
        ((rows, cols // 2), jnp.bfloat16),
        ((seqs, length, cols), jnp.bfloat16),
        ((1, width), jnp.float32),
        *block_shapes(x, w, len(following)),
    ]
    out = pl.pallas_call(
        functools.partial(head_kernel, units, following),
        in_specs=[HBM, HBM, HBM, VMEM, HBM, HBM, ANY],
        out_specs=[VMEM] * len(shapes),
        out_shape=[jax.ShapeDtypeStruct(*s) for s in shapes],
        scratch_shapes=[
            *[pltpu.VMEM(*s) for s in block_shapes(x, w, len(units))],
            pltpu.VMEM((rows, UNIT), jnp.bfloat16),
            pltpu.VMEM((rows, UNIT), jnp.bfloat16),
            pltpu.VMEM(prompt_len.shape, jnp.int32),
            pltpu.VMEM(bits.shape, jnp.int32),
            pltpu.SemaphoreType.DMA((len(units) + len(following), 2)),
            pltpu.SemaphoreType.DMA((4,)),
        ],
        compiler_params=pltpu.CompilerParams(vmem_limit_bytes=20 * MIB),
        cost_estimate=cost(rows, cols, units),
        name="main_head",
    )(in_hbm(prompt_len), in_hbm(bits), in_hbm(gain), embed, in_hbm(x), in_hbm(w), token)
    return out[:7], out[7:]


def main_next(mask, gain, embed, x, w, token, acc, sq, now, units, following, params=()):
    rows, cols = acc.shape
    shapes = [(acc.shape, jnp.float32), (sq.shape, jnp.float32), *block_shapes(x, w, len(following))]
    if params:
        two, rank, _ = params[0].shape
        shapes += [((two, rank, cols // 2), jnp.float32)] * 3 + [((two, 8, cols), jnp.float32)] * 2
    out = pl.pallas_call(
        functools.partial(next_kernel, units, following, bool(params)),
        in_specs=[VMEM, VMEM, VMEM, HBM, HBM, ANY, VMEM, VMEM] + [VMEM] * len(now) + [HBM] * len(params),
        out_specs=[VMEM] * len(shapes),
        out_shape=[jax.ShapeDtypeStruct(*s) for s in shapes],
        input_output_aliases={6: 0, 7: 1},
        scratch_shapes=[
            pltpu.VMEM((rows, UNIT), jnp.bfloat16),
            pltpu.VMEM((rows, UNIT), jnp.bfloat16),
            pltpu.SemaphoreType.DMA((len(following), 2)),
            *([pltpu.SemaphoreType.DMA((5,))] if params else []),
        ],
        compiler_params=pltpu.CompilerParams(vmem_limit_bytes=12 * MIB),
        cost_estimate=cost(rows, cols, units),
        name="main_next",
    )(mask, gain, embed, in_hbm(x), in_hbm(w), token, acc, sq, *now, *[in_hbm(v) for v in params])
    ahead = 2 + 2 * len(following)
    return out[:2], out[2:ahead], out[ahead:]


def main_last(mask, gain, embed, token, acc, sq, xs, a_mine, a_other, moments, now, units):
    rows, cols = acc.shape
    rank = a_mine.shape[0]
    out_rows = (2, 4, cols)
    shapes = [
        (acc.shape, jnp.float32),
        (sq.shape, jnp.float32),
        (xs.shape, jnp.float32),
        (sq.shape, jnp.float32),
        ((rank, cols), jnp.bfloat16),
        (out_rows, jnp.float32),
        (out_rows, jnp.float32),
    ]
    return pl.pallas_call(
        functools.partial(last_kernel, units),
        in_specs=[VMEM, VMEM, VMEM, ANY] + [VMEM] * (9 + len(now)),
        out_specs=[VMEM] * 5 + [HBM] * 2,
        out_shape=[jax.ShapeDtypeStruct(*s) for s in shapes],
        input_output_aliases={4: 0, 5: 1},
        scratch_shapes=[
            pltpu.VMEM((rows, UNIT), jnp.bfloat16),
            pltpu.VMEM((rows, UNIT), jnp.bfloat16),
            pltpu.VMEM(out_rows, jnp.float32),
            pltpu.VMEM(out_rows, jnp.float32),
            pltpu.SemaphoreType.DMA((2,)),
        ],
        compiler_params=pltpu.CompilerParams(vmem_limit_bytes=12 * MIB),
        cost_estimate=cost(rows, cols, units),
        name="main_last",
    )(mask, gain, embed, token, acc, sq, xs, a_mine, a_other, *moments, *now)[2:]


def add_kernel(mine_ref, theirs_ref, *refs):
    refs[-1][...] = (mine_ref[...].astype(jnp.float32) + theirs_ref[...].astype(jnp.float32)).astype(jnp.bfloat16)


def gather_sum_kernel(mine_ref, r1_ref, r2_ref, r3_ref, _, total_ref, sent_ref):
    total = mine_ref[...] + r1_ref[...].astype(jnp.float32)
    total += r2_ref[...].astype(jnp.float32) + r3_ref[...].astype(jnp.float32)
    total_ref[...] = total
    sent_ref[...] = total.astype(jnp.bfloat16)


def update_kernel(total_ref, theirs_ref, factors_ref, first_ref, second_ref, _, a_ref, b_ref, rows_ref, sum_ref):
    total = total_ref[...] + theirs_ref[...].astype(jnp.float32)
    new_first, new_second = adam_update(total, first_ref[...], second_ref[...])
    shipped = factor_update(new_first, new_second, factors_ref[...]).astype(jnp.bfloat16)
    a_ref[...] = shipped[0]
    b_ref[...] = shipped[1]
    at = pl.ds(pl.multiple_of((lax.axis_index("zh") * 4 + lax.axis_index("y")) * 8, 8), 8)
    sum_ref[...] = total
    rows_ref[...] = sum_ref[:, at]


def low_rank_kernel(own_mine_ref, own_other_ref, mine_ref, other_ref, out_ref):
    rows = own_mine_ref.shape[0]
    half = out_ref.shape[0]
    dims = (((1,), (1,)), ((), ()))
    prod = lax.dot_general(own_mine_ref[...], mine_ref[...], dims, preferred_element_type=jnp.float32)
    prod += lax.dot_general(own_other_ref[...], other_ref[...], dims, preferred_element_type=jnp.float32)
    rank = prod.shape[1]
    tail = jnp.concatenate([prod[half:], jnp.zeros((2 * half - rows, rank), jnp.float32)], axis=0)
    out_ref[...] = jnp.concatenate([prod[:half], tail], axis=1).astype(jnp.bfloat16)


def low_rank(own_mine, own_other, mine, other):
    half = -(-own_mine.shape[0] // 32) * 16
    return pl.pallas_call(
        low_rank_kernel,
        in_specs=[VMEM] * 4,
        out_specs=VMEM,
        out_shape=jax.ShapeDtypeStruct((half, 2 * mine.shape[0]), jnp.bfloat16),
        compiler_params=pltpu.CompilerParams(vmem_limit_bytes=8 * MIB),
        name="low_rank",
    )(own_mine, own_other, mine, other)


def final_kernel(mine_ref, r1_ref, r2_ref, r3_ref, a_ref, base_ref, scale_ref, out_ref, stage_ref, sems):
    seqs, length, _ = base_ref.shape
    kept = length - MIN_PROMPT
    rank = a_ref.shape[0]
    half = mine_ref.shape[0]
    total = mine_ref[...].astype(jnp.float32) + r1_ref[...].astype(jnp.float32)
    total += r2_ref[...].astype(jnp.float32) + r3_ref[...].astype(jnp.float32)
    low = jnp.concatenate([total[:, :rank], total[: seqs * kept - half, rank:]], axis=0)
    low = low * scale_ref[:, :rank]
    copies = []
    for seq in range(seqs):
        rows = slice(seq * kept, (seq + 1) * kept)
        adapter = jnp.dot(low[rows].astype(jnp.bfloat16), a_ref[...], preferred_element_type=jnp.float32)
        value = jnp.concatenate([base_ref[seq, :MIN_PROMPT], base_ref[seq, MIN_PROMPT:] + adapter], axis=0)
        stage_ref[seq] = value.astype(jnp.bfloat16)
        copy = pltpu.make_async_copy(stage_ref.at[seq], out_ref.at[seq], sems.at[seq])
        copy.start()
        copies.append(copy)
    for copy in copies:
        copy.wait()


def final(mine, received, a, base, scale):
    return pl.pallas_call(
        final_kernel,
        in_specs=[VMEM] * 7,
        out_specs=HBM,
        out_shape=jax.ShapeDtypeStruct(base.shape, jnp.bfloat16),
        scratch_shapes=[pltpu.VMEM(base.shape, jnp.bfloat16), pltpu.SemaphoreType.DMA((base.shape[0],))],
        compiler_params=pltpu.CompilerParams(vmem_limit_bytes=20 * MIB),
        name="final",
    )(mine, *received, a, base, scale)


def local(x, mask_bits, prompt_len, weight, norm_gain, mask_embed, grads, factors, first_moment, second_moment):
    width = x.shape[2]
    cols = weight.shape[1]
    rank = factors.shape[1]
    wide, narrow = jnp.float32, jnp.bfloat16

    gain = norm_gain.reshape(1, width)
    embed = f32(mask_embed).reshape(1, width)

    total, outgoing = pack(grads)
    from_core = exchange(outgoing, "c", (1,))
    total = total + f32(from_core)
    sent = bf16(total)
    from_y = [exchange(sent, "y", (k,)) for k in (1, 2, 3)]
    (acc, sq, mask, own_mine, own_other, xs, gain), at_z = main_head(
        prompt_len.reshape(1, -1), mask_bits, gain, embed, x, weight, from_core, (0, 1), (2, 3)
    )
    half = total.shape
    total, sent = small_call(gather_sum_kernel, [(half, wide), (half, narrow)], "sum_y", total, *from_y, (sq,))
    from_z = exchange(sent, ("zh",), (1,))
    (acc, sq), ahead, params = main_next(
        mask, gain, embed, x, weight, from_y[0], acc, sq, at_z, (2, 3), (4, 5),
        (factors, first_moment, second_moment),
    )

    a_own, b_own, rows_own, _ = small_call(
        update_kernel,
        [((rank, cols // 2), narrow), ((rank, cols // 2), narrow), ((2, 8, cols // 2), wide), (half, wide)],
        "update", total, from_z, *params[:3], (sq,),
    )
    b_other = exchange(b_own, "c", (1,))
    low = low_rank(own_mine, own_other, b_own, b_other)
    from_zl = exchange(low, ("zl",), (1,))
    (acc, sq), more, _ = main_next(mask, gain, embed, x, weight, b_other, acc, sq, ahead[:2], (4,), (6, 7))
    a_own, rows_own, _ = lax.optimization_barrier((a_own, rows_own, low))
    a_other = exchange(a_own, "c", (1,))
    rows_other = exchange(rows_own, "c", (1,))
    (low,) = small_call(add_kernel, [(low.shape, narrow)], "sum_zl", low, from_zl, (sq,))
    from_x = [exchange(low, ("x",), (k,)) for k in (1, 2, 3)]
    base, scale, a_full, out_first, out_second = main_last(
        mask, gain, embed, from_zl, acc, sq, xs, a_own, a_other, (rows_own, rows_other, *params[3:]),
        (*ahead[2:], *more), (5, 6, 7),
    )
    out = final(low, from_x, a_full, base, scale)
    return out, out_first, out_second


def solution(mesh):
    split = Mesh(mesh.devices.reshape(2, 4, 2, 4, 2), ("zh", "y", "c", "x", "zl"))
    placed = (
        P(DP, None, None),
        P(DP, None),
        P(DP),
        P(None, TENSOR),
        P(),
        P(),
        P(DP, None, None, TENSOR),
        P(None, None, TENSOR),
        P(None, None, TENSOR),
        P(None, None, TENSOR),
    )
    return jax.shard_map(
        local,
        mesh=split,
        in_specs=placed,
        out_specs=(P(DP, None, TENSOR), P(None, DP, TENSOR), P(None, DP, TENSOR)),
        check_vma=False,
    )
```

time: 54.5 us -> 40.1 us (0.74)
  local copies, waits for them, and re-layouts: 10.9 us -> 0 us
  waiting for transfers between devices: 5.28 us -> 3.06 us
  other arithmetic: 2.8 us -> 0.76 us
  Pallas kernels: 19 us -> 20.8 us
  starting transfers between devices: 15.3 us -> 14.3 us
    unnamed x30 -> x0, local copies, waits for them, and re-layouts: 9.86 us -> none
    pallas_call x5 -> x9, Pallas kernels: 8.89 us -> 15.1 us  [the longest x2 6.04 us: main_next(): pl.pallas_call(functools.partial(next_kernel, units, following, bool(para...]
    pallas_call x1, Pallas kernels: 10.1 us -> 5.69 us  [main_head(): pl.pallas_call(functools.partial(head_kernel, units, following), in_specs...]
    ppermute x12, waiting for transfers between devices: 5.28 us -> 3.06 us  [exchange(): return lax.ppermute(v, tuple(axes), pairs)]
    convert_element_type x4 -> x1, other arithmetic: 1.31 us -> 0.04 us  [bf16(): return v.astype(jnp.bfloat16)]
    ppermute x12, starting transfers between devices: 15.3 us -> 14.3 us  [exchange(): return lax.ppermute(v, tuple(axes), pairs)]
    convert_element_type x1 -> x0, local copies, waits for them, and re-layouts: 0.97 us -> none  [bf16(): return v.astype(jnp.bfloat16)]
    add x1 -> x0, other arithmetic: 0.66 us -> none  [adam_update(): beta_two * second_moment + (1.0 - beta_two) * summed_grad * summed_grad]
  transfers between devices with their start and end apart: 12 -> 12, of which waited for: 5 -> 3; matrix products, arithmetic and copies ran while one was open for 3% -> 2% of each run, Pallas kernels for 31% -> 43%
where the time goes in v3:
time: 40.1 us; the launch traced here: 39.9 us
  Pallas kernels  20.8 us (52%)
  starting transfers between devices  14.3 us (36%)
  waiting for transfers between devices  3.06 us (8%)
  between operations  0.92 us (2%)
  other arithmetic  0.76 us (2%)
    ppermute x12, starting transfers between devices, exchange(): return lax.ppermute(v, tuple(axes), pairs)  14.3 us
    pallas_call x2, Pallas kernels, main_next(): pl.pallas_call(functools.partial(next_kernel, units, following, bool(para...  6.04 us
    pallas_call x1, Pallas kernels, main_head(): pl.pallas_call(functools.partial(head_kernel, units, following), in_specs...  5.69 us
    pallas_call x1, Pallas kernels, main_last(): pl.pallas_call(functools.partial(last_kernel, units), in_specs=[VMEM, VME...  5.35 us
    ppermute x12, waiting for transfers between devices, exchange(): return lax.ppermute(v, tuple(axes), pairs)  3.06 us
    pallas_call x1, Pallas kernels, final(): pl.pallas_call(final_kernel, in_specs=[VMEM] * 7, out_specs=HBM, out_shap...  1.27 us
    pallas_call x1, Pallas kernels, pack(): pl.pallas_call(pack_kernel, in_specs=[HBM], out_specs=[VMEM, VMEM], out_s...  1.06 us
    pallas_call x3, Pallas kernels, small_call(): pl.pallas_call(kernel, in_specs=in_specs, out_specs=[VMEM] * len(shapes),...  0.93 us
  transfers between devices with their start and end apart: 12, of which 3 were waited for; matrix products, arithmetic and copies ran while one was open for 2% of the time, Pallas kernels for 43%

profile of v3, /device:TPU:0, one launch (start us, length us, event | category | flops | bytes accessed | tf_op | source)
XLA Modules:
  0.0 39.9 jit_solution(8828767161758839751)
XLA Ops:
  0.6 1.1 %pack.1 = (f32[2,64,512]{2,1,0:T(8,128)S(1)}, bf16[2,64,512]{2,1,0:T(8,128)(2,1)S(1)}) custom-call(f32[1,2,64,1024]{3,2,1,0:T(8,128)} %grad_ref.1), custom_call_target="tpu_custom_call" | custom-call | tf_op jit(solution)/shard_map/pack/pallas_call | solution.py:127
  1.7 0.1 collective-permute-start
  1.8 0.7 %reshape.21 = f32[8192]{0:T(1024)S(1)} convert(bf16[8192]{0:T(1024)(128)(2,1)} %param.15) | non-fusion elementwise | flops 8192 | bytes 49152 | tf_op jit(solution)/shard_map/reshape | solution.py:487
  2.5 0.6 %collective-permute-done.refs_6_ = bf16[2,64,512]{2,1,0:T(8,128)(2,1)S(1)} collective-permute-done((bf16[2,64,512]{2,1,0:T(8,128)(2,1)S(1)}, bf16[2,64,512]{2,1,0:T(8,128)(2,1)S(1)}, u32[]{:S(2)}, u32[]{:S(2)}) %collective-permute-start) | collective-permute-done | bytes 131104 | tf_op jit(solution)/shard_map/ppermute | solution.py:41
  3.2 3.2 %collective-permute-start.3 = (bf16[2,64,512]{2,1,0:T(8,128)(2,1)S(1)}, bf16[2,64,512]{2,1,0:T(8,128)(2,1)S(1)}, u32[]{:S(2)}, u32[]{:S(2)}) collective-permute-start(bf16[2,64,512]{2,1,0:T(8,128)(2,1)S(1)} %get-tuple-element.87), channel_id=1, source_target_pairs={{0,48},{16,32},{32,16},{48,0},{1,49},{17,33},{33,17},{49,1},{2,50}... | collective-permute-start | bytes 393224 | tf_op jit(solution)/shard_map/ppermute | solution.py:41
  6.3 0.6 %collective-permute-start.2 = (bf16[2,64,512]{2,1,0:T(8,128)(2,1)S(1)}, bf16[2,64,512]{2,1,0:T(8,128)(2,1)S(1)}, u32[]{:S(2)}, u32[]{:S(2)}) collective-permute-start(bf16[2,64,512]{2,1,0:T(8,128)(2,1)S(1)} %get-tuple-element.87), channel_id=1, source_target_pairs={{0,32},{16,48},{32,0},{48,16},{1,33},{17,49},{33,1},{49,17},{2,34}... | collective-permute-start | bytes 393224 | tf_op jit(solution)/shard_map/ppermute | solution.py:41
  7.0 0.4 collective-permute-start.1
  7.3 5.7 %main_head.1 = (f32[504,1024]{1,0:T(8,128)S(1)}, f32[504,128]{1,0:T(8,128)S(1)}, f32[3,168,128]{2,1,0:T(8,128)S(1)}, bf16[504,512]{1,0:T(8,128)(2,1)S(1)}, bf16[...) custom-call(s32[1,3]{1,0:T(1,128)} %bitcast.8, ...), custom_call_target="tpu_custom_call" | custom-call | flops 2113929216 | bytes 6258688 | tf_op jit(solution)/shard_map/main_head/pallas_call | solution.py:322
  13.0 0.0 collective-permute-done.3.r3_ref
  13.1 1.2 %collective-permute-done.2.r2_ref = bf16[2,64,512]{2,1,0:T(8,128)(2,1)S(1)} collective-permute-done((bf16[2,64,512]{2,1,0:T(8,128)(2,1)S(1)}, bf16[2,64,512]{2,1,0:T(8,128)(2,1)S(1)}, u32[]{:S(2)}, u32[]{:S(2)}) %collective-permute-start.2) | collective-permute-done | bytes 131104 | tf_op jit(solution)/shard_map/ppermute | solution.py:41
  14.2 0.0 collective-permute-done.1.r1_ref.refs_5_
  14.2 0.1 sum_y.1
  14.3 4.0 %collective-permute-start.4 = (bf16[2,64,512]{2,1,0:T(8,128)(2,1)S(1)}, bf16[2,64,512]{2,1,0:T(8,128)(2,1)S(1)}, u32[]{:S(2)}, u32[]{:S(2)}) collective-permute-start(bf16[2,64,512]{2,1,0:T(8,128)(2,1)S(1)} %get-tuple-element.51), channel_id=1, source_target_pairs={{0,64},{64,0},{1,65},{65,1},{2,66},{66,2},{3,67},{67,3},{4,68},{68... | collective-permute-start | bytes 393224 | tf_op jit(solution)/shard_map/ppermute | solution.py:41
  18.3 3.2 %main_next.2 = (f32[504,1024]{1,0:T(8,128)S(1)}, f32[504,128]{1,0:T(8,128)S(1)}, bf16[3,176,1024]{2,1,0:T(8,128)(2,1)S(1)}, bf16[1024,1024]{1,0:T(8,128)(2,1)S(1...) custom-call(f32[3,168,128]{2,1,0:T(8,128)S(1)} %get-tuple-element.52, ...), custom_call_target="tpu_custom_call", output_to_operand_aliasing={{0}: (6, {}), {1}: (7, {})} | custom-call | flops 2113929216 | bytes 6258688 | tf_op jit(solution)/shard_map/main_next/pallas_call | solution.py:349
  21.5 0.0 collective-permute-done.4.theirs_ref
  21.5 0.8 %update.1 = (bf16[64,512]{1,0:T(8,128)(2,1)S(1)}, bf16[64,512]{1,0:T(8,128)(2,1)S(1)}, f32[2,8,512]{2,1,0:T(8,128)S(1)}, f32[2,64,512]{2,1,0:T(8,128)}) custom-call(f32[2,64,512]{2,1,0:T(8,128)S(1)} %get-tuple-element.50.total_ref, bf16[2,64,512]{2,1,0:T(8,128)(2,1)S(1)} %collective-permute-done.4.theirs_ref, ...), custom_call_target="tpu_custom_call" | custom-call | tf_op jit(solution)/shard_map/update/pallas_call | solution.py:298
  22.3 0.0 collective-permute-start.5
  22.3 1.3 %collective-permute-done.5.other_ref.refs_5_ = bf16[64,512]{1,0:T(8,128)(2,1)S(1)} collective-permute-done((bf16[64,512]{1,0:T(8,128)(2,1)S(1)}, bf16[64,512]{1,0:T(8,128)(2,1)S(1)}, u32[]{:S(2)}, u32[]{:S(2)}) %collective-permute-start.5) | collective-permute-done | bytes 65568 | tf_op jit(solution)/shard_map/ppermute | solution.py:41
  23.6 0.5 %low_rank.1.mine_ref = bf16[256,128]{1,0:T(8,128)(2,1)S(1)} custom-call(bf16[504,512]{1,0:T(8,128)(2,1)S(1)} %get-tuple-element.46.own_mine_ref, bf16[504,512]{1,0:T(8,128)(2,1)S(1)} %get-tuple-element.47.own_other_ref, bf16[64,512]{1,0:T(8,128)(2,1)S(1)} %get-tuple-element.63.mine_ref, bf16[64,512]{1,0:T(8,128)(2,1)S(1)} %collective-permute-done.5.other_ref.refs_5_), custom_call_target="tpu_custom_call" | custom-call | tf_op jit(solution)/shard_map/low_rank/pallas_call | solution.py:436
  24.0 1.4 %collective-permute-start.6 = (bf16[256,128]{1,0:T(8,128)(2,1)S(1)}, bf16[256,128]{1,0:T(8,128)(2,1)S(1)}, u32[]{:S(2)}, u32[]{:S(2)}) collective-permute-start(bf16[256,128]{1,0:T(8,128)(2,1)S(1)} %low_rank.1.mine_ref), channel_id=1, source_target_pairs={{0,1},{1,0},{2,3},{3,2},{4,5},{5,4},{6,7},{7,6},{8,9},{9,8},{10,11... | collective-permute-start | bytes 196616 | tf_op jit(solution)/shard_map/ppermute | solution.py:41
  25.4 0.0 collective-permute-start.11
  25.4 0.5 %collective-permute-start.10 = (bf16[64,512]{1,0:T(8,128)(2,1)S(1)}, bf16[64,512]{1,0:T(8,128)(2,1)S(1)}, u32[]{:S(2)}, u32[]{:S(2)}) collective-permute-start(bf16[64,512]{1,0:T(8,128)(2,1)S(1)} %get-tuple-element.72.refs_7_), channel_id=1, source_target_pairs={{0,8},{8,0},{1,9},{9,1},{2,10},{10,2},{3,11},{11,3},{4,12},{12,4},... | collective-permute-start | bytes 196616 | tf_op jit(solution)/shard_map/ppermute | solution.py:41
  25.9 2.9 %main_next.3 = (f32[504,1024]{1,0:T(8,128)S(1)}, f32[504,128]{1,0:T(8,128)S(1)}, bf16[3,176,1024]{2,1,0:T(8,128)(2,1)S(1)}, bf16[1024,1024]{1,0:T(8,128)(2,1)S(1...) custom-call(f32[3,168,128]{2,1,0:T(8,128)S(1)} %get-tuple-element.52, ...), custom_call_target="tpu_custom_call", output_to_operand_aliasing={{0}: (6, {}), {1}: (7, {})} | custom-call | flops 1056964608 | bytes 3129344 | tf_op jit(solution)/shard_map/main_next/pallas_call | solution.py:349
  28.8 2.8 %collective-permute-start.9 = (bf16[256,128]{1,0:T(8,128)(2,1)S(1)}, bf16[256,128]{1,0:T(8,128)(2,1)S(1)}, u32[]{:S(2)}, u32[]{:S(2)}) collective-permute-start(bf16[256,128]{1,0:T(8,128)(2,1)S(1)} %sum_zl.1.mine_ref), channel_id=1, source_target_pairs={{0,6},{2,4},{4,2},{6,0},{1,7},{3,5},{5,3},{7,1},{8,14},{10,12},{12... | collective-permute-start | bytes 196616 | tf_op jit(solution)/shard_map/ppermute | solution.py:41
  31.7 0.8 %collective-permute-start.8 = (bf16[256,128]{1,0:T(8,128)(2,1)S(1)}, bf16[256,128]{1,0:T(8,128)(2,1)S(1)}, u32[]{:S(2)}, u32[]{:S(2)}) collective-permute-start(bf16[256,128]{1,0:T(8,128)(2,1)S(1)} %sum_zl.1.mine_ref), channel_id=1, source_target_pairs={{0,4},{2,6},{4,0},{6,2},{1,5},{3,7},{5,1},{7,3},{8,12},{10,14},{12... | collective-permute-start | bytes 196616 | tf_op jit(solution)/shard_map/ppermute | solution.py:41
  32.5 0.5 %collective-permute-start.7 = (bf16[256,128]{1,0:T(8,128)(2,1)S(1)}, bf16[256,128]{1,0:T(8,128)(2,1)S(1)}, u32[]{:S(2)}, u32[]{:S(2)}) collective-permute-start(bf16[256,128]{1,0:T(8,128)(2,1)S(1)} %sum_zl.1.mine_ref), channel_id=1, source_target_pairs={{0,2},{2,0},{4,6},{6,4},{1,3},{3,1},{5,7},{7,5},{8,10},{10,8},{12,... | collective-permute-start | bytes 196616 | tf_op jit(solution)/shard_map/ppermute | solution.py:41
  33.0 0.0 collective-permute-done.11.refs_10_
  33.0 0.0 collective-permute-done.10.refs_8_
  33.0 5.3 %main_last.1 = (f32[504,1024]{1,0:T(8,128)S(1)}, f32[504,128]{1,0:T(8,128)S(1)}, f32[3,192,1024]{2,1,0:T(8,128)S(1)}, f32[504,128]{1,0:T(8,128)S(1)}, bf16[64,10...) custom-call(f32[3,168,128]{2,1,0:T(8,128)S(1)} %get-tuple-element.52, ...), custom_call_target="tpu_custom_call", output_to_operand_aliasing={{0}: (4, {}), {1}: (5, {})} | custom-call | flops 3170893824 | bytes 9388032 | tf_op jit(solution)/shard_map/main_last/pallas_call | solution.py:382
  38.4 0.0 collective-permute-done.9.r3_ref
  38.4 0.0 collective-permute-done.8.r2_ref
  38.4 1.3 %final.1 = bf16[3,192,1024]{2,1,0:T(8,128)(2,1)} custom-call(bf16[256,128]{1,0:T(8,128)(2,1)S(1)} %sum_zl.1.mine_ref, bf16[256,128]{1,0:T(8,128)(2,1)S(1)} %collective-permute-done.7.r1_ref, bf16[256,128]{1,0:T(8,128)(2,1)S(1)} %collective-permute-done.8.r2_ref, bf16[256,128]{1,0:T(8,128)(2,1)S(1)} %collective-permute-done.9.r3_ref, ...), custom_call_target="tpu_custom_call" | custom-call | tf_op jit(solution)/shard_map/final/pallas_call | solution.py:469
  (4 shorter events, 0.1 us)
Async XLA Ops:
  1.7 1.4 %collective-permute-start = (bf16[2,64,512]{2,1,0:T(8,128)(2,1)S(1)}, bf16[2,64,512]{2,1,0:T(8,128)(2,1)S(1)}, u32[]{:S(2)}, u32[]{:S(2)}) collective-permute-start(bf16[2,64,512]{2,1,0:T(8,128)(2,1)S(1)} %get-tuple-element.45), channel_id=1, source_target_pairs={{0,8},{8,0},{1,9},{9,1},{2,10},{10,2},{3,11},{11,3},{4,12},{12,4},... | collective-permute-start | bytes 393224 | tf_op jit(solution)/shard_map/ppermute | solution.py:41
  3.2 9.9 %collective-permute-start.3 = (bf16[2,64,512]{2,1,0:T(8,128)(2,1)S(1)}, bf16[2,64,512]{2,1,0:T(8,128)(2,1)S(1)}, u32[]{:S(2)}, u32[]{:S(2)}) collective-permute-start(bf16[2,64,512]{2,1,0:T(8,128)(2,1)S(1)} %get-tuple-element.87), channel_id=1, source_target_pairs={{0,48},{16,32},{32,16},{48,0},{1,49},{17,33},{33,17},{49,1},{2,50}... | collective-permute-start | bytes 393224 | tf_op jit(solution)/shard_map/ppermute | solution.py:41
  6.3 7.9 %collective-permute-start.2 = (bf16[2,64,512]{2,1,0:T(8,128)(2,1)S(1)}, bf16[2,64,512]{2,1,0:T(8,128)(2,1)S(1)}, u32[]{:S(2)}, u32[]{:S(2)}) collective-permute-start(bf16[2,64,512]{2,1,0:T(8,128)(2,1)S(1)} %get-tuple-element.87), channel_id=1, source_target_pairs={{0,32},{16,48},{32,0},{48,16},{1,33},{17,49},{33,1},{49,17},{2,34}... | collective-permute-start | bytes 393224 | tf_op jit(solution)/shard_map/ppermute | solution.py:41
  7.0 7.3 %collective-permute-start.1 = (bf16[2,64,512]{2,1,0:T(8,128)(2,1)S(1)}, bf16[2,64,512]{2,1,0:T(8,128)(2,1)S(1)}, u32[]{:S(2)}, u32[]{:S(2)}) collective-permute-start(bf16[2,64,512]{2,1,0:T(8,128)(2,1)S(1)} %get-tuple-element.87), channel_id=1, source_target_pairs={{0,16},{16,0},{32,48},{48,32},{1,17},{17,1},{33,49},{49,33},{2,18}... | collective-permute-start | bytes 393224 | tf_op jit(solution)/shard_map/ppermute | solution.py:41
  14.3 7.2 %collective-permute-start.4 = (bf16[2,64,512]{2,1,0:T(8,128)(2,1)S(1)}, bf16[2,64,512]{2,1,0:T(8,128)(2,1)S(1)}, u32[]{:S(2)}, u32[]{:S(2)}) collective-permute-start(bf16[2,64,512]{2,1,0:T(8,128)(2,1)S(1)} %get-tuple-element.51), channel_id=1, source_target_pairs={{0,64},{64,0},{1,65},{65,1},{2,66},{66,2},{3,67},{67,3},{4,68},{68... | collective-permute-start | bytes 393224 | tf_op jit(solution)/shard_map/ppermute | solution.py:41
  22.3 1.3 %collective-permute-start.5 = (bf16[64,512]{1,0:T(8,128)(2,1)S(1)}, bf16[64,512]{1,0:T(8,128)(2,1)S(1)}, u32[]{:S(2)}, u32[]{:S(2)}) collective-permute-start(bf16[64,512]{1,0:T(8,128)(2,1)S(1)} %get-tuple-element.63.mine_ref), channel_id=1, source_target_pairs={{0,8},{8,0},{1,9},{9,1},{2,10},{10,2},{3,11},{11,3},{4,12},{12,4},... | collective-permute-start | bytes 196616 | tf_op jit(solution)/shard_map/ppermute | solution.py:41
  24.0 4.8 %collective-permute-start.6 = (bf16[256,128]{1,0:T(8,128)(2,1)S(1)}, bf16[256,128]{1,0:T(8,128)(2,1)S(1)}, u32[]{:S(2)}, u32[]{:S(2)}) collective-permute-start(bf16[256,128]{1,0:T(8,128)(2,1)S(1)} %low_rank.1.mine_ref), channel_id=1, source_target_pairs={{0,1},{1,0},{2,3},{3,2},{4,5},{5,4},{6,7},{7,6},{8,9},{9,8},{10,11... | collective-permute-start | bytes 196616 | tf_op jit(solution)/shard_map/ppermute | solution.py:41
  25.4 7.6 %collective-permute-start.11 = (f32[2,8,512]{2,1,0:T(8,128)S(1)}, f32[2,8,512]{2,1,0:T(8,128)S(1)}, u32[]{:S(2)}, u32[]{:S(2)}) collective-permute-start(f32[2,8,512]{2,1,0:T(8,128)S(1)} %get-tuple-element.73.refs_9_), channel_id=1, source_target_pairs={{0,8},{8,0},{1,9},{9,1},{2,10},{10,2},{3,11},{11,3},{4,12},{12,4},... | collective-permute-start | bytes 98312 | tf_op jit(solution)/shard_map/ppermute | solution.py:41
  25.4 7.6 %collective-permute-start.10 = (bf16[64,512]{1,0:T(8,128)(2,1)S(1)}, bf16[64,512]{1,0:T(8,128)(2,1)S(1)}, u32[]{:S(2)}, u32[]{:S(2)}) collective-permute-start(bf16[64,512]{1,0:T(8,128)(2,1)S(1)} %get-tuple-element.72.refs_7_), channel_id=1, source_target_pairs={{0,8},{8,0},{1,9},{9,1},{2,10},{10,2},{3,11},{11,3},{4,12},{12,4},... | collective-permute-start | bytes 196616 | tf_op jit(solution)/shard_map/ppermute | solution.py:41
  28.8 9.5 %collective-permute-start.9 = (bf16[256,128]{1,0:T(8,128)(2,1)S(1)}, bf16[256,128]{1,0:T(8,128)(2,1)S(1)}, u32[]{:S(2)}, u32[]{:S(2)}) collective-permute-start(bf16[256,128]{1,0:T(8,128)(2,1)S(1)} %sum_zl.1.mine_ref), channel_id=1, source_target_pairs={{0,6},{2,4},{4,2},{6,0},{1,7},{3,5},{5,3},{7,1},{8,14},{10,12},{12... | collective-permute-start | bytes 196616 | tf_op jit(solution)/shard_map/ppermute | solution.py:41
  31.7 6.7 %collective-permute-start.8 = (bf16[256,128]{1,0:T(8,128)(2,1)S(1)}, bf16[256,128]{1,0:T(8,128)(2,1)S(1)}, u32[]{:S(2)}, u32[]{:S(2)}) collective-permute-start(bf16[256,128]{1,0:T(8,128)(2,1)S(1)} %sum_zl.1.mine_ref), channel_id=1, source_target_pairs={{0,4},{2,6},{4,0},{6,2},{1,5},{3,7},{5,1},{7,3},{8,12},{10,14},{12... | collective-permute-start | bytes 196616 | tf_op jit(solution)/shard_map/ppermute | solution.py:41
  32.5 5.9 %collective-permute-start.7 = (bf16[256,128]{1,0:T(8,128)(2,1)S(1)}, bf16[256,128]{1,0:T(8,128)(2,1)S(1)}, u32[]{:S(2)}, u32[]{:S(2)}) collective-permute-start(bf16[256,128]{1,0:T(8,128)(2,1)S(1)} %sum_zl.1.mine_ref), channel_id=1, source_target_pairs={{0,2},{2,0},{4,6},{6,4},{1,3},{3,1},{5,7},{7,5},{8,10},{10,8},{12,... | collective-permute-start | bytes 196616 | tf_op jit(solution)/shard_map/ppermute | solution.py:41

commit v4 on v0

v4 whole, which is shorter than its diff:
```python
import functools
import itertools

import jax
import jax.numpy as jnp
from jax import lax
from jax.experimental import pallas as pl
from jax.experimental.pallas import tpu as pltpu
from jax.sharding import Mesh, PartitionSpec as P

beta_one = 0.9
beta_two = 0.999
learn_rate = 0.03
adam_count = 100
epsilon = 1e-08
adapter_scale = 2.0
norm_epsilon = 1e-05

SIZES = {"zh": 2, "y": 4, "c": 2, "x": 4, "zl": 2}
DP = ("zh", "y", "c")
TENSOR = ("x", "zl")
CUTS = ((0, 1024, 2048, 3072), (3072, 4096, 5120), (5120, 6144), (6144, 7168, 8192))
FEATURES = 8192
MIN_PROMPT = 24
SKIP = 16
PIECE = 96
MIB = 1 << 20


def f32(v):
    return v.astype(jnp.float32)


def bf16(v):
    return v.astype(jnp.bfloat16)


def exchange(v, axes, key):
    ids = list(itertools.product(*[range(SIZES[a]) for a in axes]))
    index = {t: i for i, t in enumerate(ids)}
    pairs = [(index[t], index[tuple(a ^ k for a, k in zip(t, key))]) for t in ids]
    return lax.ppermute(v, tuple(axes), pairs)


def adam_update(summed_grad, first_moment, second_moment):
    new_first = beta_one * first_moment + (1.0 - beta_one) * summed_grad
    new_second = beta_two * second_moment + (1.0 - beta_two) * summed_grad * summed_grad
    return new_first, new_second


def factor_update(new_first, new_second, param_rows):
    step_size = learn_rate / (1.0 - beta_one**adam_count)
    divisor = jnp.sqrt(new_second / (1.0 - beta_two**adam_count)) + epsilon
    return param_rows - step_size * new_first / divisor


def normalise(x_ref, mask_ref, gain_ref, embed_ref, k0, normed_ref, sq_ref, first):
    seqs, kept, _ = mask_ref.shape
    for seq in range(seqs):
        rows = slice(seq * kept, (seq + 1) * kept)
        squares = None if first else sq_ref[rows]
        for j in range(normed_ref.shape[1] // 128):
            block = k0 // 128 + j
            states = x_ref[seq, SKIP:, k0 + j * 128 : k0 + (j + 1) * 128].astype(jnp.float32)[MIN_PROMPT - SKIP :]
            hidden = jnp.where(mask_ref[seq] > 1.5, embed_ref[block : block + 1], states)
            squares = hidden * hidden if squares is None else squares + hidden * hidden
            normed_ref[rows, j * 128 : (j + 1) * 128] = (hidden * gain_ref[block : block + 1]).astype(jnp.bfloat16)
        sq_ref[rows] = squares


def multiply(cuts, x_ref, w_ref, mask_ref, gain_ref, embed_ref, acc_ref, sq_ref, normed, begun=None):
    def block(i):
        if i == 0 and begun is not None:
            return begun
        return normed[i % 2].at[:, : cuts[i + 1] - cuts[i]]

    def ready(i):
        normalise(x_ref, mask_ref, gain_ref, embed_ref, cuts[i], block(i), sq_ref, False)

    count = len(cuts) - 1
    if begun is None:
        ready(0)
    for i in range(count):
        if i + 1 < count:
            ready(i + 1)
        product = jnp.dot(block(i)[...], w_ref[cuts[i] : cuts[i + 1]], preferred_element_type=jnp.float32)
        if i == 0 and begun is not None:
            acc_ref[...] = product
        else:
            acc_ref[...] += product


def start(copies):
    for copy in copies:
        copy.start()


def wait(copies):
    for copy in copies:
        copy.wait()


def tensor_index():
    return lax.axis_index("x") * 2 + lax.axis_index("zl")


def pack_kernel(grad_ref, own_ref, other_ref, wide_ref, sems):
    width = own_ref.shape[2]
    core = lax.axis_index("c")
    near = pl.ds(pl.multiple_of(core * width, width), width)
    far = pl.ds(pl.multiple_of((1 - core) * width, width), width)
    other = pltpu.make_async_copy(grad_ref.at[0, :, :, far], wide_ref, sems.at[0])
    own = pltpu.make_async_copy(grad_ref.at[0, :, :, near], own_ref, sems.at[1])
    other.start()
    own.start()
    other.wait()
    other_ref[...] = wide_ref[...].astype(jnp.bfloat16)
    own.wait()


def pack(grads):
    _, two, rank, cols = grads.shape
    shape = (two, rank, cols // 2)
    return pl.pallas_call(
        pack_kernel,
        in_specs=[HBM],
        out_specs=[VMEM, VMEM],
        out_shape=[jax.ShapeDtypeStruct(shape, jnp.float32), jax.ShapeDtypeStruct(shape, jnp.bfloat16)],
        scratch_shapes=[pltpu.VMEM(shape, jnp.float32), pltpu.SemaphoreType.DMA((2,))],
        compiler_params=pltpu.CompilerParams(vmem_limit_bytes=8 * MIB),
        cost_estimate=pl.CostEstimate(flops=20_000_000_000, bytes_accessed=80_000_000, transcendentals=0),
        name="pack",
    )(in_hbm(grads))


def prepare_kernel(
    first_block, prompt_ref, bits_ref, gain_ref, embed_ref, x_ref, _, mask_ref, mine_ref, other_ref, embed_out, sq_ref,
    normed_ref,
):
    seqs, kept, _ = mask_ref.shape
    width = mine_ref.shape[1]
    col = pl.multiple_of(tensor_index() * 2 * width, 2 * width)
    core = lax.axis_index("c")
    embed_out[...] = embed_ref[...].astype(jnp.float32)
    length = bits_ref.shape[1]
    here = lax.broadcasted_iota(jnp.int32, (kept, length), 0) + MIN_PROMPT
    there = lax.broadcasted_iota(jnp.int32, (kept, length), 1)
    position = lax.broadcasted_iota(jnp.int32, (kept, 1), 0) + MIN_PROMPT
    for seq in range(seqs):
        bits = jnp.where(here == there, bits_ref[seq : seq + 1, :], 0)
        chosen = 1.0 + jnp.sum((bits == 1).astype(jnp.float32), axis=1, keepdims=True)
        column = jnp.where(position >= prompt_ref[0:1, seq : seq + 1], chosen, 0.0)
        mask_ref[seq] = jnp.broadcast_to(column, (kept, 128))

    for at_core, dst in ((core, mine_ref), (1 - core, other_ref)):
        for seq in range(seqs):
            rows = slice(seq * kept, (seq + 1) * kept)
            for j in range(width // 128):
                lanes = pl.multiple_of(col + at_core * width + j * 128, 128)
                block = pl.ds(lanes // 128, 1)
                states = x_ref[seq, SKIP:, pl.ds(lanes, 128)].astype(jnp.float32)[MIN_PROMPT - SKIP :]
                hidden = jnp.where(mask_ref[seq] > 1.5, embed_out[block], states)
                dst[rows, j * 128 : (j + 1) * 128] = (hidden * gain_ref[block]).astype(jnp.bfloat16)
    normalise(x_ref, mask_ref, gain_ref, embed_out, first_block, normed_ref, sq_ref, True)


def y_kernel(
    cuts, normed_in, mask_ref, gain_ref, embed_ref, x_ref, w_ref, _, sq_in, acc_ref, sq_ref, normed_a, normed_b
):
    multiply(cuts, x_ref, w_ref, mask_ref, gain_ref, embed_ref, acc_ref, sq_ref, (normed_a, normed_b), normed_in)


def chip_rows():
    return pl.ds(pl.multiple_of((lax.axis_index("zh") * 4 + lax.axis_index("y")) * 8, 8), 8)


def core_lanes(width):
    return pl.ds(pl.multiple_of(lax.axis_index("c") * width, width), width)


def part_kernel(
    cuts, mask_ref, gain_ref, embed_ref, x_ref, w_ref, _, acc_in, sq_in, acc_ref, sq_ref, normed_a, normed_b
):
    multiply(cuts, x_ref, w_ref, mask_ref, gain_ref, embed_ref, acc_ref, sq_ref, (normed_a, normed_b))


def last_kernel(
    cuts, mask_ref, gain_ref, embed_ref, x_ref, w_ref, _, acc_in, sq_in, rows_mine, rows_other, first_ref, second_ref,
    acc_ref, sq_ref, base_ref, scale_ref, first_out, second_out, normed_a, normed_b, first_buf, second_buf, sems,
):
    seqs, kept, _ = mask_ref.shape
    cols = w_ref.shape[1]
    col = pl.multiple_of(tensor_index() * cols, cols)
    even = lax.axis_index("c") == 0

    mine, other = rows_mine[...], rows_other[...]
    summed = jnp.concatenate([jnp.where(even, mine, other), jnp.where(even, other, mine)], axis=2)
    share = summed.shape[1] // 2
    first, second = adam_update(summed, first_ref[:, chip_rows()], second_ref[:, chip_rows()])
    first_buf[...] = jnp.where(even, first[:, :share], first[:, share:])
    second_buf[...] = jnp.where(even, second[:, :share], second[:, share:])
    out = [
        pltpu.make_async_copy(first_buf, first_out, sems.at[0]),
        pltpu.make_async_copy(second_buf, second_out, sems.at[1]),
    ]
    start(out)

    multiply(cuts, x_ref, w_ref, mask_ref, gain_ref, embed_ref, acc_ref, sq_ref, (normed_a, normed_b))
    for seq in range(seqs):
        rows = slice(seq * kept, (seq + 1) * kept)
        mean = jnp.sum(sq_ref[rows], axis=1, keepdims=True) * (1.0 / FEATURES)
        scale = jnp.broadcast_to(lax.rsqrt(mean + norm_epsilon), (kept, 128))
        code = mask_ref[seq]
        scale_ref[rows] = jnp.where(code > 0.5, adapter_scale * scale, 0.0)
        for j in range(cols // 128):
            lanes = slice(j * 128, (j + 1) * 128)
            at = pl.multiple_of(col + j * 128, 128)
            states = x_ref[seq, :, pl.ds(at, 128)].astype(jnp.float32)
            head, states = states[:MIN_PROMPT], states[MIN_PROMPT:]
            hidden = jnp.where(code > 1.5, embed_ref[pl.ds(at // 128, 1)], states)
            value = jnp.where(code > 0.5, hidden + scale * acc_ref[rows, lanes], states)
            base_ref[seq, :MIN_PROMPT, lanes] = head
            base_ref[seq, MIN_PROMPT:, lanes] = value
    wait(out)


VMEM = pl.BlockSpec(memory_space=pltpu.VMEM)
SMEM = pl.BlockSpec(memory_space=pltpu.SMEM)
HBM = pl.BlockSpec(memory_space=pltpu.HBM)
ANY = pl.BlockSpec(memory_space=pl.ANY)


def in_hbm(v):
    return pltpu.with_memory_space_constraint(v, pltpu.HBM)


def in_vmem(v):
    return pltpu.with_memory_space_constraint(v, pltpu.VMEM)


def cost(rows, cols, cuts):
    depth = cuts[-1] - cuts[0]
    return pl.CostEstimate(flops=2 * rows * depth * cols, bytes_accessed=4 * rows * cols, transcendentals=0)


def small_call(kernel, shapes, name, *args, scratch=()):
    in_specs = [ANY if isinstance(v, tuple) else VMEM for v in args]
    args = [v[0] if isinstance(v, tuple) else v for v in args]
    return pl.pallas_call(
        kernel,
        in_specs=in_specs,
        out_specs=[VMEM] * len(shapes),
        out_shape=[jax.ShapeDtypeStruct(*v) for v in shapes],
        scratch_shapes=[pltpu.VMEM(*v) for v in scratch],
        compiler_params=pltpu.CompilerParams(vmem_limit_bytes=4 * MIB),
        name=name,
    )(*args)


def widest(cuts):
    return max(b - a for a, b in zip(cuts, cuts[1:]))


def prepare(prompt_len, bits, gain, embed, x, token, cols, block):
    seqs, length, width = x.shape
    kept = length - MIN_PROMPT
    rows = seqs * kept
    shapes = [
        ((seqs, kept, 128), jnp.float32),
        ((rows, cols // 2), jnp.bfloat16),
        ((rows, cols // 2), jnp.bfloat16),
        (embed.shape, jnp.float32),
        ((rows, 128), jnp.float32),
        ((rows, block), jnp.bfloat16),
    ]
    return pl.pallas_call(
        functools.partial(prepare_kernel, 0),
        in_specs=[VMEM] * 5 + [ANY],
        out_specs=[VMEM] * len(shapes),
        out_shape=[jax.ShapeDtypeStruct(*s) for s in shapes],
        compiler_params=pltpu.CompilerParams(vmem_limit_bytes=8 * MIB),
        name="prepare",
    )(*[in_vmem(v) for v in (prompt_len, bits, gain, embed, x)], token)


def main_first(normed, common, token, sq, cuts):
    mask, gain, embed, x, w = common
    rows, cols = normed.shape[0], w.shape[1]
    scratch = pltpu.VMEM((rows, widest(cuts)), jnp.bfloat16)
    return pl.pallas_call(
        functools.partial(y_kernel, cuts),
        in_specs=[VMEM] * 6 + [ANY, VMEM],
        out_specs=[VMEM] * 2,
        out_shape=[jax.ShapeDtypeStruct((rows, cols), jnp.float32), jax.ShapeDtypeStruct(sq.shape, jnp.float32)],
        input_output_aliases={7: 1},
        scratch_shapes=[scratch, scratch],
        compiler_params=pltpu.CompilerParams(vmem_limit_bytes=12 * MIB),
        cost_estimate=cost(rows, cols, cuts),
        name="main_y",
    )(normed, mask, gain, embed, in_vmem(x), in_vmem(w), token, sq)


def main_part(kernel, name, cuts, common, token, state, extra, extra_specs, shapes, out_specs, scratch=()):
    mask, gain, embed, x, w = common
    rows, cols = state[0].shape
    shapes = [(state[0].shape, jnp.float32), (state[1].shape, jnp.float32), *shapes]
    normed = pltpu.VMEM((rows, widest(cuts)), jnp.bfloat16)
    out = pl.pallas_call(
        functools.partial(kernel, cuts),
        in_specs=[VMEM] * 5 + [ANY] + [VMEM] * 2 + extra_specs,
        out_specs=[VMEM] * 2 + out_specs,
        out_shape=[jax.ShapeDtypeStruct(*s) for s in shapes],
        input_output_aliases={6: 0, 7: 1},
        scratch_shapes=[normed, normed, *scratch],
        compiler_params=pltpu.CompilerParams(vmem_limit_bytes=12 * MIB),
        cost_estimate=cost(rows, cols, cuts),
        name=name,
    )(mask, gain, embed, in_vmem(x), in_vmem(w), token, *state, *extra)
    return out[:2], out[2:]


def add_kernel(mine_ref, theirs_ref, *refs):
    refs[-1][...] = (mine_ref[...].astype(jnp.float32) + theirs_ref[...].astype(jnp.float32)).astype(jnp.bfloat16)


def gather_sum_kernel(mine_ref, r1_ref, r2_ref, r3_ref, _, total_ref, sent_ref):
    total = mine_ref[...] + r1_ref[...].astype(jnp.float32)
    total += r2_ref[...].astype(jnp.float32) + r3_ref[...].astype(jnp.float32)
    total_ref[...] = total
    sent_ref[...] = total.astype(jnp.bfloat16)


def parity():
    return lax.rem(lax.axis_index("y"), 2)


def by_parity(v):
    groups = v.reshape(v.shape[0] // 16, 2, 8, v.shape[1])
    flat = (v.shape[0] // 2, v.shape[1])
    even = parity() == 0
    mine = jnp.where(even, groups[:, 0], groups[:, 1])
    others = jnp.where(even, groups[:, 1], groups[:, 0])
    return mine.reshape(flat), others.reshape(flat)


def from_parity(mine, others):
    shape = (mine.shape[0] // 8, 8, mine.shape[1])
    even = parity() == 0
    mine, others = mine.reshape(shape), others.reshape(shape)
    groups = jnp.stack([jnp.where(even, mine, others), jnp.where(even, others, mine)], axis=1)
    return groups.reshape(2 * shape[0] * 8, shape[2])


def core_sum_kernel(mine_ref, theirs_ref, total_ref, same_ref, flip_ref):
    a = mine_ref[0] + theirs_ref[0].astype(jnp.float32)
    b = mine_ref[1] + theirs_ref[1].astype(jnp.float32)
    mine, others = by_parity(a)
    total = jnp.concatenate([b, mine], axis=0)
    total_ref[...] = total
    same_ref[...] = total.astype(jnp.bfloat16)
    flip_ref[...] = jnp.concatenate([b, others], axis=0).astype(jnp.bfloat16)


def update_kernel(total_ref, theirs_ref, factors_ref, first_ref, second_ref, _, a_ref, b_ref, rows_ref, sum_ref):
    rank, width = b_ref.shape
    at = core_lanes(width)
    total = total_ref[...] + theirs_ref[...].astype(jnp.float32)
    first, second = adam_update(total[:rank], first_ref[1, :, at], second_ref[1, :, at])
    b_ref[...] = factor_update(first, second, factors_ref[1, :, at]).astype(jnp.bfloat16)
    mine = [by_parity(ref[0, :, at])[0] for ref in (factors_ref, first_ref, second_ref)]
    first, second = adam_update(total[rank:], mine[1], mine[2])
    a_ref[...] = factor_update(first, second, mine[0]).astype(jnp.bfloat16)
    sum_ref[...] = total
    group = lax.axis_index("zh") * 2 + lax.axis_index("y") // 2
    rows_ref[0] = sum_ref[pl.ds(pl.multiple_of(rank + group * 8, 8), 8)]
    rows_ref[1] = sum_ref[chip_rows()]


ROW_BY_ROW = (((1,), (1,)), ((), ()))


def low_rank_first_kernel(own_ref, mine_ref, out_ref):
    out_ref[...] = lax.dot_general(own_ref[...], mine_ref[...], ROW_BY_ROW, preferred_element_type=jnp.float32)


def low_rank_kernel(first_ref, own_ref, other_ref, out_ref):
    rows, rank = first_ref.shape
    half = out_ref.shape[0]
    prod = lax.dot_general(own_ref[...], other_ref[...], ROW_BY_ROW, preferred_element_type=jnp.float32)
    prod += first_ref[...]
    tail = jnp.concatenate([prod[half:], jnp.zeros((2 * half - rows, rank), jnp.float32)], axis=0)
    out_ref[...] = jnp.concatenate([prod[:half], tail], axis=1).astype(jnp.bfloat16)


def join_kernel(a_mine, a_core, a_y, a_y_core, _, a_ref):
    mine = from_parity(a_mine[...].astype(jnp.float32), a_y[...].astype(jnp.float32))
    other = from_parity(a_core[...].astype(jnp.float32), a_y_core[...].astype(jnp.float32))
    even = lax.axis_index("c") == 0
    joined = jnp.concatenate([jnp.where(even, mine, other), jnp.where(even, other, mine)], axis=1)
    a_ref[...] = joined.astype(jnp.bfloat16)


def final_kernel(mine_ref, r1_ref, r2_ref, r3_ref, a_ref, base_ref, scale_ref, out_ref, stage_ref, sems):
    seqs, length, _ = base_ref.shape
    kept = length - MIN_PROMPT
    rank = a_ref.shape[0]
    half = mine_ref.shape[0]
    total = mine_ref[...].astype(jnp.float32) + r1_ref[...].astype(jnp.float32)
    total += r2_ref[...].astype(jnp.float32) + r3_ref[...].astype(jnp.float32)
    low = jnp.concatenate([total[:, :rank], total[: seqs * kept - half, rank:]], axis=0)
    low = (low * scale_ref[:, :rank]).astype(jnp.bfloat16)
    a = a_ref[...]
    copies = []
    for seq in range(seqs):
        adapter = jnp.dot(low[seq * kept : (seq + 1) * kept], a, preferred_element_type=jnp.float32)
        for piece in range(length // PIECE):
            rows = slice(piece * PIECE, (piece + 1) * PIECE)
            value = base_ref[seq, rows]
            if rows.stop > MIN_PROMPT:
                lead = max(MIN_PROMPT - rows.start, 0)
                part = value[lead:] + adapter[rows.start + lead - MIN_PROMPT : rows.stop - MIN_PROMPT]
                value = jnp.concatenate([value[:lead], part], axis=0) if lead else part
            stage_ref[seq, rows] = value.astype(jnp.bfloat16)
            at = pl.ds(rows.start, PIECE)
            copy = pltpu.make_async_copy(stage_ref.at[seq, at], out_ref.at[seq, at], sems.at[seq, piece])
            copy.start()
            copies.append(copy)
    wait(copies)


def final(mine, received, a, base, scale):
    return pl.pallas_call(
        final_kernel,
        in_specs=[VMEM] * 7,
        out_specs=HBM,
        out_shape=jax.ShapeDtypeStruct(base.shape, jnp.bfloat16),
        scratch_shapes=[
            pltpu.VMEM(base.shape, jnp.bfloat16),
            pltpu.SemaphoreType.DMA((base.shape[0], base.shape[1] // PIECE)),
        ],
        compiler_params=pltpu.CompilerParams(vmem_limit_bytes=20 * MIB),
        name="final",
    )(mine, *received, a, base, scale)


def local(x, mask_bits, prompt_len, weight, norm_gain, mask_embed, grads, factors, first_moment, second_moment):
    width = x.shape[2]
    cols = weight.shape[1]
    two, rank, _ = factors.shape
    wide, narrow = jnp.float32, jnp.bfloat16
    gain = norm_gain.reshape(width // 128, 128)
    embed = mask_embed.reshape(width // 128, 128)

    own, outgoing = pack(grads)
    from_core = exchange(outgoing, "c", (1,))
    held = (rank + rank // 2, cols // 2)
    total, same, flip = small_call(
        core_sum_kernel, [(held, wide), (held, narrow), (held, narrow)], "sum_c", own, from_core
    )
    from_y = [exchange(v, "y", (k,)) for v, k in ((flip, 3), (same, 2), (flip, 1))]

    mask, own_mine, own_other, embed, sq, normed = prepare(
        prompt_len.reshape(1, -1), mask_bits, gain, embed, x, same, cols, CUTS[0][1]
    )
    common = (mask, gain, embed, x, weight)
    state = main_first(normed, common, same, sq, CUTS[0])
    total, sent = small_call(
        gather_sum_kernel, [(held, wide), (held, narrow)], "sum_y", total, *from_y, (state[1],)
    )
    from_z = exchange(sent, ("zh",), (1,))
    state, _ = main_part(part_kernel, "main_z", CUTS[1], common, sent, state, [], [], [], [])

    params = [in_vmem(v) for v in (factors, first_moment, second_moment)]
    part = (rank, cols // 2)
    half_part = (rank // 2, cols // 2)
    a_half, b_own, rows_own = small_call(
        update_kernel, [(half_part, narrow), (part, narrow), ((two, 8, cols // 2), wide)],
        "update", total, from_z, *params, (state[1],), scratch=[(held, wide)],
    )
    b_other = exchange(b_own, "c", (1,))
    rows = own_mine.shape[0]
    (low,) = small_call(low_rank_first_kernel, [((rows, rank), wide)], "low_rank_first", own_mine, b_own)
    packed = (-(-rows // 32) * 16, 2 * rank)
    (low,) = small_call(low_rank_kernel, [(packed, narrow)], "low_rank", low, own_other, b_other)
    from_zl = exchange(low, ("zl",), (1,))
    a_half, rows_own, _ = lax.optimization_barrier((a_half, rows_own, low))
    a_y = exchange(a_half, "y", (1,))
    rows_other = exchange(rows_own, "c", (1,))
    state, _ = main_part(part_kernel, "main_zl", CUTS[2], common, low, state, [], [], [], [])
    (low,) = small_call(add_kernel, [(low.shape, narrow)], "sum_zl", low, from_zl, (state[1],))
    from_x = [exchange(low, ("x",), (k,)) for k in (3, 2, 1)]
    a_half, a_y, _ = lax.optimization_barrier((a_half, a_y, low))
    a_parts = (a_half, exchange(a_half, "c", (1,)), a_y, exchange(a_y, "c", (1,)))
    four = ((two, 4, cols), wide)
    state, (base, scale, out_first, out_second) = main_part(
        last_kernel, "main_x", CUTS[3], common, low, state, [rows_own, rows_other, *params[1:]], [VMEM] * 4,
        [(x.shape[:2] + (cols,), wide), (state[1].shape, wide), four, four], [VMEM] * 2 + [HBM] * 2,
        [pltpu.VMEM(*four), pltpu.VMEM(*four), pltpu.SemaphoreType.DMA((2,))],
    )
    (a,) = small_call(join_kernel, [((rank, cols), narrow)], "join_a", *a_parts, (scale,))
    out = final(low, from_x, a, base, scale)
    return out, out_first, out_second


def solution(mesh):
    split = Mesh(mesh.devices.reshape(2, 4, 2, 4, 2), ("zh", "y", "c", "x", "zl"))
    placed = (
        P(DP, None, None),
        P(DP, None),
        P(DP),
        P(None, TENSOR),
        P(),
        P(),
        P(DP, None, None, TENSOR),
        P(None, None, TENSOR),
        P(None, None, TENSOR),
        P(None, None, TENSOR),
    )
    return jax.shard_map(
        local,
        mesh=split,
        in_specs=placed,
        out_specs=(P(DP, None, TENSOR), P(None, DP, TENSOR), P(None, DP, TENSOR)),
        check_vma=False,
    )
```

time: 258 us -> 37.6 us (0.15)
  the two profiles are of different devices: /device:TPU:0 before, /device:TPU:1 now
where the time goes in v4:
time: 37.6 us; the launch traced here: 37.5 us
  starting transfers between devices  19.1 us (51%)
  Pallas kernels  15.6 us (41%)
  waiting for transfers between devices  1.7 us (5%)
  between operations  1.03 us (3%)
    ppermute x14, starting transfers between devices, exchange(): return lax.ppermute(v, tuple(axes), pairs)  19.1 us
    pallas_call x3, Pallas kernels, main_part(): pl.pallas_call(functools.partial(kernel, cuts), in_specs=[VMEM] * 5 + [AN...  7.63 us
    pallas_call x1, Pallas kernels, main_first(): pl.pallas_call(functools.partial(y_kernel, cuts), in_specs=[VMEM] * 6 + [...  3.57 us
    ppermute x14, waiting for transfers between devices, exchange(): return lax.ppermute(v, tuple(axes), pairs)  1.7 us
    pallas_call x1, Pallas kernels, final(): pl.pallas_call(final_kernel, in_specs=[VMEM] * 7, out_specs=HBM, out_shap...  1.28 us
    pallas_call x1, Pallas kernels, pack(): pl.pallas_call(pack_kernel, in_specs=[HBM], out_specs=[VMEM, VMEM], out_s...  1.21 us
    pallas_call x7, Pallas kernels, small_call(): pl.pallas_call(kernel, in_specs=in_specs, out_specs=[VMEM] * len(shapes),...  1 us
    pallas_call x1, Pallas kernels, prepare(): pl.pallas_call(functools.partial(prepare_kernel, 0), in_specs=[VMEM] * 5...  0.92 us
  transfers between devices with their start and end apart: 14, of which 3 were waited for; matrix products, arithmetic and copies ran while one was open for 0% of the time, Pallas kernels for 33%

profile of v4, /device:TPU:1, one launch (start us, length us, event | category | flops | bytes accessed | tf_op | source)
XLA Modules:
  0.0 37.5 jit_solution(9781827588829159424)
XLA Ops:
  0.7 1.2 %pack.1 = (f32[2,64,512]{2,1,0:T(8,128)S(1)}, bf16[2,64,512]{2,1,0:T(8,128)(2,1)S(1)}) custom-call(f32[1,2,64,1024]{3,2,1,0:T(8,128)} %grad_ref.1), custom_call_target="tpu_custom_call" | custom-call | flops 20000000000 | bytes 80000000 | tf_op jit(solution)/shard_map/pack/pallas_call | solution.py:124
  1.9 1.5 %collective-permute-start = (bf16[2,64,512]{2,1,0:T(8,128)(2,1)S(1)}, bf16[2,64,512]{2,1,0:T(8,128)(2,1)S(1)}, u32[]{:S(2)}, u32[]{:S(2)}) collective-permute-start(bf16[2,64,512]{2,1,0:T(8,128)(2,1)S(1)} %get-tuple-element.34), channel_id=1, source_target_pairs={{0,8},{8,0},{1,9},{9,1},{2,10},{10,2},{3,11},{11,3},{4,12},{12,4},... | collective-permute-start | bytes 393224 | tf_op jit(solution)/shard_map/ppermute | solution.py:42
  3.4 1.0 %collective-permute-done.theirs_ref = bf16[2,64,512]{2,1,0:T(8,128)(2,1)S(1)} collective-permute-done((bf16[2,64,512]{2,1,0:T(8,128)(2,1)S(1)}, bf16[2,64,512]{2,1,0:T(8,128)(2,1)S(1)}, u32[]{:S(2)}, u32[]{:S(2)}) %collective-permute-start) | collective-permute-done | bytes 131104 | tf_op jit(solution)/shard_map/ppermute | solution.py:42
  4.4 2.9 %collective-permute-start.1 = (bf16[96,512]{1,0:T(8,128)(2,1)S(1)}, bf16[96,512]{1,0:T(8,128)(2,1)S(1)}, u32[]{:S(2)}, u32[]{:S(2)}) collective-permute-start(bf16[96,512]{1,0:T(8,128)(2,1)S(1)} %get-tuple-element.38), channel_id=1, source_target_pairs={{0,48},{16,32},{32,16},{48,0},{1,49},{17,33},{33,17},{49,1},{2,50}... | collective-permute-start | bytes 294920 | tf_op jit(solution)/shard_map/ppermute | solution.py:42
  7.3 0.0 collective-permute-start.3
  7.3 1.3 %collective-permute-start.2 = (bf16[96,512]{1,0:T(8,128)(2,1)S(1)}, bf16[96,512]{1,0:T(8,128)(2,1)S(1)}, u32[]{:S(2)}, u32[]{:S(2)}) collective-permute-start(bf16[96,512]{1,0:T(8,128)(2,1)S(1)} %get-tuple-element.35._), channel_id=1, source_target_pairs={{0,32},{16,48},{32,0},{48,16},{1,33},{17,49},{33,1},{49,17},{2,34}... | collective-permute-start | bytes 294920 | tf_op jit(solution)/shard_map/ppermute | solution.py:42
  8.6 0.9 %prepare.1 = (f32[3,168,128]{2,1,0:T(8,128)S(1)}, bf16[504,512]{1,0:T(8,128)(2,1)S(1)}, bf16[504,512]{1,0:T(8,128)(2,1)S(1)}, f32[64,128]{1,0:T(8,128)S(1)}, f32...) custom-call(s32[1,3]{1,0:T(1,128)S(1)} %bitcast.9, s32[3,192]{1,0:T(4,128)S(1)} %copy-done.7, f32[64,128]{1,0:T(8,128)S(1)} %bitcast.3, ...), custom_call_target="tpu_custom_call" | custom-call | tf_op jit(solution)/shard_map/prepare/pallas_call | solution.py:276
  9.6 0.0 copy-done
  9.6 3.6 %main_y.1 = (f32[504,1024]{1,0:T(8,128)S(1)}, f32[504,128]{1,0:T(8,128)S(1)}) custom-call(bf16[504,1024]{1,0:T(8,128)(2,1)S(1)} %get-tuple-element.39.normed_in, f32[3,168,128]{2,1,0:T(8,128)S(1)} %get-tuple-element.40.mask_ref, f32[64,128]{1,0:T(8,128)S(1)} %bitcast.4, f32[64,128]{1,0:T(8,128)S(1)} %get-tuple-element.41.embed_ref, ...), custom_call_target="tpu_custom_call", output_to_operand_aliasing={{1}: (7, {})} | custom-call | flops 3170893824 | bytes 2064384 | tf_op jit(solution)/shard_map/main_y/pallas_call | solution.py:290
  13.1 0.1 collective-permute-done.2.r2_ref
  13.2 0.0 collective-permute-done.1.r1_ref
  13.2 0.0 collective-permute-done.3.r3_ref
  13.3 4.2 %collective-permute-start.4 = (bf16[96,512]{1,0:T(8,128)(2,1)S(1)}, bf16[96,512]{1,0:T(8,128)(2,1)S(1)}, u32[]{:S(2)}, u32[]{:S(2)}) collective-permute-start(bf16[96,512]{1,0:T(8,128)(2,1)S(1)} %get-tuple-element.45._), channel_id=1, source_target_pairs={{0,64},{64,0},{1,65},{65,1},{2,66},{66,2},{3,67},{67,3},{4,68},{68... | collective-permute-start | bytes 294920 | tf_op jit(solution)/shard_map/ppermute | solution.py:42
  17.5 2.5 %main_z.1 = (f32[504,1024]{1,0:T(8,128)S(1)}, f32[504,128]{1,0:T(8,128)S(1)}) custom-call(f32[3,168,128]{2,1,0:T(8,128)S(1)} %get-tuple-element.40.mask_ref, f32[64,128]{1,0:T(8,128)S(1)} %bitcast.5, f32[64,128]{1,0:T(8,128)S(1)} %get-tuple-element.41.embed_ref, bf16[3,192,8192]{2,1,0:T(8,128)(2,1)S(1)} %copy-done.1, ...), custom_call_target="tpu_custom_call", output_to_operand_aliasing={{0}: (6, {}), {1}: (7, {})} | custom-call | flops 2113929216 | bytes 2064384 | tf_op jit(solution)/shard_map/main_z/pallas_call | solution.py:308
  20.0 0.0 collective-permute-done.4.theirs_ref
  20.0 0.2 update.1
  20.3 1.3 %collective-permute-start.5 = (bf16[64,512]{1,0:T(8,128)(2,1)S(1)}, bf16[64,512]{1,0:T(8,128)(2,1)S(1)}, u32[]{:S(2)}, u32[]{:S(2)}) collective-permute-start(bf16[64,512]{1,0:T(8,128)(2,1)S(1)} %get-tuple-element.48.mine_ref), channel_id=1, source_target_pairs={{0,8},{8,0},{1,9},{9,1},{2,10},{10,2},{3,11},{11,3},{4,12},{12,4},... | collective-permute-start | bytes 196616 | tf_op jit(solution)/shard_map/ppermute | solution.py:42
  21.6 0.3 low_rank_first.1.first_ref
  21.8 0.6 %collective-permute-done.5.other_ref = bf16[64,512]{1,0:T(8,128)(2,1)S(1)} collective-permute-done((bf16[64,512]{1,0:T(8,128)(2,1)S(1)}, bf16[64,512]{1,0:T(8,128)(2,1)S(1)}, u32[]{:S(2)}, u32[]{:S(2)}) %collective-permute-start.5) | collective-permute-done | bytes 65568 | tf_op jit(solution)/shard_map/ppermute | solution.py:42
  22.5 0.3 low_rank.1._.mine_ref
  22.8 1.2 %collective-permute-start.6 = (bf16[256,128]{1,0:T(8,128)(2,1)S(1)}, bf16[256,128]{1,0:T(8,128)(2,1)S(1)}, u32[]{:S(2)}, u32[]{:S(2)}) collective-permute-start(bf16[256,128]{1,0:T(8,128)(2,1)S(1)} %low_rank.1._.mine_ref), channel_id=1, source_target_pairs={{0,1},{1,0},{2,3},{3,2},{4,5},{5,4},{6,7},{7,6},{8,9},{9,8},{10,11... | collective-permute-start | bytes 196616 | tf_op jit(solution)/shard_map/ppermute | solution.py:42
  24.0 0.6 %collective-permute-start.13 = (f32[2,8,512]{2,1,0:T(8,128)S(1)}, f32[2,8,512]{2,1,0:T(8,128)S(1)}, u32[]{:S(2)}, u32[]{:S(2)}) collective-permute-start(f32[2,8,512]{2,1,0:T(8,128)S(1)} %get-tuple-element.58.rows_mine), channel_id=1, source_target_pairs={{0,8},{8,0},{1,9},{9,1},{2,10},{10,2},{3,11},{11,3},{4,12},{12,4},... | collective-permute-start | bytes 98312 | tf_op jit(solution)/shard_map/ppermute | solution.py:42
  24.6 1.4 %collective-permute-start.10 = (bf16[32,512]{1,0:T(8,128)(2,1)S(1)}, bf16[32,512]{1,0:T(8,128)(2,1)S(1)}, u32[]{:S(2)}, u32[]{:S(2)}) collective-permute-start(bf16[32,512]{1,0:T(8,128)(2,1)S(1)} %get-tuple-element.55.a_mine), channel_id=1, source_target_pairs={{0,16},{16,0},{32,48},{48,32},{1,17},{17,1},{33,49},{49,33},{2,18}... | collective-permute-start | bytes 98312 | tf_op jit(solution)/shard_map/ppermute | solution.py:42
  26.0 1.4 %main_zl.1 = (f32[504,1024]{1,0:T(8,128)S(1)}, f32[504,128]{1,0:T(8,128)S(1)}) custom-call(f32[3,168,128]{2,1,0:T(8,128)S(1)} %get-tuple-element.40.mask_ref, f32[64,128]{1,0:T(8,128)S(1)} %bitcast.6, f32[64,128]{1,0:T(8,128)S(1)} %get-tuple-element.41.embed_ref, bf16[3,192,8192]{2,1,0:T(8,128)(2,1)S(1)} %copy-done.1, ...), custom_call_target="tpu_custom_call", output_to_operand_aliasing={{0}: (6, {}), {1}: (7, {})} | custom-call | flops 1056964608 | bytes 2064384 | tf_op jit(solution)/shard_map/main_zl/pallas_call | solution.py:308
  27.4 2.6 %collective-permute-start.7 = (bf16[256,128]{1,0:T(8,128)(2,1)S(1)}, bf16[256,128]{1,0:T(8,128)(2,1)S(1)}, u32[]{:S(2)}, u32[]{:S(2)}) collective-permute-start(bf16[256,128]{1,0:T(8,128)(2,1)S(1)} %sum_zl.1._.mine_ref), channel_id=1, source_target_pairs={{0,6},{2,4},{4,2},{6,0},{1,7},{3,5},{5,3},{7,1},{8,14},{10,12},{12... | collective-permute-start | bytes 196616 | tf_op jit(solution)/shard_map/ppermute | solution.py:42
  30.0 0.5 %collective-permute-start.8 = (bf16[256,128]{1,0:T(8,128)(2,1)S(1)}, bf16[256,128]{1,0:T(8,128)(2,1)S(1)}, u32[]{:S(2)}, u32[]{:S(2)}) collective-permute-start(bf16[256,128]{1,0:T(8,128)(2,1)S(1)} %sum_zl.1._.mine_ref), channel_id=1, source_target_pairs={{0,4},{2,6},{4,0},{6,2},{1,5},{3,7},{5,1},{7,3},{8,12},{10,14},{12... | collective-permute-start | bytes 196616 | tf_op jit(solution)/shard_map/ppermute | solution.py:42
  30.5 0.2 collective-permute-start.9
  30.8 1.1 %collective-permute-start.11 = (bf16[32,512]{1,0:T(8,128)(2,1)S(1)}, bf16[32,512]{1,0:T(8,128)(2,1)S(1)}, u32[]{:S(2)}, u32[]{:S(2)}) collective-permute-start(bf16[32,512]{1,0:T(8,128)(2,1)S(1)} %get-tuple-element.55.a_mine), channel_id=1, source_target_pairs={{0,8},{8,0},{1,9},{9,1},{2,10},{10,2},{3,11},{11,3},{4,12},{12,4},... | collective-permute-start | bytes 98312 | tf_op jit(solution)/shard_map/ppermute | solution.py:42
  31.9 0.3 collective-permute-start.12
  32.2 3.8 %main_x.1 = (f32[504,1024]{1,0:T(8,128)S(1)}, f32[504,128]{1,0:T(8,128)S(1)}, f32[3,192,1024]{2,1,0:T(8,128)S(1)}, f32[504,128]{1,0:T(8,128)S(1)}, f32[2,4,1024]{2,1,0:T(4,128)}, /*index=5*/f32[2,4,1024]{2,1,0:T(4,128)}) custom-call(f32[3,168,128]{2,1,0:T(8,128)S(1)} %get-tuple-element.40.mask_ref, ...), custom_call_target="tpu_custom_call", output_to_operand_aliasing={{0}: (6, {}), {1}: (7, {})} | custom-call | flops 2113929216 | bytes 2064384 | tf_op jit(solution)/shard_map/main_x/pallas_call | solution.py:308
  36.0 0.1 join_a.1.a_ref
  36.1 1.3 %final.1 = bf16[3,192,1024]{2,1,0:T(8,128)(2,1)} custom-call(bf16[256,128]{1,0:T(8,128)(2,1)S(1)} %sum_zl.1._.mine_ref, bf16[256,128]{1,0:T(8,128)(2,1)S(1)} %collective-permute-done.7.r1_ref, bf16[256,128]{1,0:T(8,128)(2,1)S(1)} %collective-permute-done.8.r2_ref, bf16[256,128]{1,0:T(8,128)(2,1)S(1)} %collective-permute-done.9.r3_ref, ...), custom_call_target="tpu_custom_call" | custom-call | tf_op jit(solution)/shard_map/final/pallas_call | solution.py:432
  (28 shorter events, 0.2 us)
Async XLA Ops:
  0.6 8.0 %copy-start.4 = (f32[8192]{0:T(1024)S(1)}, f32[8192]{0:T(1024)}, u32[]{:S(2)}) copy-start(f32[8192]{0:T(1024)} %param.14) | copy-start | bytes 98308
  0.6 8.0 %copy-start.8 = (s32[3]{0:T(128)S(1)}, s32[3]{0:T(128)}, u32[]{:S(2)}) copy-start(s32[3]{0:T(128)} %param.12) | copy-start | bytes 40
  0.7 8.0 %copy-start.6 = (bf16[8192]{0:T(1024)(128)(2,1)S(1)}, bf16[8192]{0:T(1024)(128)(2,1)}, u32[]{:S(2)}) copy-start(bf16[8192]{0:T(1024)(128)(2,1)} %param.15) | copy-start | bytes 49156
  0.7 8.0 %copy-start.7 = (s32[3,192]{1,0:T(4,128)S(1)}, s32[3,192]{1,0:T(4,128)}, u32[]{:S(2)}) copy-start(s32[3,192]{1,0:T(4,128)} %bits_ref.1) | copy-start | bytes 6916
  0.7 8.0 %copy-start.1 = (bf16[3,192,8192]{2,1,0:T(8,128)(2,1)S(1)}, bf16[3,192,8192]{2,1,0:T(8,128)(2,1)}, u32[]{:S(2)}) copy-start(bf16[3,192,8192]{2,1,0:T(8,128)(2,1)} %x_ref.9) | copy-start | bytes 28311556
  0.7 8.9 %copy-start = (bf16[8192,1024]{1,0:T(8,128)(2,1)S(1)}, bf16[8192,1024]{1,0:T(8,128)(2,1)}, u32[]{:S(2)}) copy-start(bf16[8192,1024]{1,0:T(8,128)(2,1)} %w_ref.7) | copy-start | bytes 50331652
  1.9 2.5 %collective-permute-start = (bf16[2,64,512]{2,1,0:T(8,128)(2,1)S(1)}, bf16[2,64,512]{2,1,0:T(8,128)(2,1)S(1)}, u32[]{:S(2)}, u32[]{:S(2)}) collective-permute-start(bf16[2,64,512]{2,1,0:T(8,128)(2,1)S(1)} %get-tuple-element.34), channel_id=1, source_target_pairs={{0,8},{8,0},{1,9},{9,1},{2,10},{10,2},{3,11},{11,3},{4,12},{12,4},... | collective-permute-start | bytes 393224 | tf_op jit(solution)/shard_map/ppermute | solution.py:42
  4.4 8.8 %collective-permute-start.1 = (bf16[96,512]{1,0:T(8,128)(2,1)S(1)}, bf16[96,512]{1,0:T(8,128)(2,1)S(1)}, u32[]{:S(2)}, u32[]{:S(2)}) collective-permute-start(bf16[96,512]{1,0:T(8,128)(2,1)S(1)} %get-tuple-element.38), channel_id=1, source_target_pairs={{0,48},{16,32},{32,16},{48,0},{1,49},{17,33},{33,17},{49,1},{2,50}... | collective-permute-start | bytes 294920 | tf_op jit(solution)/shard_map/ppermute | solution.py:42
  7.3 5.9 %collective-permute-start.3 = (bf16[96,512]{1,0:T(8,128)(2,1)S(1)}, bf16[96,512]{1,0:T(8,128)(2,1)S(1)}, u32[]{:S(2)}, u32[]{:S(2)}) collective-permute-start(bf16[96,512]{1,0:T(8,128)(2,1)S(1)} %get-tuple-element.38), channel_id=1, source_target_pairs={{0,16},{16,0},{32,48},{48,32},{1,17},{17,1},{33,49},{49,33},{2,18}... | collective-permute-start | bytes 294920 | tf_op jit(solution)/shard_map/ppermute | solution.py:42
  7.3 5.9 %collective-permute-start.2 = (bf16[96,512]{1,0:T(8,128)(2,1)S(1)}, bf16[96,512]{1,0:T(8,128)(2,1)S(1)}, u32[]{:S(2)}, u32[]{:S(2)}) collective-permute-start(bf16[96,512]{1,0:T(8,128)(2,1)S(1)} %get-tuple-element.35._), channel_id=1, source_target_pairs={{0,32},{16,48},{32,0},{48,16},{1,33},{17,49},{33,1},{49,17},{2,34}... | collective-permute-start | bytes 294920 | tf_op jit(solution)/shard_map/ppermute | solution.py:42
  13.3 6.7 %collective-permute-start.4 = (bf16[96,512]{1,0:T(8,128)(2,1)S(1)}, bf16[96,512]{1,0:T(8,128)(2,1)S(1)}, u32[]{:S(2)}, u32[]{:S(2)}) collective-permute-start(bf16[96,512]{1,0:T(8,128)(2,1)S(1)} %get-tuple-element.45._), channel_id=1, source_target_pairs={{0,64},{64,0},{1,65},{65,1},{2,66},{66,2},{3,67},{67,3},{4,68},{68... | collective-permute-start | bytes 294920 | tf_op jit(solution)/shard_map/ppermute | solution.py:42
  17.5 2.5 %copy-start.2 = (f32[2,64,1024]{2,1,0:T(8,128)S(1)}, f32[2,64,1024]{2,1,0:T(8,128)}, u32[]{:S(2)}) copy-start(f32[2,64,1024]{2,1,0:T(8,128)} %first_ref.3) | copy-start | bytes 1572868
  17.5 2.5 %copy-start.3 = (f32[2,64,1024]{2,1,0:T(8,128)S(1)}, f32[2,64,1024]{2,1,0:T(8,128)}, u32[]{:S(2)}) copy-start(f32[2,64,1024]{2,1,0:T(8,128)} %second_ref.3) | copy-start | bytes 1572868
  17.5 2.5 %copy-start.5 = (f32[2,64,1024]{2,1,0:T(8,128)S(1)}, f32[2,64,1024]{2,1,0:T(8,128)}, u32[]{:S(2)}) copy-start(f32[2,64,1024]{2,1,0:T(8,128)} %factors_ref.1) | copy-start | bytes 1572868
  20.3 2.2 %collective-permute-start.5 = (bf16[64,512]{1,0:T(8,128)(2,1)S(1)}, bf16[64,512]{1,0:T(8,128)(2,1)S(1)}, u32[]{:S(2)}, u32[]{:S(2)}) collective-permute-start(bf16[64,512]{1,0:T(8,128)(2,1)S(1)} %get-tuple-element.48.mine_ref), channel_id=1, source_target_pairs={{0,8},{8,0},{1,9},{9,1},{2,10},{10,2},{3,11},{11,3},{4,12},{12,4},... | collective-permute-start | bytes 196616 | tf_op jit(solution)/shard_map/ppermute | solution.py:42
  22.8 4.6 %collective-permute-start.6 = (bf16[256,128]{1,0:T(8,128)(2,1)S(1)}, bf16[256,128]{1,0:T(8,128)(2,1)S(1)}, u32[]{:S(2)}, u32[]{:S(2)}) collective-permute-start(bf16[256,128]{1,0:T(8,128)(2,1)S(1)} %low_rank.1._.mine_ref), channel_id=1, source_target_pairs={{0,1},{1,0},{2,3},{3,2},{4,5},{5,4},{6,7},{7,6},{8,9},{9,8},{10,11... | collective-permute-start | bytes 196616 | tf_op jit(solution)/shard_map/ppermute | solution.py:42
  24.0 7.9 %collective-permute-start.13 = (f32[2,8,512]{2,1,0:T(8,128)S(1)}, f32[2,8,512]{2,1,0:T(8,128)S(1)}, u32[]{:S(2)}, u32[]{:S(2)}) collective-permute-start(f32[2,8,512]{2,1,0:T(8,128)S(1)} %get-tuple-element.58.rows_mine), channel_id=1, source_target_pairs={{0,8},{8,0},{1,9},{9,1},{2,10},{10,2},{3,11},{11,3},{4,12},{12,4},... | collective-permute-start | bytes 98312 | tf_op jit(solution)/shard_map/ppermute | solution.py:42
  24.6 6.1 %collective-permute-start.10 = (bf16[32,512]{1,0:T(8,128)(2,1)S(1)}, bf16[32,512]{1,0:T(8,128)(2,1)S(1)}, u32[]{:S(2)}, u32[]{:S(2)}) collective-permute-start(bf16[32,512]{1,0:T(8,128)(2,1)S(1)} %get-tuple-element.55.a_mine), channel_id=1, source_target_pairs={{0,16},{16,0},{32,48},{48,32},{1,17},{17,1},{33,49},{49,33},{2,18}... | collective-permute-start | bytes 98312 | tf_op jit(solution)/shard_map/ppermute | solution.py:42
  27.4 8.6 %collective-permute-start.7 = (bf16[256,128]{1,0:T(8,128)(2,1)S(1)}, bf16[256,128]{1,0:T(8,128)(2,1)S(1)}, u32[]{:S(2)}, u32[]{:S(2)}) collective-permute-start(bf16[256,128]{1,0:T(8,128)(2,1)S(1)} %sum_zl.1._.mine_ref), channel_id=1, source_target_pairs={{0,6},{2,4},{4,2},{6,0},{1,7},{3,5},{5,3},{7,1},{8,14},{10,12},{12... | collective-permute-start | bytes 196616 | tf_op jit(solution)/shard_map/ppermute | solution.py:42
  30.0 6.1 %collective-permute-start.8 = (bf16[256,128]{1,0:T(8,128)(2,1)S(1)}, bf16[256,128]{1,0:T(8,128)(2,1)S(1)}, u32[]{:S(2)}, u32[]{:S(2)}) collective-permute-start(bf16[256,128]{1,0:T(8,128)(2,1)S(1)} %sum_zl.1._.mine_ref), channel_id=1, source_target_pairs={{0,4},{2,6},{4,0},{6,2},{1,5},{3,7},{5,1},{7,3},{8,12},{10,14},{12... | collective-permute-start | bytes 196616 | tf_op jit(solution)/shard_map/ppermute | solution.py:42
  30.5 5.5 %collective-permute-start.9 = (bf16[256,128]{1,0:T(8,128)(2,1)S(1)}, bf16[256,128]{1,0:T(8,128)(2,1)S(1)}, u32[]{:S(2)}, u32[]{:S(2)}) collective-permute-start(bf16[256,128]{1,0:T(8,128)(2,1)S(1)} %sum_zl.1._.mine_ref), channel_id=1, source_target_pairs={{0,2},{2,0},{4,6},{6,4},{1,3},{3,1},{5,7},{7,5},{8,10},{10,8},{12,... | collective-permute-start | bytes 196616 | tf_op jit(solution)/shard_map/ppermute | solution.py:42
  30.8 5.2 %collective-permute-start.11 = (bf16[32,512]{1,0:T(8,128)(2,1)S(1)}, bf16[32,512]{1,0:T(8,128)(2,1)S(1)}, u32[]{:S(2)}, u32[]{:S(2)}) collective-permute-start(bf16[32,512]{1,0:T(8,128)(2,1)S(1)} %get-tuple-element.55.a_mine), channel_id=1, source_target_pairs={{0,8},{8,0},{1,9},{9,1},{2,10},{10,2},{3,11},{11,3},{4,12},{12,4},... | collective-permute-start | bytes 98312 | tf_op jit(solution)/shard_map/ppermute | solution.py:42
  31.9 4.1 %collective-permute-start.12 = (bf16[32,512]{1,0:T(8,128)(2,1)S(1)}, bf16[32,512]{1,0:T(8,128)(2,1)S(1)}, u32[]{:S(2)}, u32[]{:S(2)}) collective-permute-start(bf16[32,512]{1,0:T(8,128)(2,1)S(1)} %collective-permute-done.10.a_y), channel_id=1, source_target_pairs={{0,8},{8,0},{1,9},{9,1},{2,10},{10,2},{3,11},{11,3},{4,12},{12,4},... | collective-permute-start | bytes 98312 | tf_op jit(solution)/shard_map/ppermute | solution.py:42

commit v5 on v4

--- a/solution.py
+++ b/solution.py
@@ -19,7 +19,7 @@
 SIZES = {"zh": 2, "y": 4, "c": 2, "x": 4, "zl": 2}
 DP = ("zh", "y", "c")
 TENSOR = ("x", "zl")
-CUTS = ((0, 1024, 2048, 3072), (3072, 4096, 5120), (5120, 6144), (6144, 7168, 8192))
+CUTS = ((0, 1024, 2048, 3072), (3072, 4096, 4864), (4864, 5376), (5376, 6400, 7424, 8192))
 FEATURES = 8192
 MIN_PROMPT = 24
 SKIP = 16
@@ -135,7 +135,7 @@
 
 def prepare_kernel(
     first_block, prompt_ref, bits_ref, gain_ref, embed_ref, x_ref, _, mask_ref, mine_ref, other_ref, embed_out, sq_ref,
-    normed_ref,
+    normed_ref, rest_ref,
 ):
     seqs, kept, _ = mask_ref.shape
     width = mine_ref.shape[1]
@@ -156,10 +156,13 @@
         for seq in range(seqs):
             rows = slice(seq * kept, (seq + 1) * kept)
             for j in range(width // 128):
-                lanes = pl.multiple_of(col + at_core * width + j * 128, 128)
-                block = pl.ds(lanes // 128, 1)
-                states = x_ref[seq, SKIP:, pl.ds(lanes, 128)].astype(jnp.float32)[MIN_PROMPT - SKIP :]
-                hidden = jnp.where(mask_ref[seq] > 1.5, embed_out[block], states)
+                at = pl.multiple_of(at_core * width + j * 128, 128)
+                lanes = pl.ds(at, 128)
+                block = pl.ds((col + at) // 128, 1)
+                states = x_ref[seq, :, pl.ds(pl.multiple_of(col + at, 128), 128)].astype(jnp.float32)
+                hidden = jnp.where(mask_ref[seq] > 1.5, embed_out[block], states[MIN_PROMPT:])
+                rest_ref[seq, :MIN_PROMPT, lanes] = states[:MIN_PROMPT]
+                rest_ref[seq, MIN_PROMPT:, lanes] = hidden
                 dst[rows, j * 128 : (j + 1) * 128] = (hidden * gain_ref[block]).astype(jnp.bfloat16)
     normalise(x_ref, mask_ref, gain_ref, embed_out, first_block, normed_ref, sq_ref, True)
 
@@ -186,42 +189,25 @@
 
 def last_kernel(
     cuts, mask_ref, gain_ref, embed_ref, x_ref, w_ref, _, acc_in, sq_in, rows_mine, rows_other, first_ref, second_ref,
-    acc_ref, sq_ref, base_ref, scale_ref, first_out, second_out, normed_a, normed_b, first_buf, second_buf, sems,
+    acc_ref, sq_ref, scale_ref, first_out, second_out, normed_a, normed_b,
 ):
     seqs, kept, _ = mask_ref.shape
-    cols = w_ref.shape[1]
-    col = pl.multiple_of(tensor_index() * cols, cols)
     even = lax.axis_index("c") == 0
 
+    args = (x_ref, w_ref, mask_ref, gain_ref, embed_ref, acc_ref, sq_ref, (normed_a, normed_b))
+    multiply(cuts[:2], *args)
     mine, other = rows_mine[...], rows_other[...]
     summed = jnp.concatenate([jnp.where(even, mine, other), jnp.where(even, other, mine)], axis=2)
     share = summed.shape[1] // 2
     first, second = adam_update(summed, first_ref[:, chip_rows()], second_ref[:, chip_rows()])
-    first_buf[...] = jnp.where(even, first[:, :share], first[:, share:])
-    second_buf[...] = jnp.where(even, second[:, :share], second[:, share:])
-    out = [
-        pltpu.make_async_copy(first_buf, first_out, sems.at[0]),
-        pltpu.make_async_copy(second_buf, second_out, sems.at[1]),
-    ]
-    start(out)
-
-    multiply(cuts, x_ref, w_ref, mask_ref, gain_ref, embed_ref, acc_ref, sq_ref, (normed_a, normed_b))
+    first_out[...] = jnp.where(even, first[:, :share], first[:, share:])
+    second_out[...] = jnp.where(even, second[:, :share], second[:, share:])
+    multiply(cuts[1:], *args)
     for seq in range(seqs):
         rows = slice(seq * kept, (seq + 1) * kept)
         mean = jnp.sum(sq_ref[rows], axis=1, keepdims=True) * (1.0 / FEATURES)
         scale = jnp.broadcast_to(lax.rsqrt(mean + norm_epsilon), (kept, 128))
-        code = mask_ref[seq]
-        scale_ref[rows] = jnp.where(code > 0.5, adapter_scale * scale, 0.0)
-        for j in range(cols // 128):
-            lanes = slice(j * 128, (j + 1) * 128)
-            at = pl.multiple_of(col + j * 128, 128)
-            states = x_ref[seq, :, pl.ds(at, 128)].astype(jnp.float32)
-            head, states = states[:MIN_PROMPT], states[MIN_PROMPT:]
-            hidden = jnp.where(code > 1.5, embed_ref[pl.ds(at // 128, 1)], states)
-            value = jnp.where(code > 0.5, hidden + scale * acc_ref[rows, lanes], states)
-            base_ref[seq, :MIN_PROMPT, lanes] = head
-            base_ref[seq, MIN_PROMPT:, lanes] = value
-    wait(out)
+        scale_ref[rows] = jnp.where(mask_ref[seq] > 0.5, scale, 0.0)
 
 
 VMEM = pl.BlockSpec(memory_space=pltpu.VMEM)
@@ -272,6 +258,7 @@
         (embed.shape, jnp.float32),
         ((rows, 128), jnp.float32),
         ((rows, block), jnp.bfloat16),
+        ((seqs, length, cols), jnp.float32),
     ]
     return pl.pallas_call(
         functools.partial(prepare_kernel, 0),
@@ -392,55 +379,75 @@
     out_ref[...] = jnp.concatenate([prod[:half], tail], axis=1).astype(jnp.bfloat16)
 
 
-def join_kernel(a_mine, a_core, a_y, a_y_core, _, a_ref):
-    mine = from_parity(a_mine[...].astype(jnp.float32), a_y[...].astype(jnp.float32))
-    other = from_parity(a_core[...].astype(jnp.float32), a_y_core[...].astype(jnp.float32))
+def pair_kernel(mine_ref, other_ref, _, out_ref):
+    out_ref[...] = jnp.concatenate([mine_ref[...], other_ref[...]], axis=0)
+
+
+def join_kernel(here_ref, there_ref, _, a_ref):
+    here, there = here_ref[...].astype(jnp.float32), there_ref[...].astype(jnp.float32)
+    half = here.shape[0] // 2
+    mine, other = from_parity(here[:half], there[:half]), from_parity(here[half:], there[half:])
     even = lax.axis_index("c") == 0
     joined = jnp.concatenate([jnp.where(even, mine, other), jnp.where(even, other, mine)], axis=1)
     a_ref[...] = joined.astype(jnp.bfloat16)
 
 
-def final_kernel(mine_ref, r1_ref, r2_ref, r3_ref, a_ref, base_ref, scale_ref, out_ref, stage_ref, sems):
-    seqs, length, _ = base_ref.shape
+def final_kernel(
+    mine_ref, r1_ref, r2_ref, r3_ref, a_ref, rest_ref, acc_ref, scale_ref, first_ref, second_ref,
+    out_ref, first_out, second_out, stage_ref, sems, moment_sems,
+):
+    copies = [
+        pltpu.make_async_copy(first_ref, first_out, moment_sems.at[0]),
+        pltpu.make_async_copy(second_ref, second_out, moment_sems.at[1]),
+    ]
+    start(copies)
+    seqs, length, cols = rest_ref.shape
     kept = length - MIN_PROMPT
     rank = a_ref.shape[0]
     half = mine_ref.shape[0]
     total = mine_ref[...].astype(jnp.float32) + r1_ref[...].astype(jnp.float32)
     total += r2_ref[...].astype(jnp.float32) + r3_ref[...].astype(jnp.float32)
     low = jnp.concatenate([total[:, :rank], total[: seqs * kept - half, rank:]], axis=0)
-    low = (low * scale_ref[:, :rank]).astype(jnp.bfloat16)
+    low = (low * (adapter_scale * scale_ref[:, :rank])).astype(jnp.bfloat16)
     a = a_ref[...]
-    copies = []
     for seq in range(seqs):
         adapter = jnp.dot(low[seq * kept : (seq + 1) * kept], a, preferred_element_type=jnp.float32)
         for piece in range(length // PIECE):
-            rows = slice(piece * PIECE, (piece + 1) * PIECE)
-            value = base_ref[seq, rows]
-            if rows.stop > MIN_PROMPT:
-                lead = max(MIN_PROMPT - rows.start, 0)
-                part = value[lead:] + adapter[rows.start + lead - MIN_PROMPT : rows.stop - MIN_PROMPT]
-                value = jnp.concatenate([value[:lead], part], axis=0) if lead else part
-            stage_ref[seq, rows] = value.astype(jnp.bfloat16)
-            at = pl.ds(rows.start, PIECE)
+            begin, end = piece * PIECE, (piece + 1) * PIECE
+            lead = max(MIN_PROMPT - begin, 0)
+            own = slice(begin + lead - MIN_PROMPT, end - MIN_PROMPT)
+            rows = slice(seq * kept + own.start, seq * kept + own.stop)
+            for j in range(cols // 128):
+                lanes = slice(j * 128, (j + 1) * 128)
+                value = rest_ref[seq, begin + lead : end, lanes] + scale_ref[rows] * acc_ref[rows, lanes]
+                value += adapter[own, lanes]
+                if lead:
+                    value = jnp.concatenate([rest_ref[seq, begin : begin + lead, lanes], value], axis=0)
+                stage_ref[seq, begin:end, lanes] = value.astype(jnp.bfloat16)
+            at = pl.ds(begin, PIECE)
             copy = pltpu.make_async_copy(stage_ref.at[seq, at], out_ref.at[seq, at], sems.at[seq, piece])
             copy.start()
             copies.append(copy)
     wait(copies)
 
 
-def final(mine, received, a, base, scale):
+def final(mine, received, a, rest, acc, scale, moments):
     return pl.pallas_call(
         final_kernel,
-        in_specs=[VMEM] * 7,
-        out_specs=HBM,
-        out_shape=jax.ShapeDtypeStruct(base.shape, jnp.bfloat16),
+        in_specs=[VMEM] * 10,
+        out_specs=[HBM] * 3,
+        out_shape=[
+            jax.ShapeDtypeStruct(rest.shape, jnp.bfloat16),
+            *[jax.ShapeDtypeStruct(v.shape, jnp.float32) for v in moments],
+        ],
         scratch_shapes=[
-            pltpu.VMEM(base.shape, jnp.bfloat16),
-            pltpu.SemaphoreType.DMA((base.shape[0], base.shape[1] // PIECE)),
+            pltpu.VMEM(rest.shape, jnp.bfloat16),
+            pltpu.SemaphoreType.DMA((rest.shape[0], rest.shape[1] // PIECE)),
+            pltpu.SemaphoreType.DMA((2,)),
         ],
-        compiler_params=pltpu.CompilerParams(vmem_limit_bytes=20 * MIB),
+        compiler_params=pltpu.CompilerParams(vmem_limit_bytes=16 * MIB),
         name="final",
-    )(mine, *received, a, base, scale)
+    )(mine, *received, a, rest, acc, scale, *moments)
 
 
 def local(x, mask_bits, prompt_len, weight, norm_gain, mask_embed, grads, factors, first_moment, second_moment):
@@ -457,9 +464,9 @@
     total, same, flip = small_call(
         core_sum_kernel, [(held, wide), (held, narrow), (held, narrow)], "sum_c", own, from_core
     )
-    from_y = [exchange(v, "y", (k,)) for v, k in ((flip, 3), (same, 2), (flip, 1))]
-
-    mask, own_mine, own_other, embed, sq, normed = prepare(
+    from_y = [exchange(v, "y", (k,)) for v, k in ((flip, 1), (flip, 3), (same, 2))]
+
+    mask, own_mine, own_other, embed, sq, normed, rest = prepare(
         prompt_len.reshape(1, -1), mask_bits, gain, embed, x, same, cols, CUTS[0][1]
     )
     common = (mask, gain, embed, x, weight)
@@ -478,28 +485,25 @@
         "update", total, from_z, *params, (state[1],), scratch=[(held, wide)],
     )
     b_other = exchange(b_own, "c", (1,))
+    a_core = exchange(a_half, "c", (1,))
+    rows_other = exchange(rows_own, "c", (1,))
     rows = own_mine.shape[0]
     (low,) = small_call(low_rank_first_kernel, [((rows, rank), wide)], "low_rank_first", own_mine, b_own)
     packed = (-(-rows // 32) * 16, 2 * rank)
     (low,) = small_call(low_rank_kernel, [(packed, narrow)], "low_rank", low, own_other, b_other)
     from_zl = exchange(low, ("zl",), (1,))
-    a_half, rows_own, _ = lax.optimization_barrier((a_half, rows_own, low))
-    a_y = exchange(a_half, "y", (1,))
-    rows_other = exchange(rows_own, "c", (1,))
+    (a_here,) = small_call(pair_kernel, [(part, narrow)], "pair_a", a_half, a_core, (low,))
+    a_there = exchange(a_here, "y", (1,))
     state, _ = main_part(part_kernel, "main_zl", CUTS[2], common, low, state, [], [], [], [])
     (low,) = small_call(add_kernel, [(low.shape, narrow)], "sum_zl", low, from_zl, (state[1],))
-    from_x = [exchange(low, ("x",), (k,)) for k in (3, 2, 1)]
-    a_half, a_y, _ = lax.optimization_barrier((a_half, a_y, low))
-    a_parts = (a_half, exchange(a_half, "c", (1,)), a_y, exchange(a_y, "c", (1,)))
+    from_x = [exchange(low, ("x",), (k,)) for k in (1, 3, 2)]
     four = ((two, 4, cols), wide)
-    state, (base, scale, out_first, out_second) = main_part(
+    state, (scale, *moments) = main_part(
         last_kernel, "main_x", CUTS[3], common, low, state, [rows_own, rows_other, *params[1:]], [VMEM] * 4,
-        [(x.shape[:2] + (cols,), wide), (state[1].shape, wide), four, four], [VMEM] * 2 + [HBM] * 2,
-        [pltpu.VMEM(*four), pltpu.VMEM(*four), pltpu.SemaphoreType.DMA((2,))],
-    )
-    (a,) = small_call(join_kernel, [((rank, cols), narrow)], "join_a", *a_parts, (scale,))
-    out = final(low, from_x, a, base, scale)
-    return out, out_first, out_second
+        [(state[1].shape, wide), four, four], [VMEM] * 3,
+    )
+    (a,) = small_call(join_kernel, [((rank, cols), narrow)], "join_a", a_here, a_there, (scale,))
+    return final(low, from_x, a, rest, state[0], scale, moments)
 
 
 def solution(mesh):

time: 37.6 us -> 36.4 us (0.968)
  the two profiles are of different devices: /device:TPU:1 before, /device:TPU:0 now
where the time goes in v5:
time: 36.4 us; the launch traced here: 36.2 us
  starting transfers between devices  16.9 us (46%)
  Pallas kernels  15 us (41%)
  waiting for transfers between devices  3.16 us (9%)
  between operations  0.99 us (3%)
    ppermute x13, starting transfers between devices, exchange(): return lax.ppermute(v, tuple(axes), pairs)  16.9 us
    pallas_call x3, Pallas kernels, main_part(): pl.pallas_call(functools.partial(kernel, cuts), in_specs=[VMEM] * 5 + [AN...  6.84 us
    pallas_call x1, Pallas kernels, main_first(): pl.pallas_call(functools.partial(y_kernel, cuts), in_specs=[VMEM] * 6 + [...  3.53 us
    ppermute x13, waiting for transfers between devices, exchange(): return lax.ppermute(v, tuple(axes), pairs)  3.16 us
    pallas_call x1, Pallas kernels, final(): pl.pallas_call(final_kernel, in_specs=[VMEM] * 10, out_specs=[HBM] * 3, o...  1.38 us
    pallas_call x1, Pallas kernels, pack(): pl.pallas_call(pack_kernel, in_specs=[HBM], out_specs=[VMEM, VMEM], out_s...  1.21 us
    pallas_call x1, Pallas kernels, prepare(): pl.pallas_call(functools.partial(prepare_kernel, 0), in_specs=[VMEM] * 5...  1.05 us
    pallas_call x8, Pallas kernels, small_call(): pl.pallas_call(kernel, in_specs=in_specs, out_specs=[VMEM] * len(shapes),...  1.01 us
  transfers between devices with their start and end apart: 13, of which 6 were waited for; matrix products, arithmetic and copies ran while one was open for 0% of the time, Pallas kernels for 33%

profile of v5, /device:TPU:0, one launch (start us, length us, event | category | flops | bytes accessed | tf_op | source)
XLA Modules:
  0.0 36.2 jit_solution(5619981813853011192)
XLA Ops:
  0.7 1.2 %pack.1 = (f32[2,64,512]{2,1,0:T(8,128)S(1)}, bf16[2,64,512]{2,1,0:T(8,128)(2,1)S(1)}) custom-call(f32[1,2,64,1024]{3,2,1,0:T(8,128)} %grad_ref.1), custom_call_target="tpu_custom_call" | custom-call | flops 20000000000 | bytes 80000000 | tf_op jit(solution)/shard_map/pack/pallas_call | solution.py:124
  1.9 0.1 collective-permute-start
  2.0 1.3 %collective-permute-done.theirs_ref = bf16[2,64,512]{2,1,0:T(8,128)(2,1)S(1)} collective-permute-done((bf16[2,64,512]{2,1,0:T(8,128)(2,1)S(1)}, bf16[2,64,512]{2,1,0:T(8,128)(2,1)S(1)}, u32[]{:S(2)}, u32[]{:S(2)}) %collective-permute-start) | collective-permute-done | bytes 131104 | tf_op jit(solution)/shard_map/ppermute | solution.py:42
  3.4 3.2 %collective-permute-start.2 = (bf16[96,512]{1,0:T(8,128)(2,1)S(1)}, bf16[96,512]{1,0:T(8,128)(2,1)S(1)}, u32[]{:S(2)}, u32[]{:S(2)}) collective-permute-start(bf16[96,512]{1,0:T(8,128)(2,1)S(1)} %get-tuple-element.35), channel_id=1, source_target_pairs={{0,48},{16,32},{32,16},{48,0},{1,49},{17,33},{33,17},{49,1},{2,50}... | collective-permute-start | bytes 294920 | tf_op jit(solution)/shard_map/ppermute | solution.py:42
  6.6 0.1 collective-permute-start.1
  6.7 1.5 %collective-permute-start.3 = (bf16[96,512]{1,0:T(8,128)(2,1)S(1)}, bf16[96,512]{1,0:T(8,128)(2,1)S(1)}, u32[]{:S(2)}, u32[]{:S(2)}) collective-permute-start(bf16[96,512]{1,0:T(8,128)(2,1)S(1)} %get-tuple-element.32._), channel_id=1, source_target_pairs={{0,32},{16,48},{32,0},{48,16},{1,33},{17,49},{33,1},{49,17},{2,34}... | collective-permute-start | bytes 294920 | tf_op jit(solution)/shard_map/ppermute | solution.py:42
  8.2 1.0 %prepare.1 = (f32[3,168,128]{2,1,0:T(8,128)S(1)}, bf16[504,512]{1,0:T(8,128)(2,1)S(1)}, bf16[504,512]{1,0:T(8,128)(2,1)S(1)}, f32[64,128]{1,0:T(8,128)S(1)}, f32...) custom-call(s32[1,3]{1,0:T(1,128)S(1)} %bitcast.9, s32[3,192]{1,0:T(4,128)S(1)} %copy-done.7, ...), custom_call_target="tpu_custom_call" | custom-call | tf_op jit(solution)/shard_map/prepare/pallas_call | solution.py:263
  9.2 0.1 copy-done
  9.3 3.5 %main_y.1 = (f32[504,1024]{1,0:T(8,128)S(1)}, f32[504,128]{1,0:T(8,128)S(1)}) custom-call(bf16[504,1024]{1,0:T(8,128)(2,1)S(1)} %get-tuple-element.36.normed_in, f32[3,168,128]{2,1,0:T(8,128)S(1)} %get-tuple-element.37.mask_ref, f32[64,128]{1,0:T(8,128)S(1)} %bitcast.4, f32[64,128]{1,0:T(8,128)S(1)} %get-tuple-element.38.embed_ref, ...), custom_call_target="tpu_custom_call", output_to_operand_aliasing={{1}: (7, {})} | custom-call | flops 3170893824 | bytes 2064384 | tf_op jit(solution)/shard_map/main_y/pallas_call | solution.py:277
  12.9 0.0 collective-permute-done.1.r1_ref
  12.9 0.2 collective-permute-done.3.r3_ref
  13.1 4.0 %collective-permute-start.4 = (bf16[96,512]{1,0:T(8,128)(2,1)S(1)}, bf16[96,512]{1,0:T(8,128)(2,1)S(1)}, u32[]{:S(2)}, u32[]{:S(2)}) collective-permute-start(bf16[96,512]{1,0:T(8,128)(2,1)S(1)} %get-tuple-element.42._), channel_id=1, source_target_pairs={{0,64},{64,0},{1,65},{65,1},{2,66},{66,2},{3,67},{67,3},{4,68},{68... | collective-permute-start | bytes 294920 | tf_op jit(solution)/shard_map/ppermute | solution.py:42
  17.1 2.2 %main_z.1 = (f32[504,1024]{1,0:T(8,128)S(1)}, f32[504,128]{1,0:T(8,128)S(1)}) custom-call(f32[3,168,128]{2,1,0:T(8,128)S(1)} %get-tuple-element.37.mask_ref, f32[64,128]{1,0:T(8,128)S(1)} %bitcast.5, f32[64,128]{1,0:T(8,128)S(1)} %get-tuple-element.38.embed_ref, bf16[3,192,8192]{2,1,0:T(8,128)(2,1)S(1)} %copy-done.1, ...), custom_call_target="tpu_custom_call", output_to_operand_aliasing={{0}: (6, {}), {1}: (7, {})} | custom-call | flops 1849688064 | bytes 2064384 | tf_op jit(solution)/shard_map/main_z/pallas_call | solution.py:295
  19.3 0.5 %collective-permute-done.4.theirs_ref = bf16[96,512]{1,0:T(8,128)(2,1)S(1)} collective-permute-done((bf16[96,512]{1,0:T(8,128)(2,1)S(1)}, bf16[96,512]{1,0:T(8,128)(2,1)S(1)}, u32[]{:S(2)}, u32[]{:S(2)}) %collective-permute-start.4) | collective-permute-done | bytes 98336 | tf_op jit(solution)/shard_map/ppermute | solution.py:42
  19.8 0.2 update.1
  20.0 0.1 collective-permute-start.5
  20.1 0.5 %collective-permute-start.10 = (bf16[32,512]{1,0:T(8,128)(2,1)S(1)}, bf16[32,512]{1,0:T(8,128)(2,1)S(1)}, u32[]{:S(2)}, u32[]{:S(2)}) collective-permute-start(bf16[32,512]{1,0:T(8,128)(2,1)S(1)} %get-tuple-element.49.mine_ref), channel_id=1, source_target_pairs={{0,8},{8,0},{1,9},{9,1},{2,10},{10,2},{3,11},{11,3},{4,12},{12,4},... | collective-permute-start | bytes 98312 | tf_op jit(solution)/shard_map/ppermute | solution.py:42
  20.6 0.3 low_rank_first.1.first_ref
  20.9 0.5 %collective-permute-done.5.other_ref = bf16[64,512]{1,0:T(8,128)(2,1)S(1)} collective-permute-done((bf16[64,512]{1,0:T(8,128)(2,1)S(1)}, bf16[64,512]{1,0:T(8,128)(2,1)S(1)}, u32[]{:S(2)}, u32[]{:S(2)}) %collective-permute-start.5) | collective-permute-done | bytes 65568 | tf_op jit(solution)/shard_map/ppermute | solution.py:42
  21.4 0.3 low_rank.1._.mine_ref
  21.7 1.5 %collective-permute-start.6 = (bf16[256,128]{1,0:T(8,128)(2,1)S(1)}, bf16[256,128]{1,0:T(8,128)(2,1)S(1)}, u32[]{:S(2)}, u32[]{:S(2)}) collective-permute-start(bf16[256,128]{1,0:T(8,128)(2,1)S(1)} %low_rank.1._.mine_ref), channel_id=1, source_target_pairs={{0,1},{1,0},{2,3},{3,2},{4,5},{5,4},{6,7},{7,6},{8,9},{9,8},{10,11... | collective-permute-start | bytes 196616 | tf_op jit(solution)/shard_map/ppermute | solution.py:42
  23.2 1.7 %collective-permute-start.11 = (bf16[64,512]{1,0:T(8,128)(2,1)S(1)}, bf16[64,512]{1,0:T(8,128)(2,1)S(1)}, u32[]{:S(2)}, u32[]{:S(2)}) collective-permute-start(bf16[64,512]{1,0:T(8,128)(2,1)S(1)} %pair_a.1.here_ref), channel_id=1, source_target_pairs={{0,16},{16,0},{32,48},{48,32},{1,17},{17,1},{33,49},{49,33},{2,18}... | collective-permute-start | bytes 196616 | tf_op jit(solution)/shard_map/ppermute | solution.py:42
  25.0 0.8 %main_zl.1 = (f32[504,1024]{1,0:T(8,128)S(1)}, f32[504,128]{1,0:T(8,128)S(1)}) custom-call(f32[3,168,128]{2,1,0:T(8,128)S(1)} %get-tuple-element.37.mask_ref, f32[64,128]{1,0:T(8,128)S(1)} %bitcast.6, f32[64,128]{1,0:T(8,128)S(1)} %get-tuple-element.38.embed_ref, bf16[3,192,8192]{2,1,0:T(8,128)(2,1)S(1)} %copy-done.1, ...), custom_call_target="tpu_custom_call", output_to_operand_aliasing={{0}: (6, {}), {1}: (7, {})} | custom-call | flops 528482304 | bytes 2064384 | tf_op jit(solution)/shard_map/main_zl/pallas_call | solution.py:295
  25.8 0.3 collective-permute-done.6.theirs_ref
  26.1 3.1 %collective-permute-start.9 = (bf16[256,128]{1,0:T(8,128)(2,1)S(1)}, bf16[256,128]{1,0:T(8,128)(2,1)S(1)}, u32[]{:S(2)}, u32[]{:S(2)}) collective-permute-start(bf16[256,128]{1,0:T(8,128)(2,1)S(1)} %sum_zl.1._.mine_ref), channel_id=1, source_target_pairs={{0,4},{2,6},{4,0},{6,2},{1,5},{3,7},{5,1},{7,3},{8,12},{10,14},{12... | collective-permute-start | bytes 196616 | tf_op jit(solution)/shard_map/ppermute | solution.py:42
  29.2 1.1 %collective-permute-start.8 = (bf16[256,128]{1,0:T(8,128)(2,1)S(1)}, bf16[256,128]{1,0:T(8,128)(2,1)S(1)}, u32[]{:S(2)}, u32[]{:S(2)}) collective-permute-start(bf16[256,128]{1,0:T(8,128)(2,1)S(1)} %sum_zl.1._.mine_ref), channel_id=1, source_target_pairs={{0,6},{2,4},{4,2},{6,0},{1,7},{3,5},{5,3},{7,1},{8,14},{10,12},{12... | collective-permute-start | bytes 196616 | tf_op jit(solution)/shard_map/ppermute | solution.py:42
  30.3 0.0 collective-permute-start.7
  30.3 0.0 collective-permute-done.12.rows_other
  30.3 3.9 %main_x.1 = (f32[504,1024]{1,0:T(8,128)S(1)}, f32[504,128]{1,0:T(8,128)S(1)}, f32[504,128]{1,0:T(8,128)S(1)}, f32[2,4,1024]{2,1,0:T(4,128)S(1)}, f32[2,4,1024]{2,1,0:T(4,128)S(1)}) custom-call(f32[3,168,128]{2,1,0:T(8,128)S(1)} %get-tuple-element.37.mask_ref, f32[64,128]{1,0:T(8,128)S(1)} %bitcast.7, ...), custom_call_target="tpu_custom_call", output_to_operand_aliasing={{0}: (6, {}), {1}: (7, {})} | custom-call | flops 2906652672 | bytes 2064384 | tf_op jit(solution)/shard_map/main_x/pallas_call | solution.py:295
  34.2 0.1 join_a.1.a_ref
  34.3 0.3 collective-permute-done.8.r2_ref
  34.7 1.4 %final.1 = (bf16[3,192,1024]{2,1,0:T(8,128)(2,1)}, f32[2,4,1024]{2,1,0:T(4,128)}, f32[2,4,1024]{2,1,0:T(4,128)}) custom-call(bf16[256,128]{1,0:T(8,128)(2,1)S(1)} %sum_zl.1._.mine_ref, bf16[256,128]{1,0:T(8,128)(2,1)S(1)} %collective-permute-done.7.r1_ref, bf16[256,128]{1,0:T(8,128)(2,1)S(1)} %collective-permute-done.8.r2_ref, ...), custom_call_target="tpu_custom_call" | custom-call | tf_op jit(solution)/shard_map/final/pallas_call | solution.py:435
  (27 shorter events, 0.2 us)
Async XLA Ops:
  0.6 7.5 %copy-start.6 = (bf16[8192]{0:T(1024)(128)(2,1)S(1)}, bf16[8192]{0:T(1024)(128)(2,1)}, u32[]{:S(2)}) copy-start(bf16[8192]{0:T(1024)(128)(2,1)} %param.15) | copy-start | bytes 49156
  0.6 7.5 %copy-start.4 = (f32[8192]{0:T(1024)S(1)}, f32[8192]{0:T(1024)}, u32[]{:S(2)}) copy-start(f32[8192]{0:T(1024)} %param.14) | copy-start | bytes 98308
  0.7 7.5 %copy-start.8 = (s32[3]{0:T(128)S(1)}, s32[3]{0:T(128)}, u32[]{:S(2)}) copy-start(s32[3]{0:T(128)} %param.12) | copy-start | bytes 40
  0.7 7.5 %copy-start.7 = (s32[3,192]{1,0:T(4,128)S(1)}, s32[3,192]{1,0:T(4,128)}, u32[]{:S(2)}) copy-start(s32[3,192]{1,0:T(4,128)} %bits_ref.1) | copy-start | bytes 6916
  0.7 7.5 %copy-start.1 = (bf16[3,192,8192]{2,1,0:T(8,128)(2,1)S(1)}, bf16[3,192,8192]{2,1,0:T(8,128)(2,1)}, u32[]{:S(2)}) copy-start(bf16[3,192,8192]{2,1,0:T(8,128)(2,1)} %x_ref.9) | copy-start | bytes 28311556
  0.7 8.6 %copy-start = (bf16[8192,1024]{1,0:T(8,128)(2,1)S(1)}, bf16[8192,1024]{1,0:T(8,128)(2,1)}, u32[]{:S(2)}) copy-start(bf16[8192,1024]{1,0:T(8,128)(2,1)} %w_ref.7) | copy-start | bytes 50331652
  1.9 1.4 %collective-permute-start = (bf16[2,64,512]{2,1,0:T(8,128)(2,1)S(1)}, bf16[2,64,512]{2,1,0:T(8,128)(2,1)S(1)}, u32[]{:S(2)}, u32[]{:S(2)}) collective-permute-start(bf16[2,64,512]{2,1,0:T(8,128)(2,1)S(1)} %get-tuple-element.31), channel_id=1, source_target_pairs={{0,8},{8,0},{1,9},{9,1},{2,10},{10,2},{3,11},{11,3},{4,12},{12,4},... | collective-permute-start | bytes 393224 | tf_op jit(solution)/shard_map/ppermute | solution.py:42
  3.4 9.5 %collective-permute-start.2 = (bf16[96,512]{1,0:T(8,128)(2,1)S(1)}, bf16[96,512]{1,0:T(8,128)(2,1)S(1)}, u32[]{:S(2)}, u32[]{:S(2)}) collective-permute-start(bf16[96,512]{1,0:T(8,128)(2,1)S(1)} %get-tuple-element.35), channel_id=1, source_target_pairs={{0,48},{16,32},{32,16},{48,0},{1,49},{17,33},{33,17},{49,1},{2,50}... | collective-permute-start | bytes 294920 | tf_op jit(solution)/shard_map/ppermute | solution.py:42
  6.6 6.3 %collective-permute-start.1 = (bf16[96,512]{1,0:T(8,128)(2,1)S(1)}, bf16[96,512]{1,0:T(8,128)(2,1)S(1)}, u32[]{:S(2)}, u32[]{:S(2)}) collective-permute-start(bf16[96,512]{1,0:T(8,128)(2,1)S(1)} %get-tuple-element.35), channel_id=1, source_target_pairs={{0,16},{16,0},{32,48},{48,32},{1,17},{17,1},{33,49},{49,33},{2,18}... | collective-permute-start | bytes 294920 | tf_op jit(solution)/shard_map/ppermute | solution.py:42
  6.7 6.3 %collective-permute-start.3 = (bf16[96,512]{1,0:T(8,128)(2,1)S(1)}, bf16[96,512]{1,0:T(8,128)(2,1)S(1)}, u32[]{:S(2)}, u32[]{:S(2)}) collective-permute-start(bf16[96,512]{1,0:T(8,128)(2,1)S(1)} %get-tuple-element.32._), channel_id=1, source_target_pairs={{0,32},{16,48},{32,0},{48,16},{1,33},{17,49},{33,1},{49,17},{2,34}... | collective-permute-start | bytes 294920 | tf_op jit(solution)/shard_map/ppermute | solution.py:42
  13.1 6.7 %collective-permute-start.4 = (bf16[96,512]{1,0:T(8,128)(2,1)S(1)}, bf16[96,512]{1,0:T(8,128)(2,1)S(1)}, u32[]{:S(2)}, u32[]{:S(2)}) collective-permute-start(bf16[96,512]{1,0:T(8,128)(2,1)S(1)} %get-tuple-element.42._), channel_id=1, source_target_pairs={{0,64},{64,0},{1,65},{65,1},{2,66},{66,2},{3,67},{67,3},{4,68},{68... | collective-permute-start | bytes 294920 | tf_op jit(solution)/shard_map/ppermute | solution.py:42
  17.0 2.7 %copy-start.2 = (f32[2,64,1024]{2,1,0:T(8,128)S(1)}, f32[2,64,1024]{2,1,0:T(8,128)}, u32[]{:S(2)}) copy-start(f32[2,64,1024]{2,1,0:T(8,128)} %first_ref.3) | copy-start | bytes 1572868
  17.1 2.7 %copy-start.3 = (f32[2,64,1024]{2,1,0:T(8,128)S(1)}, f32[2,64,1024]{2,1,0:T(8,128)}, u32[]{:S(2)}) copy-start(f32[2,64,1024]{2,1,0:T(8,128)} %second_ref.3) | copy-start | bytes 1572868
  17.1 2.7 %copy-start.5 = (f32[2,64,1024]{2,1,0:T(8,128)S(1)}, f32[2,64,1024]{2,1,0:T(8,128)}, u32[]{:S(2)}) copy-start(f32[2,64,1024]{2,1,0:T(8,128)} %factors_ref.1) | copy-start | bytes 1572868
  20.0 1.3 %collective-permute-start.5 = (bf16[64,512]{1,0:T(8,128)(2,1)S(1)}, bf16[64,512]{1,0:T(8,128)(2,1)S(1)}, u32[]{:S(2)}, u32[]{:S(2)}) collective-permute-start(bf16[64,512]{1,0:T(8,128)(2,1)S(1)} %get-tuple-element.45.mine_ref), channel_id=1, source_target_pairs={{0,8},{8,0},{1,9},{9,1},{2,10},{10,2},{3,11},{11,3},{4,12},{12,4},... | collective-permute-start | bytes 196616 | tf_op jit(solution)/shard_map/ppermute | solution.py:42
  20.1 3.1 %collective-permute-start.10 = (bf16[32,512]{1,0:T(8,128)(2,1)S(1)}, bf16[32,512]{1,0:T(8,128)(2,1)S(1)}, u32[]{:S(2)}, u32[]{:S(2)}) collective-permute-start(bf16[32,512]{1,0:T(8,128)(2,1)S(1)} %get-tuple-element.49.mine_ref), channel_id=1, source_target_pairs={{0,8},{8,0},{1,9},{9,1},{2,10},{10,2},{3,11},{11,3},{4,12},{12,4},... | collective-permute-start | bytes 98312 | tf_op jit(solution)/shard_map/ppermute | solution.py:42
  21.7 4.3 %collective-permute-start.6 = (bf16[256,128]{1,0:T(8,128)(2,1)S(1)}, bf16[256,128]{1,0:T(8,128)(2,1)S(1)}, u32[]{:S(2)}, u32[]{:S(2)}) collective-permute-start(bf16[256,128]{1,0:T(8,128)(2,1)S(1)} %low_rank.1._.mine_ref), channel_id=1, source_target_pairs={{0,1},{1,0},{2,3},{3,2},{4,5},{5,4},{6,7},{7,6},{8,9},{9,8},{10,11... | collective-permute-start | bytes 196616 | tf_op jit(solution)/shard_map/ppermute | solution.py:42
  23.2 7.1 %collective-permute-start.12 = (f32[2,8,512]{2,1,0:T(8,128)S(1)}, f32[2,8,512]{2,1,0:T(8,128)S(1)}, u32[]{:S(2)}, u32[]{:S(2)}) collective-permute-start(f32[2,8,512]{2,1,0:T(8,128)S(1)} %get-tuple-element.51.rows_mine), channel_id=1, source_target_pairs={{0,8},{8,0},{1,9},{9,1},{2,10},{10,2},{3,11},{11,3},{4,12},{12,4},... | collective-permute-start | bytes 98312 | tf_op jit(solution)/shard_map/ppermute | solution.py:42
  23.2 11.0 %collective-permute-start.11 = (bf16[64,512]{1,0:T(8,128)(2,1)S(1)}, bf16[64,512]{1,0:T(8,128)(2,1)S(1)}, u32[]{:S(2)}, u32[]{:S(2)}) collective-permute-start(bf16[64,512]{1,0:T(8,128)(2,1)S(1)} %pair_a.1.here_ref), channel_id=1, source_target_pairs={{0,16},{16,0},{32,48},{48,32},{1,17},{17,1},{33,49},{49,33},{2,18}... | collective-permute-start | bytes 196616 | tf_op jit(solution)/shard_map/ppermute | solution.py:42
  26.1 8.2 %collective-permute-start.9 = (bf16[256,128]{1,0:T(8,128)(2,1)S(1)}, bf16[256,128]{1,0:T(8,128)(2,1)S(1)}, u32[]{:S(2)}, u32[]{:S(2)}) collective-permute-start(bf16[256,128]{1,0:T(8,128)(2,1)S(1)} %sum_zl.1._.mine_ref), channel_id=1, source_target_pairs={{0,4},{2,6},{4,0},{6,2},{1,5},{3,7},{5,1},{7,3},{8,12},{10,14},{12... | collective-permute-start | bytes 196616 | tf_op jit(solution)/shard_map/ppermute | solution.py:42
  29.2 5.5 %collective-permute-start.8 = (bf16[256,128]{1,0:T(8,128)(2,1)S(1)}, bf16[256,128]{1,0:T(8,128)(2,1)S(1)}, u32[]{:S(2)}, u32[]{:S(2)}) collective-permute-start(bf16[256,128]{1,0:T(8,128)(2,1)S(1)} %sum_zl.1._.mine_ref), channel_id=1, source_target_pairs={{0,6},{2,4},{4,2},{6,0},{1,7},{3,5},{5,3},{7,1},{8,14},{10,12},{12... | collective-permute-start | bytes 196616 | tf_op jit(solution)/shard_map/ppermute | solution.py:42
  30.3 4.3 %collective-permute-start.7 = (bf16[256,128]{1,0:T(8,128)(2,1)S(1)}, bf16[256,128]{1,0:T(8,128)(2,1)S(1)}, u32[]{:S(2)}, u32[]{:S(2)}) collective-permute-start(bf16[256,128]{1,0:T(8,128)(2,1)S(1)} %sum_zl.1._.mine_ref), channel_id=1, source_target_pairs={{0,2},{2,0},{4,6},{6,4},{1,3},{3,1},{5,7},{7,5},{8,10},{10,8},{12,... | collective-permute-start | bytes 196616 | tf_op jit(solution)/shard_map/ppermute | solution.py:42

commit v6 on v5

--- a/solution.py
+++ b/solution.py
@@ -19,7 +19,7 @@
 SIZES = {"zh": 2, "y": 4, "c": 2, "x": 4, "zl": 2}
 DP = ("zh", "y", "c")
 TENSOR = ("x", "zl")
-CUTS = ((0, 1024, 2048, 3072), (3072, 4096, 4864), (4864, 5376), (5376, 6400, 7424, 8192))
+CUTS = ((0, 1024, 2048, 3072), (3072, 4096, 4864), (4864, 5632), (5632, 6656, 7680, 8192))
 FEATURES = 8192
 MIN_PROMPT = 24
 SKIP = 16

time: 36.4 us -> 36.3 us (level)
  transfers between devices with their start and end apart: 13 -> 13, of which waited for: 6 -> 5; matrix products, arithmetic and copies ran while one was open for 0% -> 0% of each run, Pallas kernels for 33% -> 34%
where the time goes in v6:
time: 36.3 us; the launch traced here: 36.2 us
  starting transfers between devices  17.1 us (47%)
  Pallas kernels  15.1 us (42%)
  waiting for transfers between devices  2.94 us (8%)
  between operations  1 us (3%)
    ppermute x13, starting transfers between devices, exchange(): return lax.ppermute(v, tuple(axes), pairs)  17.1 us
    pallas_call x3, Pallas kernels, main_part(): pl.pallas_call(functools.partial(kernel, cuts), in_specs=[VMEM] * 5 + [AN...  6.92 us
    pallas_call x1, Pallas kernels, main_first(): pl.pallas_call(functools.partial(y_kernel, cuts), in_specs=[VMEM] * 6 + [...  3.53 us
    ppermute x13, waiting for transfers between devices, exchange(): return lax.ppermute(v, tuple(axes), pairs)  2.94 us
    pallas_call x1, Pallas kernels, final(): pl.pallas_call(final_kernel, in_specs=[VMEM] * 10, out_specs=[HBM] * 3, o...  1.38 us
    pallas_call x1, Pallas kernels, pack(): pl.pallas_call(pack_kernel, in_specs=[HBM], out_specs=[VMEM, VMEM], out_s...  1.21 us
    pallas_call x1, Pallas kernels, prepare(): pl.pallas_call(functools.partial(prepare_kernel, 0), in_specs=[VMEM] * 5...  1.05 us
    pallas_call x8, Pallas kernels, small_call(): pl.pallas_call(kernel, in_specs=in_specs, out_specs=[VMEM] * len(shapes),...  1.01 us
  transfers between devices with their start and end apart: 13, of which 5 were waited for; matrix products, arithmetic and copies ran while one was open for 0% of the time, Pallas kernels for 34%

profile of v6, /device:TPU:0, one launch (start us, length us, event | category | flops | bytes accessed | tf_op | source)
XLA Modules:
  0.0 36.2 jit_solution(5869332061005310877)
XLA Ops:
  0.7 1.2 %pack.1 = (f32[2,64,512]{2,1,0:T(8,128)S(1)}, bf16[2,64,512]{2,1,0:T(8,128)(2,1)S(1)}) custom-call(f32[1,2,64,1024]{3,2,1,0:T(8,128)} %grad_ref.1), custom_call_target="tpu_custom_call" | custom-call | flops 20000000000 | bytes 80000000 | tf_op jit(solution)/shard_map/pack/pallas_call | solution.py:124
  1.9 0.1 collective-permute-start
  2.0 1.3 %collective-permute-done.theirs_ref = bf16[2,64,512]{2,1,0:T(8,128)(2,1)S(1)} collective-permute-done((bf16[2,64,512]{2,1,0:T(8,128)(2,1)S(1)}, bf16[2,64,512]{2,1,0:T(8,128)(2,1)S(1)}, u32[]{:S(2)}, u32[]{:S(2)}) %collective-permute-start) | collective-permute-done | bytes 131104 | tf_op jit(solution)/shard_map/ppermute | solution.py:42
  3.4 3.2 %collective-permute-start.2 = (bf16[96,512]{1,0:T(8,128)(2,1)S(1)}, bf16[96,512]{1,0:T(8,128)(2,1)S(1)}, u32[]{:S(2)}, u32[]{:S(2)}) collective-permute-start(bf16[96,512]{1,0:T(8,128)(2,1)S(1)} %get-tuple-element.35), channel_id=1, source_target_pairs={{0,48},{16,32},{32,16},{48,0},{1,49},{17,33},{33,17},{49,1},{2,50}... | collective-permute-start | bytes 294920 | tf_op jit(solution)/shard_map/ppermute | solution.py:42
  6.6 0.1 collective-permute-start.1
  6.7 1.5 %collective-permute-start.3 = (bf16[96,512]{1,0:T(8,128)(2,1)S(1)}, bf16[96,512]{1,0:T(8,128)(2,1)S(1)}, u32[]{:S(2)}, u32[]{:S(2)}) collective-permute-start(bf16[96,512]{1,0:T(8,128)(2,1)S(1)} %get-tuple-element.32._), channel_id=1, source_target_pairs={{0,32},{16,48},{32,0},{48,16},{1,33},{17,49},{33,1},{49,17},{2,34}... | collective-permute-start | bytes 294920 | tf_op jit(solution)/shard_map/ppermute | solution.py:42
  8.2 1.0 %prepare.1 = (f32[3,168,128]{2,1,0:T(8,128)S(1)}, bf16[504,512]{1,0:T(8,128)(2,1)S(1)}, bf16[504,512]{1,0:T(8,128)(2,1)S(1)}, f32[64,128]{1,0:T(8,128)S(1)}, f32...) custom-call(s32[1,3]{1,0:T(1,128)S(1)} %bitcast.9, s32[3,192]{1,0:T(4,128)S(1)} %copy-done.7, ...), custom_call_target="tpu_custom_call" | custom-call | tf_op jit(solution)/shard_map/prepare/pallas_call | solution.py:263
  9.2 0.1 copy-done
  9.3 3.5 %main_y.1 = (f32[504,1024]{1,0:T(8,128)S(1)}, f32[504,128]{1,0:T(8,128)S(1)}) custom-call(bf16[504,1024]{1,0:T(8,128)(2,1)S(1)} %get-tuple-element.36.normed_in, f32[3,168,128]{2,1,0:T(8,128)S(1)} %get-tuple-element.37.mask_ref, f32[64,128]{1,0:T(8,128)S(1)} %bitcast.4, f32[64,128]{1,0:T(8,128)S(1)} %get-tuple-element.38.embed_ref, ...), custom_call_target="tpu_custom_call", output_to_operand_aliasing={{1}: (7, {})} | custom-call | flops 3170893824 | bytes 2064384 | tf_op jit(solution)/shard_map/main_y/pallas_call | solution.py:277
  12.8 0.0 collective-permute-done.2.r2_ref
  12.9 0.2 collective-permute-done.3.r3_ref
  13.1 4.0 %collective-permute-start.4 = (bf16[96,512]{1,0:T(8,128)(2,1)S(1)}, bf16[96,512]{1,0:T(8,128)(2,1)S(1)}, u32[]{:S(2)}, u32[]{:S(2)}) collective-permute-start(bf16[96,512]{1,0:T(8,128)(2,1)S(1)} %get-tuple-element.42._), channel_id=1, source_target_pairs={{0,64},{64,0},{1,65},{65,1},{2,66},{66,2},{3,67},{67,3},{4,68},{68... | collective-permute-start | bytes 294920 | tf_op jit(solution)/shard_map/ppermute | solution.py:42
  17.1 2.2 %main_z.1 = (f32[504,1024]{1,0:T(8,128)S(1)}, f32[504,128]{1,0:T(8,128)S(1)}) custom-call(f32[3,168,128]{2,1,0:T(8,128)S(1)} %get-tuple-element.37.mask_ref, f32[64,128]{1,0:T(8,128)S(1)} %bitcast.5, f32[64,128]{1,0:T(8,128)S(1)} %get-tuple-element.38.embed_ref, bf16[3,192,8192]{2,1,0:T(8,128)(2,1)S(1)} %copy-done.1, ...), custom_call_target="tpu_custom_call", output_to_operand_aliasing={{0}: (6, {}), {1}: (7, {})} | custom-call | flops 1849688064 | bytes 2064384 | tf_op jit(solution)/shard_map/main_z/pallas_call | solution.py:295
  19.3 0.5 %collective-permute-done.4.theirs_ref = bf16[96,512]{1,0:T(8,128)(2,1)S(1)} collective-permute-done((bf16[96,512]{1,0:T(8,128)(2,1)S(1)}, bf16[96,512]{1,0:T(8,128)(2,1)S(1)}, u32[]{:S(2)}, u32[]{:S(2)}) %collective-permute-start.4) | collective-permute-done | bytes 98336 | tf_op jit(solution)/shard_map/ppermute | solution.py:42
  19.8 0.2 update.1
  20.0 0.1 collective-permute-start.5
  20.1 0.3 low_rank_first.1.first_ref
  20.4 0.6 %collective-permute-start.10 = (bf16[32,512]{1,0:T(8,128)(2,1)S(1)}, bf16[32,512]{1,0:T(8,128)(2,1)S(1)}, u32[]{:S(2)}, u32[]{:S(2)}) collective-permute-start(bf16[32,512]{1,0:T(8,128)(2,1)S(1)} %get-tuple-element.49.mine_ref), channel_id=1, source_target_pairs={{0,8},{8,0},{1,9},{9,1},{2,10},{10,2},{3,11},{11,3},{4,12},{12,4},... | collective-permute-start | bytes 98312 | tf_op jit(solution)/shard_map/ppermute | solution.py:42
  21.0 0.1 collective-permute-start.12
  21.1 0.3 collective-permute-done.5.other_ref
  21.4 0.3 low_rank.1._.mine_ref
  21.7 1.5 %collective-permute-start.6 = (bf16[256,128]{1,0:T(8,128)(2,1)S(1)}, bf16[256,128]{1,0:T(8,128)(2,1)S(1)}, u32[]{:S(2)}, u32[]{:S(2)}) collective-permute-start(bf16[256,128]{1,0:T(8,128)(2,1)S(1)} %low_rank.1._.mine_ref), channel_id=1, source_target_pairs={{0,1},{1,0},{2,3},{3,2},{4,5},{5,4},{6,7},{7,6},{8,9},{9,8},{10,11... | collective-permute-start | bytes 196616 | tf_op jit(solution)/shard_map/ppermute | solution.py:42
  23.2 1.1 %main_zl.1 = (f32[504,1024]{1,0:T(8,128)S(1)}, f32[504,128]{1,0:T(8,128)S(1)}) custom-call(f32[3,168,128]{2,1,0:T(8,128)S(1)} %get-tuple-element.37.mask_ref, f32[64,128]{1,0:T(8,128)S(1)} %bitcast.6, f32[64,128]{1,0:T(8,128)S(1)} %get-tuple-element.38.embed_ref, bf16[3,192,8192]{2,1,0:T(8,128)(2,1)S(1)} %copy-done.1, ...), custom_call_target="tpu_custom_call", output_to_operand_aliasing={{0}: (6, {}), {1}: (7, {})} | custom-call | flops 792723456 | bytes 2064384 | tf_op jit(solution)/shard_map/main_zl/pallas_call | solution.py:295
  24.3 0.0 collective-permute-done.10.other_ref
  24.3 1.7 %collective-permute-start.11 = (bf16[64,512]{1,0:T(8,128)(2,1)S(1)}, bf16[64,512]{1,0:T(8,128)(2,1)S(1)}, u32[]{:S(2)}, u32[]{:S(2)}) collective-permute-start(bf16[64,512]{1,0:T(8,128)(2,1)S(1)} %pair_a.1.here_ref), channel_id=1, source_target_pairs={{0,16},{16,0},{32,48},{48,32},{1,17},{17,1},{33,49},{49,33},{2,18}... | collective-permute-start | bytes 196616 | tf_op jit(solution)/shard_map/ppermute | solution.py:42
  26.1 3.1 %collective-permute-start.9 = (bf16[256,128]{1,0:T(8,128)(2,1)S(1)}, bf16[256,128]{1,0:T(8,128)(2,1)S(1)}, u32[]{:S(2)}, u32[]{:S(2)}) collective-permute-start(bf16[256,128]{1,0:T(8,128)(2,1)S(1)} %sum_zl.1._.mine_ref), channel_id=1, source_target_pairs={{0,4},{2,6},{4,0},{6,2},{1,5},{3,7},{5,1},{7,3},{8,12},{10,14},{12... | collective-permute-start | bytes 196616 | tf_op jit(solution)/shard_map/ppermute | solution.py:42
  29.2 1.1 %collective-permute-start.8 = (bf16[256,128]{1,0:T(8,128)(2,1)S(1)}, bf16[256,128]{1,0:T(8,128)(2,1)S(1)}, u32[]{:S(2)}, u32[]{:S(2)}) collective-permute-start(bf16[256,128]{1,0:T(8,128)(2,1)S(1)} %sum_zl.1._.mine_ref), channel_id=1, source_target_pairs={{0,6},{2,4},{4,2},{6,0},{1,7},{3,5},{5,3},{7,1},{8,14},{10,12},{12... | collective-permute-start | bytes 196616 | tf_op jit(solution)/shard_map/ppermute | solution.py:42
  30.4 0.0 collective-permute-start.7
  30.4 3.6 %main_x.1 = (f32[504,1024]{1,0:T(8,128)S(1)}, f32[504,128]{1,0:T(8,128)S(1)}, f32[504,128]{1,0:T(8,128)S(1)}, f32[2,4,1024]{2,1,0:T(4,128)S(1)}, f32[2,4,1024]{2,1,0:T(4,128)S(1)}) custom-call(f32[3,168,128]{2,1,0:T(8,128)S(1)} %get-tuple-element.37.mask_ref, f32[64,128]{1,0:T(8,128)S(1)} %bitcast.7, ...), custom_call_target="tpu_custom_call", output_to_operand_aliasing={{0}: (6, {}), {1}: (7, {})} | custom-call | flops 2642411520 | bytes 2064384 | tf_op jit(solution)/shard_map/main_x/pallas_call | solution.py:295
  34.0 0.1 join_a.1.a_ref
  34.1 0.6 %collective-permute-done.8.r2_ref = bf16[256,128]{1,0:T(8,128)(2,1)S(1)} collective-permute-done((bf16[256,128]{1,0:T(8,128)(2,1)S(1)}, bf16[256,128]{1,0:T(8,128)(2,1)S(1)}, u32[]{:S(2)}, u32[]{:S(2)}) %collective-permute-start.8) | collective-permute-done | bytes 65568 | tf_op jit(solution)/shard_map/ppermute | solution.py:42
  34.7 1.4 %final.1 = (bf16[3,192,1024]{2,1,0:T(8,128)(2,1)}, f32[2,4,1024]{2,1,0:T(4,128)}, f32[2,4,1024]{2,1,0:T(4,128)}) custom-call(bf16[256,128]{1,0:T(8,128)(2,1)S(1)} %sum_zl.1._.mine_ref, bf16[256,128]{1,0:T(8,128)(2,1)S(1)} %collective-permute-done.7.r1_ref, bf16[256,128]{1,0:T(8,128)(2,1)S(1)} %collective-permute-done.8.r2_ref, ...), custom_call_target="tpu_custom_call" | custom-call | tf_op jit(solution)/shard_map/final/pallas_call | solution.py:435
  (27 shorter events, 0.2 us)
Async XLA Ops:
  0.6 7.5 %copy-start.6 = (bf16[8192]{0:T(1024)(128)(2,1)S(1)}, bf16[8192]{0:T(1024)(128)(2,1)}, u32[]{:S(2)}) copy-start(bf16[8192]{0:T(1024)(128)(2,1)} %param.15) | copy-start | bytes 49156
  0.6 7.5 %copy-start.4 = (f32[8192]{0:T(1024)S(1)}, f32[8192]{0:T(1024)}, u32[]{:S(2)}) copy-start(f32[8192]{0:T(1024)} %param.14) | copy-start | bytes 98308
  0.7 7.5 %copy-start.8 = (s32[3]{0:T(128)S(1)}, s32[3]{0:T(128)}, u32[]{:S(2)}) copy-start(s32[3]{0:T(128)} %param.12) | copy-start | bytes 40
  0.7 7.5 %copy-start.7 = (s32[3,192]{1,0:T(4,128)S(1)}, s32[3,192]{1,0:T(4,128)}, u32[]{:S(2)}) copy-start(s32[3,192]{1,0:T(4,128)} %bits_ref.1) | copy-start | bytes 6916
  0.7 7.5 %copy-start.1 = (bf16[3,192,8192]{2,1,0:T(8,128)(2,1)S(1)}, bf16[3,192,8192]{2,1,0:T(8,128)(2,1)}, u32[]{:S(2)}) copy-start(bf16[3,192,8192]{2,1,0:T(8,128)(2,1)} %x_ref.9) | copy-start | bytes 28311556
  0.7 8.6 %copy-start = (bf16[8192,1024]{1,0:T(8,128)(2,1)S(1)}, bf16[8192,1024]{1,0:T(8,128)(2,1)}, u32[]{:S(2)}) copy-start(bf16[8192,1024]{1,0:T(8,128)(2,1)} %w_ref.7) | copy-start | bytes 50331652
  1.9 1.4 %collective-permute-start = (bf16[2,64,512]{2,1,0:T(8,128)(2,1)S(1)}, bf16[2,64,512]{2,1,0:T(8,128)(2,1)S(1)}, u32[]{:S(2)}, u32[]{:S(2)}) collective-permute-start(bf16[2,64,512]{2,1,0:T(8,128)(2,1)S(1)} %get-tuple-element.31), channel_id=1, source_target_pairs={{0,8},{8,0},{1,9},{9,1},{2,10},{10,2},{3,11},{11,3},{4,12},{12,4},... | collective-permute-start | bytes 393224 | tf_op jit(solution)/shard_map/ppermute | solution.py:42
  3.4 9.5 %collective-permute-start.2 = (bf16[96,512]{1,0:T(8,128)(2,1)S(1)}, bf16[96,512]{1,0:T(8,128)(2,1)S(1)}, u32[]{:S(2)}, u32[]{:S(2)}) collective-permute-start(bf16[96,512]{1,0:T(8,128)(2,1)S(1)} %get-tuple-element.35), channel_id=1, source_target_pairs={{0,48},{16,32},{32,16},{48,0},{1,49},{17,33},{33,17},{49,1},{2,50}... | collective-permute-start | bytes 294920 | tf_op jit(solution)/shard_map/ppermute | solution.py:42
  6.6 6.3 %collective-permute-start.1 = (bf16[96,512]{1,0:T(8,128)(2,1)S(1)}, bf16[96,512]{1,0:T(8,128)(2,1)S(1)}, u32[]{:S(2)}, u32[]{:S(2)}) collective-permute-start(bf16[96,512]{1,0:T(8,128)(2,1)S(1)} %get-tuple-element.35), channel_id=1, source_target_pairs={{0,16},{16,0},{32,48},{48,32},{1,17},{17,1},{33,49},{49,33},{2,18}... | collective-permute-start | bytes 294920 | tf_op jit(solution)/shard_map/ppermute | solution.py:42
  6.7 6.3 %collective-permute-start.3 = (bf16[96,512]{1,0:T(8,128)(2,1)S(1)}, bf16[96,512]{1,0:T(8,128)(2,1)S(1)}, u32[]{:S(2)}, u32[]{:S(2)}) collective-permute-start(bf16[96,512]{1,0:T(8,128)(2,1)S(1)} %get-tuple-element.32._), channel_id=1, source_target_pairs={{0,32},{16,48},{32,0},{48,16},{1,33},{17,49},{33,1},{49,17},{2,34}... | collective-permute-start | bytes 294920 | tf_op jit(solution)/shard_map/ppermute | solution.py:42
  13.1 6.7 %collective-permute-start.4 = (bf16[96,512]{1,0:T(8,128)(2,1)S(1)}, bf16[96,512]{1,0:T(8,128)(2,1)S(1)}, u32[]{:S(2)}, u32[]{:S(2)}) collective-permute-start(bf16[96,512]{1,0:T(8,128)(2,1)S(1)} %get-tuple-element.42._), channel_id=1, source_target_pairs={{0,64},{64,0},{1,65},{65,1},{2,66},{66,2},{3,67},{67,3},{4,68},{68... | collective-permute-start | bytes 294920 | tf_op jit(solution)/shard_map/ppermute | solution.py:42
  17.0 2.7 %copy-start.2 = (f32[2,64,1024]{2,1,0:T(8,128)S(1)}, f32[2,64,1024]{2,1,0:T(8,128)}, u32[]{:S(2)}) copy-start(f32[2,64,1024]{2,1,0:T(8,128)} %first_ref.3) | copy-start | bytes 1572868
  17.1 2.7 %copy-start.3 = (f32[2,64,1024]{2,1,0:T(8,128)S(1)}, f32[2,64,1024]{2,1,0:T(8,128)}, u32[]{:S(2)}) copy-start(f32[2,64,1024]{2,1,0:T(8,128)} %second_ref.3) | copy-start | bytes 1572868
  17.1 2.7 %copy-start.5 = (f32[2,64,1024]{2,1,0:T(8,128)S(1)}, f32[2,64,1024]{2,1,0:T(8,128)}, u32[]{:S(2)}) copy-start(f32[2,64,1024]{2,1,0:T(8,128)} %factors_ref.1) | copy-start | bytes 1572868
  20.0 1.3 %collective-permute-start.5 = (bf16[64,512]{1,0:T(8,128)(2,1)S(1)}, bf16[64,512]{1,0:T(8,128)(2,1)S(1)}, u32[]{:S(2)}, u32[]{:S(2)}) collective-permute-start(bf16[64,512]{1,0:T(8,128)(2,1)S(1)} %get-tuple-element.45.mine_ref), channel_id=1, source_target_pairs={{0,8},{8,0},{1,9},{9,1},{2,10},{10,2},{3,11},{11,3},{4,12},{12,4},... | collective-permute-start | bytes 196616 | tf_op jit(solution)/shard_map/ppermute | solution.py:42
  20.4 3.9 %collective-permute-start.10 = (bf16[32,512]{1,0:T(8,128)(2,1)S(1)}, bf16[32,512]{1,0:T(8,128)(2,1)S(1)}, u32[]{:S(2)}, u32[]{:S(2)}) collective-permute-start(bf16[32,512]{1,0:T(8,128)(2,1)S(1)} %get-tuple-element.49.mine_ref), channel_id=1, source_target_pairs={{0,8},{8,0},{1,9},{9,1},{2,10},{10,2},{3,11},{11,3},{4,12},{12,4},... | collective-permute-start | bytes 98312 | tf_op jit(solution)/shard_map/ppermute | solution.py:42
  21.0 9.4 %collective-permute-start.12 = (f32[2,8,512]{2,1,0:T(8,128)S(1)}, f32[2,8,512]{2,1,0:T(8,128)S(1)}, u32[]{:S(2)}, u32[]{:S(2)}) collective-permute-start(f32[2,8,512]{2,1,0:T(8,128)S(1)} %get-tuple-element.51.rows_mine), channel_id=1, source_target_pairs={{0,8},{8,0},{1,9},{9,1},{2,10},{10,2},{3,11},{11,3},{4,12},{12,4},... | collective-permute-start | bytes 98312 | tf_op jit(solution)/shard_map/ppermute | solution.py:42
  21.7 4.4 %collective-permute-start.6 = (bf16[256,128]{1,0:T(8,128)(2,1)S(1)}, bf16[256,128]{1,0:T(8,128)(2,1)S(1)}, u32[]{:S(2)}, u32[]{:S(2)}) collective-permute-start(bf16[256,128]{1,0:T(8,128)(2,1)S(1)} %low_rank.1._.mine_ref), channel_id=1, source_target_pairs={{0,1},{1,0},{2,3},{3,2},{4,5},{5,4},{6,7},{7,6},{8,9},{9,8},{10,11... | collective-permute-start | bytes 196616 | tf_op jit(solution)/shard_map/ppermute | solution.py:42
  24.3 9.7 %collective-permute-start.11 = (bf16[64,512]{1,0:T(8,128)(2,1)S(1)}, bf16[64,512]{1,0:T(8,128)(2,1)S(1)}, u32[]{:S(2)}, u32[]{:S(2)}) collective-permute-start(bf16[64,512]{1,0:T(8,128)(2,1)S(1)} %pair_a.1.here_ref), channel_id=1, source_target_pairs={{0,16},{16,0},{32,48},{48,32},{1,17},{17,1},{33,49},{49,33},{2,18}... | collective-permute-start | bytes 196616 | tf_op jit(solution)/shard_map/ppermute | solution.py:42
  26.1 8.0 %collective-permute-start.9 = (bf16[256,128]{1,0:T(8,128)(2,1)S(1)}, bf16[256,128]{1,0:T(8,128)(2,1)S(1)}, u32[]{:S(2)}, u32[]{:S(2)}) collective-permute-start(bf16[256,128]{1,0:T(8,128)(2,1)S(1)} %sum_zl.1._.mine_ref), channel_id=1, source_target_pairs={{0,4},{2,6},{4,0},{6,2},{1,5},{3,7},{5,1},{7,3},{8,12},{10,14},{12... | collective-permute-start | bytes 196616 | tf_op jit(solution)/shard_map/ppermute | solution.py:42
  29.2 5.5 %collective-permute-start.8 = (bf16[256,128]{1,0:T(8,128)(2,1)S(1)}, bf16[256,128]{1,0:T(8,128)(2,1)S(1)}, u32[]{:S(2)}, u32[]{:S(2)}) collective-permute-start(bf16[256,128]{1,0:T(8,128)(2,1)S(1)} %sum_zl.1._.mine_ref), channel_id=1, source_target_pairs={{0,6},{2,4},{4,2},{6,0},{1,7},{3,5},{5,3},{7,1},{8,14},{10,12},{12... | collective-permute-start | bytes 196616 | tf_op jit(solution)/shard_map/ppermute | solution.py:42
  30.4 4.3 %collective-permute-start.7 = (bf16[256,128]{1,0:T(8,128)(2,1)S(1)}, bf16[256,128]{1,0:T(8,128)(2,1)S(1)}, u32[]{:S(2)}, u32[]{:S(2)}) collective-permute-start(bf16[256,128]{1,0:T(8,128)(2,1)S(1)} %sum_zl.1._.mine_ref), channel_id=1, source_target_pairs={{0,2},{2,0},{4,6},{6,4},{1,3},{3,1},{5,7},{7,5},{8,10},{10,8},{12,... | collective-permute-start | bytes 196616 | tf_op jit(solution)/shard_map/ppermute | solution.py:42
